TPU v7x, 32 devices: a whole 2x2x4 slice. The times are simulated.
32 devices in a mesh: section: 2 (over x), dp: 4 (over z), tensor: 4 (over y, core).
Axes of the slice: x: 2, y: 2, z: 4, core: 2. Of those that a mesh axis runs over, the one named last changes fastest.
Arguments:
- tokens: bfloat16 [8, 2048, 768], P('dp', 'tensor'), may hold values from -6 to 6
- qkv_weight: bfloat16 [2, 3, 768, 768], P('section', None, None, 'tensor'), may hold values from -0.21875 to 0.21875
- out_weight: bfloat16 [2, 768, 768], P('section', 'tensor'), may hold values from -2.5 to 2.5
- up_weight: bfloat16 [2, 768, 3072], P('section', None, 'tensor'), may hold values from -0.21875 to 0.21875
- down_weight: bfloat16 [2, 3072, 768], P('section', 'tensor'), may hold values from -0.109375 to 0.109375
- vectors: float32 [2, 3, 768], P('section'), may hold values from -4 to 4
- lengths: int32 [8], P('dp'), may hold values from 1024 to 2048, as said below
- selected: int32 [8, 256], P('dp'), may hold values from 0 to 2047, as said below
- cotangent: bfloat16 [8, 2048, 768], P('dp', 'tensor'), may hold values from -6 to 6
Outputs:
- section_results: float32 [2, 8, 2048, 768], P('section', 'dp', 'tensor')
- qkv_grad: float32 [2, 3, 768, 768], P('section', None, 'dp', 'tensor')
- out_proj_grad: float32 [2, 768, 768], P('section', 'tensor', 'dp')
- up_grad: float32 [2, 768, 3072], P('section', 'dp', 'tensor')
- down_grad: float32 [2, 3072, 768], P('section', 'tensor', 'dp')
- vector_grad: float32 [2, 3, 768], P('section', None, 'dp')
Inputs may be any that keep to these rules, and one draw needn't show every extreme that they name: `lengths`: in each group of 2 consecutive sequences one has length 2048; every length is at least half of 2048. `selected`: each row holds 256 distinct positions in increasing order, all below that sequence's length.
All inputs are finite; a program needn't handle non-finite values.
Results may differ from a plain program's by a relative error of at most 0.02.
Values may be sent and summed in bfloat16 or wider, within the bound.
No kernel may reach another device: no remote copies, remote signals or barrier semaphores. Data moves between devices by JAX's collectives and lax.ppermute only.
A program may use at most 256 MiB of HBM per device.

v0:
```python
import functools

import jax
import jax.numpy as jnp
from jax import lax
from jax.experimental import pallas as pl
from jax.experimental.pallas import tpu as pltpu
from jax.sharding import PartitionSpec as P

HEADS = 12
EPSILON = 1e-06
NEGATIVE = -1e30
BF = jnp.bfloat16
F32 = jnp.float32
PAD = 256
MIB = 1 << 20


def swap(block, axis, bit):
    count = lax.axis_size(axis)
    return lax.ppermute(block, axis, [(i, i ^ bit) for i in range(count)])


def hop(block, source, target):
    return lax.ppermute(block, "section", [(source, target)])


def dot(left, right):
    return lax.dot_general(left, right, (((1,), (0,)), ((), ())), preferred_element_type=F32)


def dot_nt(left, right):
    return lax.dot_general(left, right, (((1,), (1,)), ((), ())), preferred_element_type=F32)


def dot_tn(left, right):
    return lax.dot_general(left, right, (((0,), (0,)), ((), ())), preferred_element_type=F32)


def unit_rows(values):
    scale = lax.rsqrt(jnp.mean(values * values, axis=-1, keepdims=True) + EPSILON)
    return values * scale, scale


def norm_back(unit, scale, gain, grad):
    e = grad * gain
    return scale * (e - unit * jnp.mean(e * unit, axis=-1, keepdims=True))


def gelu_pair(x):
    c = 0.7978845608028654
    a = 0.044715
    xx = x * x
    th = jnp.tanh(c * (x + a * (x * xx)))
    half = 0.5 * (1.0 + th)
    slope = half + (0.5 * x) * (1.0 - th * th) * (c * (1.0 + (3.0 * a) * xx))
    return x * half, slope


def lanes(rows, width):
    return lax.broadcasted_iota(jnp.int32, (rows, width), 1)


def subs(rows, width):
    return lax.broadcasted_iota(jnp.int32, (rows, width), 0)


def head_of(values, lane, head, width):
    zero = jnp.zeros_like(values)
    return jnp.where((lane >= head * width) & (lane < (head + 1) * width), values, zero)


def three_pieces(column):
    first = column.astype(BF)
    rest = column - first.astype(F32)
    second = rest.astype(BF)
    third = (rest - second.astype(F32)).astype(BF)
    return first, second, third


def params(limit=56, grid=None):
    if grid is None:
        return pltpu.CompilerParams(vmem_limit_bytes=limit * MIB)
    return pltpu.CompilerParams(
        vmem_limit_bytes=limit * MIB, dimension_semantics=("arbitrary",) * grid
    )


def cost(us):
    return pl.CostEstimate(
        flops=int(us * 1e8), bytes_accessed=int(us * 3.3e6), transcendentals=0
    )


def after(value, *others):
    return lax.optimization_barrier((value,) + others)[0]


VM = pl.BlockSpec(memory_space=pltpu.VMEM)
SM = pl.BlockSpec(memory_space=pltpu.SMEM)
HB = pl.BlockSpec(memory_space=pl.ANY)


def shape(dims, dtype):
    return jax.ShapeDtypeStruct(dims, dtype)


def halves_out(partial, low, keep_ref, send_ref):
    pick = partial.shape[0] // 2
    half = pick // 2
    for s in range(2):
        first = partial[s * pick : s * pick + half]
        second = partial[s * pick + half : (s + 1) * pick]
        keep_ref[s] = jnp.where(low == 0, first, second).astype(BF)
        send_ref[s] = jnp.where(low == 0, second, first).astype(BF)


def halves_in(own_ref, other_ref, low):
    parts = []
    for s in range(2):
        own, other = own_ref[s].astype(F32), other_ref[s].astype(F32)
        parts.append(jnp.where(low == 0, own, other))
        parts.append(jnp.where(low == 0, other, own))
    return jnp.concatenate(parts, 0)


def pick_kernel(rows_ref, sel_ref, keep_ref, send_ref):
    tensor = lax.axis_index("tensor")
    own = rows_ref.shape[1]
    pick = sel_ref.shape[1]
    parts = []
    for s in range(2):
        table = (sel_ref[s : s + 1, :] == subs(own, pick) + tensor * own).astype(F32).astype(BF)
        parts.append(dot_tn(table, rows_ref[s]))
    halves_out(jnp.concatenate(parts, 0), tensor & 1, keep_ref, send_ref)


def pick_rows(rows, selected):
    _, _, d = rows.shape
    out = shape((2, selected.shape[1] // 2, d), BF)
    return pl.pallas_call(
        pick_kernel,
        out_shape=(out, out),
        in_specs=[VM, VM],
        out_specs=(VM, VM),
        compiler_params=params(),
        cost_estimate=cost(3),
        name="pick",
    )(rows, selected)


def routed_attn_kernel(
    heads, info, own_ref, other_ref, gains_ref, qkv_ref, mix_ref,
    picked_ref, normed_ref, q_ref, k_ref, v_ref, mixed_ref, keep_ref, send_ref,
):
    low = info[2]
    picked = halves_in(own_ref, other_ref, low)
    picked_ref[...] = picked.astype(BF)
    unit, _ = unit_rows(picked)
    normed = (unit * gains_ref[0:1, :]).astype(BF)
    normed_ref[...] = normed
    width = qkv_ref.shape[1] // heads
    q = dot_nt(normed, qkv_ref[0]).astype(BF)
    k = dot_nt(normed, qkv_ref[1]).astype(BF)
    v = dot_nt(normed, qkv_ref[2]).astype(BF)
    q = (q.astype(F32) * width ** (-0.5)).astype(BF)
    q_ref[...] = q
    k_ref[...] = k
    v_ref[...] = v
    pick = picked.shape[0] // 2
    lane = lanes(pick, heads * width)
    allowed = lanes(pick, pick) <= subs(pick, pick)
    parts = []
    for s in range(2):
        span = slice(s * pick, (s + 1) * pick)
        total = jnp.zeros((pick, heads * width), F32)
        for h in range(heads):
            scores = dot_nt(head_of(q[span], lane, h, width), k[span])
            scores = jnp.where(allowed, scores, NEGATIVE)
            expos = jnp.exp(scores - jnp.max(scores, axis=-1, keepdims=True))
            probs = expos / jnp.sum(expos, axis=-1, keepdims=True)
            total = total + dot(probs.astype(BF), head_of(v[span], lane, h, width))
        parts.append(total.astype(BF))
    mixed = jnp.concatenate(parts, 0)
    mixed_ref[...] = mixed
    halves_out(dot(mixed, mix_ref[...]), low, keep_ref, send_ref)


def routed_attn(info, own, other, gains, qkv_w, mix_w, heads):
    _, half, d = own.shape
    rows = 4 * half
    cols = qkv_w.shape[1]
    part = shape((2, half, d), BF)
    wide, narrow = shape((rows, d), BF), shape((rows, cols), BF)
    return pl.pallas_call(
        functools.partial(routed_attn_kernel, heads),
        out_shape=(wide, wide, narrow, narrow, narrow, narrow, part, part),
        in_specs=[SM] + [VM] * 5,
        out_specs=(VM,) * 8,
        compiler_params=params(),
        cost_estimate=cost(5),
        name="routed_attn",
    )(info, own, other, gains, qkv_w, mix_w)


def routed_mlp_kernel(
    info, picked_ref, own_ref, other_ref, gains_ref, up_ref, down_ref,
    attn_ref, normed_ref, act_ref, slope_ref, keep_ref, send_ref,
):
    low = info[2]
    attn = halves_in(own_ref, other_ref, low)
    attn_ref[...] = attn.astype(BF)
    unit, _ = unit_rows(picked_ref[...].astype(F32) + attn)
    normed = (unit * gains_ref[1:2, :]).astype(BF)
    normed_ref[...] = normed
    act, slope = gelu_pair(dot(normed, up_ref[...]))
    act = act.astype(BF)
    act_ref[...] = act
    slope_ref[...] = slope
    halves_out(dot(act, down_ref[...]), low, keep_ref, send_ref)


def routed_mlp(info, picked, own, other, gains, up_w, down_w):
    rows, d = picked.shape
    hidden = up_w.shape[1]
    part = shape((2, rows // 4, d), BF)
    return pl.pallas_call(
        routed_mlp_kernel,
        out_shape=(
            shape((rows, d), BF), shape((rows, d), BF), shape((rows, hidden), BF),
            shape((rows, hidden), F32), part, part,
        ),
        in_specs=[SM] + [VM] * 6,
        out_specs=(VM,) * 6,
        compiler_params=params(),
        cost_estimate=cost(6),
        name="routed_mlp",
    )(info, picked, own, other, gains, up_w, down_w)


def update_kernel(picked_ref, attn_ref, mlp_ref, mlp2_ref, gains_ref, both_ref, update_ref):
    d = picked_ref.shape[2]
    weight = gains_ref[2:3, :] * d ** (-0.5)
    for s in range(2):
        router = jnp.sum(picked_ref[s].astype(F32) * weight, axis=-1, keepdims=True)
        both = attn_ref[s].astype(F32) + (mlp_ref[s].astype(F32) + mlp2_ref[s].astype(F32))
        both_ref[s] = both.astype(BF)
        update_ref[s] = (router * both).astype(BF)


def make_update(picked_half, attn_half, mlp_half, mlp_far, gains):
    out = shape(picked_half.shape, BF)
    return pl.pallas_call(
        update_kernel,
        out_shape=(out, out),
        in_specs=[VM] * 5,
        out_specs=(VM, VM),
        compiler_params=params(),
        cost_estimate=cost(2.5),
        name="update",
    )(picked_half, attn_half, mlp_half, mlp_far, gains)


def routed_back_mlp_kernel(
    info, sel_own, sel_back, sel_other, picked_ref, attn_ref, gains_ref, slope_ref, up_ref, down_ref,
    d_sel_ref, d_mlp_ref, d_pre_ref, gain_ref, keep_ref, send_ref,
):
    low = info[2]
    d = picked_ref.shape[1]
    parts = []
    for s, own in enumerate((sel_own[...], sel_back[...])):
        other = sel_other[s]
        parts += [jnp.where(low == 0, own, other), jnp.where(low == 0, other, own)]
    d_sel = jnp.concatenate(parts, 0).astype(F32)
    d_sel_ref[...] = d_sel
    picked = picked_ref[...].astype(F32)
    router = jnp.sum(picked * (gains_ref[2:3, :] * d ** (-0.5)), axis=-1, keepdims=True)
    d_mlp = (router * d_sel).astype(BF)
    d_mlp_ref[...] = d_mlp
    d_pre = (dot_nt(d_mlp, down_ref[...]) * slope_ref[...]).astype(BF)
    d_pre_ref[...] = d_pre
    d_normed = dot_nt(d_pre, up_ref[...])
    unit, _ = unit_rows(picked + attn_ref[...].astype(F32))
    gain_ref[...] = jnp.sum(d_normed * unit, axis=0, keepdims=True)
    halves_out(d_normed, low, keep_ref, send_ref)


def routed_back_mlp(info, sel_own, sel_back, sel_other, picked, attn, gains, slope, up_w, down_w):
    rows, d = picked.shape
    hidden = up_w.shape[1]
    part = shape((2, rows // 4, d), BF)
    return pl.pallas_call(
        routed_back_mlp_kernel,
        out_shape=(
            shape((rows, d), F32), shape((rows, d), BF), shape((rows, hidden), BF),
            shape((1, d), F32), part, part,
        ),
        in_specs=[SM] + [VM] * 9,
        out_specs=(VM,) * 6,
        compiler_params=params(),
        cost_estimate=cost(6),
        name="routed_back_mlp",
    )(info, sel_own, sel_back, sel_other, picked, attn, gains, slope, up_w, down_w)


def routed_back_attn_kernel(
    heads, info, own_ref, other_ref, d_sel_ref, picked_ref, attn_ref, both_own, both_other,
    gains_ref, q_ref, k_ref, v_ref, qkv_ref, mix_ref,
    d_mid_ref, d_low_ref, d_qkv_ref, vec_ref, keep_ref, send_ref,
):
    low = info[2]
    rows, d = picked_ref.shape
    d_normed2 = halves_in(own_ref, other_ref, low)
    picked = picked_ref[...].astype(F32)
    d_sel = d_sel_ref[...]
    router_row = gains_ref[2:3, :] * d ** (-0.5)
    router = jnp.sum(picked * router_row, axis=-1, keepdims=True)
    unit2, scale2 = unit_rows(picked + attn_ref[...].astype(F32))
    d_mid = norm_back(unit2, scale2, gains_ref[1:2, :], d_normed2)
    both = halves_in(both_own, both_other.at[2:], low)
    d_router = jnp.sum(d_sel * both, axis=-1, keepdims=True)
    d_mid_ref[...] = d_mid + d_router * router_row
    d_weight = jnp.sum(picked * d_router, axis=0, keepdims=True) * d ** (-0.5)
    vec_ref[1:2, :] = jnp.where(info[0] == 0, d_weight, jnp.zeros_like(d_weight))
    d_low = (router * d_sel + d_mid).astype(BF)
    d_low_ref[...] = d_low
    d_mixed = dot_nt(d_low, mix_ref[...]).astype(BF)
    width = qkv_ref.shape[1] // heads
    pick = rows // 2
    lane = lanes(pick, heads * width)
    allowed = subs(pick, pick) <= lanes(pick, pick)
    dq_parts, dk_parts, dv_parts = [], [], []
    for s in range(2):
        span = slice(s * pick, (s + 1) * pick)
        q, k, v, dm = q_ref[span, :], k_ref[span, :], v_ref[span, :], d_mixed[span]
        dq = jnp.zeros((pick, heads * width), F32)
        dk, dv = dq, dq
        for h in range(heads):
            qh, kh = head_of(q, lane, h, width), head_of(k, lane, h, width)
            dh = head_of(dm, lane, h, width)
            scores = jnp.where(allowed, dot_nt(k, qh), NEGATIVE)
            expos = jnp.exp(scores - jnp.max(scores, axis=0, keepdims=True))
            probs = expos / jnp.sum(expos, axis=0, keepdims=True)
            d_probs = dot_nt(v, dh)
            inner = jnp.sum(probs * d_probs, axis=0, keepdims=True)
            d_scores = (probs * (d_probs - inner)).astype(BF)
            dv = dv + dot(probs.astype(BF), dh)
            dk = dk + dot(d_scores, qh)
            dq = dq + dot_tn(d_scores, kh)
        dq_parts.append(dq * width ** (-0.5))
        dk_parts.append(dk)
        dv_parts.append(dv)
    d_normed = jnp.zeros((rows, d), F32)
    for i, parts in enumerate((dq_parts, dk_parts, dv_parts)):
        whole = jnp.concatenate(parts, 0).astype(BF)
        d_qkv_ref[i] = whole
        d_normed = d_normed + dot(whole, qkv_ref[i])
    unit, _ = unit_rows(picked)
    vec_ref[0:1, :] = jnp.sum(d_normed * unit, axis=0, keepdims=True)
    halves_out(d_normed, low, keep_ref, send_ref)


def routed_back_attn(
    info, own, other, d_sel, picked, attn, both_own, both_other, gains, q, k, v, qkv_w, mix_w, heads
):
    rows, d = picked.shape
    part = shape((2, rows // 4, d), BF)
    return pl.pallas_call(
        functools.partial(routed_back_attn_kernel, heads),
        out_shape=(
            shape((rows, d), F32), shape((rows, d), BF), shape((3,) + q.shape, BF),
            shape((2, d), F32), part, part,
        ),
        in_specs=[SM] + [VM] * 13,
        out_specs=(VM,) * 6,
        compiler_params=params(),
        cost_estimate=cost(8),
        name="routed_back_attn",
    )(info, own, other, d_sel, picked, attn, both_own, both_other, gains, q, k, v, qkv_w, mix_w)


def finish_kernel(
    info, own_ref, other_ref, d_mid_ref, picked_ref, gains_ref, sel_ref,
    d_rows_ref, far_ref, sent_ref, result_ref, out_ref,
):
    tensor, section, low = info[0], info[1], info[2]
    own = d_rows_ref.shape[0]
    pick = sel_ref.shape[1]

    @pl.when(section == 0)
    def _():
        d_normed = halves_in(own_ref, other_ref, low)
        unit, scale = unit_rows(picked_ref[...].astype(F32))
        d_picked = d_mid_ref[...] + norm_back(unit, scale, gains_ref[0:1, :], d_normed)
        d_picked = d_picked.astype(BF)
        for s in range(2):
            table = (sel_ref[s : s + 1, :] == subs(own, pick) + tensor * own).astype(F32).astype(BF)
            base = (d_rows_ref if s == 0 else far_ref)[...].astype(F32)
            out_ref[s] = base + dot(table, d_picked[s * pick : (s + 1) * pick])

    @pl.when(section != 0)
    def _():
        out_ref[0] = sent_ref[...].astype(F32)
        out_ref[1] = result_ref[...]


def finish(info, own, other, d_mid, picked, gains, sel_row, d_rows, far, sent, result):
    rows, d = d_rows.shape
    return pl.pallas_call(
        finish_kernel,
        out_shape=shape((2, rows, d), F32),
        in_specs=[SM] + [VM] * 10,
        out_specs=VM,
        compiler_params=params(),
        cost_estimate=cost(6),
        name="finish",
    )(info, own, other, d_mid, picked, gains, sel_row, d_rows, far, sent, result)


def pack_kernel(gains_ref, qkv_ref, mix_ref, out_ref):
    cols, d = mix_ref.shape
    for n in range(3):
        out_ref[n * cols : (n + 1) * cols, :] = qkv_ref[n]
    out_ref[3 * cols : 4 * cols, :] = mix_ref[...]
    rows = subs(16, d)
    extra = jnp.zeros((16, d), F32)
    for n in range(3):
        for p, piece in enumerate(three_pieces(gains_ref[n : n + 1, :])):
            extra = jnp.where(rows == 3 * n + p, piece.astype(F32), extra)
    out_ref[4 * cols :, :] = extra.astype(BF)


def pack_weights(gains, qkv_w, mix_w):
    cols, d = mix_w.shape
    return pl.pallas_call(
        pack_kernel,
        out_shape=shape((4 * cols + 16, d), BF),
        in_specs=[VM] * 3,
        out_specs=VM,
        compiler_params=params(),
        cost_estimate=cost(2),
        name="pack",
    )(gains, qkv_w, mix_w)


def prepare_kernel(info, g0, q0, m0, far_ref, gains_ref, qkv_ref, mix_ref):
    cols = m0.shape[0]
    own = info[1] == 1
    extra = far_ref[4 * cols :, :].astype(F32)
    for n in range(3):
        far = (extra[3 * n : 3 * n + 1] + extra[3 * n + 1 : 3 * n + 2]) + extra[3 * n + 2 : 3 * n + 3]
        gains_ref[n : n + 1, :] = jnp.where(own, g0[n : n + 1, :], far)
    qkv_ref[...] = jnp.zeros_like(qkv_ref)
    for n in range(3):
        qkv_ref[n, :cols, :] = jnp.where(own, q0[n], far_ref[n * cols : (n + 1) * cols, :])
    mix_ref[...] = jnp.zeros_like(mix_ref)
    mix_ref[:cols, :] = jnp.where(own, m0[...], far_ref[3 * cols : 4 * cols, :])


def prepare(info, gains, qkv_w, mix_w, far):
    d = mix_w.shape[1]
    return pl.pallas_call(
        prepare_kernel,
        out_shape=(shape(gains.shape, F32), shape((3, PAD, d), BF), shape((PAD, d), BF)),
        in_specs=[SM] + [VM] * 4,
        out_specs=(VM,) * 3,
        compiler_params=params(),
        cost_estimate=cost(2),
        name="prepare",
    )(info, gains, qkv_w, mix_w, far)


def project_kernel(
    heads, width, info, tok0, tok1, tok2a, tok2b, tok3a, tok3b, upd_own, upd_other, sel_ref,
    gains_ref, qkv_ref, rows_ref, normed_ref, q_ref, k_ref, v_ref, buf,
):
    tensor, low, length = info[0], info[2], info[3]
    r = pl.program_id(0)
    own, d = buf.shape
    for i, tok in enumerate((tok0, tok1)):
        @pl.when(r == i)
        def _():
            buf[...] = tok[...]

    for i, tok_a, tok_b in ((2, tok2a, tok2b), (3, tok3a, tok3b)):
        @pl.when(r == i)
        def _():
            buf[: own // 2] = tok_a[...]
            buf[own // 2 :] = tok_b[...]

    place = jnp.bitwise_xor(r, tensor) * own
    pick = sel_ref.shape[1]
    first, second = upd_own[...], upd_other[...]
    update = jnp.concatenate(
        [jnp.where(low == 0, first, second), jnp.where(low == 0, second, first)], 0
    )
    sel = jnp.where(info[1] == 0, sel_ref[0:1, :], sel_ref[1:2, :])
    table = (sel == subs(own, pick) + place).astype(F32).astype(BF)
    rows = (buf[...].astype(F32) + dot(table, update)).astype(BF)

    @pl.when(r == 0)
    def _():
        rows_ref[...] = rows

    unit, _ = unit_rows(rows.astype(F32))
    normed = (unit * gains_ref[0:1, :]).astype(BF)
    normed_ref[0] = normed
    lane = lanes(own, PAD)
    cols = heads * width
    one, zero = jnp.float32(1), jnp.float32(0)
    q = dot_nt(normed, qkv_ref[0]).astype(BF).astype(F32) * width ** (-0.5)
    q_ref[0] = jnp.where(lane == cols + 3, one, q).astype(BF)
    key_at = subs(own, PAD) + place
    extra = jnp.where(lane < cols + 3, one, jnp.where(key_at < length, zero, NEGATIVE))
    k = dot_nt(normed, qkv_ref[1])
    k_ref[0] = jnp.where((lane >= cols) & (lane < cols + 4), extra, k).astype(BF)
    v = dot_nt(normed, qkv_ref[2])
    v_ref[0] = jnp.where((lane >= cols) & (lane < cols + 3), one, v).astype(BF)


def project(info, toks, upd_own, upd_other, sel, gains, qkv_w, heads, width, count):
    own, d = toks[0].shape
    full = lambda dims: pl.BlockSpec(dims, lambda r, info: (0,) * len(dims))
    placed = lambda w: pl.BlockSpec((1, own, w), lambda r, info: (jnp.bitwise_xor(r, info[0]), 0, 0))
    padded = shape((count, own, PAD), BF)
    return pl.pallas_call(
        functools.partial(project_kernel, heads, width),
        out_shape=(shape((own, d), BF), shape((count, own, d), BF), padded, padded, padded),
        grid_spec=pltpu.PrefetchScalarGridSpec(
            num_scalar_prefetch=1,
            grid=(count,),
            in_specs=[full(tok.shape) for tok in toks]
            + [full(upd_own.shape)] * 2
            + [full(sel.shape), full(gains.shape), full(qkv_w.shape)],
            out_specs=(full((own, d)), placed(d), placed(PAD), placed(PAD), placed(PAD)),
            scratch_shapes=[pltpu.VMEM((own, d), BF)],
        ),
        compiler_params=params(grid=1),
        cost_estimate=cost(9),
        name="project",
    )(info, *toks, upd_own, upd_other, sel, gains, qkv_w)


def attention_kernel(
    heads, width, base, per, info, q_ref, k_ref, v_ref, mix_ref,
    send_ref, keep_ref, mixed_ref, lse_ref,
):
    i = pl.program_id(0)
    block = q_ref.shape[1]
    cols = heads * width
    steps = k_ref.shape[0] // block
    place = jnp.bitwise_xor(base + 1 - i // per, info[0]) * per + i % per

    def run(step):
        span = (step + 1) * block
        q = q_ref[0]
        lane = lanes(block, PAD)
        total = jnp.zeros((block, PAD), F32)
        lse = jnp.zeros((block, 128), F32)
        zero = jnp.zeros_like(q)
        for h in range(heads):
            here = (lane >= h * width) & (lane < (h + 1) * width)
            qh = jnp.where(here | (lane == cols + 3), q, zero)
            scores = dot_nt(qh, k_ref[0:span, :])
            causal = lanes(block, block) <= subs(block, block)
            tail = jnp.where(causal, scores[:, span - block :], NEGATIVE)
            high = jnp.max(tail, axis=-1, keepdims=True)
            if step:
                high = jnp.maximum(high, jnp.max(scores[:, : span - block], axis=-1, keepdims=True))
            probs = jnp.exp(tail - high).astype(BF)
            if step:
                probs = jnp.concatenate(
                    [jnp.exp(scores[:, : span - block] - high).astype(BF), probs], 1
                )
            out = dot(probs, v_ref[0:span, :])
            norm = jnp.sum(jnp.where(lane == cols, out, 0.0), axis=-1, keepdims=True)
            total = jnp.where(here, out / norm, total)
            lse = jnp.where(lanes(block, 128) == h, high + jnp.log(norm), lse)
        lse_ref[0] = lse
        mixed = total.astype(BF)
        mixed_ref[0] = mixed
        part = dot(mixed, mix_ref[...]).astype(BF)

        @pl.when(i < per)
        def _():
            send_ref[...] = part

        @pl.when(i >= per)
        def _():
            keep_ref[...] = part

    for step in range(steps):
        @pl.when(place == step)
        def _():
            run(step)


def attention(info, q, k, v, mix_w, heads, width, base, block=256):
    count, own, _ = q.shape
    total = count * own
    d = mix_w.shape[1]
    per = own // block
    k, v = k.reshape(total, PAD), v.reshape(total, PAD)
    full = lambda dims: pl.BlockSpec(dims, lambda i, info: (0,) * len(dims))
    rel = lambda w: pl.BlockSpec((1, block, w), lambda i, info: (1 - i // per, i % per, 0))
    out = shape((own, d), BF)
    return pl.pallas_call(
        functools.partial(attention_kernel, heads, width, base, per),
        out_shape=(out, out, shape((2, own, PAD), BF), shape((2, own, 128), F32)),
        grid_spec=pltpu.PrefetchScalarGridSpec(
            num_scalar_prefetch=1,
            grid=(2 * per,),
            in_specs=[
                pl.BlockSpec(
                    (1, block, PAD),
                    lambda i, info: (
                        jnp.bitwise_xor(base + 1 - i // per, info[0]), i % per, 0,
                    ),
                ),
                full(k.shape), full(v.shape), full(mix_w.shape),
            ],
            out_specs=(
                pl.BlockSpec((block, d), lambda i, info: (jnp.minimum(i, per - 1), 0)),
                pl.BlockSpec((block, d), lambda i, info: (jnp.maximum(i - per, 0), 0)),
                rel(PAD), rel(128),
            ),
        ),
        compiler_params=params(grid=1),
        cost_estimate=cost(0.3),
        name="attention",
    )(info, q, k, v, mix_w)


def mlp_kernel(
    half, rows_ref, keep_ref, near_ref, far_ref, cot_ref, gains_ref,
    p0a, p0b, p1a, p1b, p2a, p2b, p3a, p3b,
    result_ref, low_ref, d_mid_ref, d_mid_low_ref, keep_out, send_out,
    vec_ref, up_v, down_v, slope_v, act_v, pre_v, rows_v, result_v, low_v, sems, out_sems,
):
    leaving = []

    def leave(src, dst):
        copy = pltpu.make_async_copy(src, dst, out_sems.at[len(leaving)])
        copy.start()
        leaving.append(copy)

    parity = lax.axis_index("dp") & 1
    first = pl.ds(pl.multiple_of(parity * half, half), half)
    second = pl.ds(pl.multiple_of((1 - parity) * half, half), half)
    copies = {}
    count = 0
    for i in range(4):
        for n, (name, dest) in enumerate((("up", up_v), ("down", down_v))):
            a, b = ((p0a, p0b), (p1a, p1b), (p2a, p2b), (p3a, p3b))[i]
            moves = [(a.at[n], dest.at[i, first, :]), (b.at[n], dest.at[i, second, :])]
            some = []
            for src, dst in moves:
                copy = pltpu.make_async_copy(src, dst, sems.at[count])
                copy.start()
                some.append(copy)
                count += 1
            copies[name, i] = some
    attn = keep_ref[...].astype(F32) + near_ref[...].astype(F32) + far_ref[...].astype(F32)
    middle = rows_ref[...].astype(F32) + attn
    unit2, scale2 = unit_rows(middle)
    normed = (unit2 * gains_ref[1:2, :]).astype(BF)
    rows_v[0] = normed
    leave(rows_v.at[0], send_out.at[4])
    mlp = jnp.zeros_like(middle)
    for i in range(4):
        for copy in copies["up", i]:
            copy.wait()
        act, slope = gelu_pair(dot(normed, up_v[i]))
        act = act.astype(BF)
        act_v[i] = act
        leave(act_v.at[i], (keep_out if i % 2 == 0 else send_out).at[i // 2])
        slope_v[i] = slope
        for copy in copies["down", i]:
            copy.wait()
        mlp = mlp + dot(act, down_v[i])
    unit3, scale3 = unit_rows(middle + mlp)
    gain3 = gains_ref[2:3, :]
    result = unit3 * gain3
    result_v[...] = result
    leave(result_v, result_ref)
    low_v[...] = result.astype(BF)
    leave(low_v, low_ref)
    cot = cot_ref[0].astype(F32)
    vec_ref[1:2, :] = jnp.sum(cot * unit3, axis=0, keepdims=True)
    d_final = norm_back(unit3, scale3, gain3, cot)
    d_mlp = d_final.astype(BF)
    rows_v[1] = d_mlp
    leave(rows_v.at[1], send_out.at[5])
    d_normed = jnp.zeros_like(middle)
    for i in range(4):
        d_pre = (dot_nt(d_mlp, down_v[i]) * slope_v[i]).astype(BF)
        pre_v[i] = d_pre
        leave(pre_v.at[i], (keep_out if i % 2 == 0 else send_out).at[2 + i // 2])
        d_normed = d_normed + dot_nt(d_pre, up_v[i])
    vec_ref[0:1, :] = jnp.sum(d_normed * unit2, axis=0, keepdims=True)
    d_mid = d_final + norm_back(unit2, scale2, gains_ref[1:2, :], d_normed)
    d_mid_ref[...] = d_mid
    low = d_mid.astype(BF)
    d_mid_low_ref[...] = low
    rows_v[2] = low
    leave(rows_v.at[2], send_out.at[6])
    for copy in leaving:
        copy.wait()


def mlp_pass(rows, keep, near, far, cot, gains, pieces):
    own, d = rows.shape
    hidden = pieces[0].shape[2]
    half = d // 2
    wide, low = shape((own, d), F32), shape((own, d), BF)
    return pl.pallas_call(
        functools.partial(mlp_kernel, half),
        out_shape=(
            wide, low, wide, low, shape((4, own, d), BF), shape((7, own, d), BF), shape((2, d), F32)
        ),
        in_specs=[VM] * 6 + [HB] * 8,
        out_specs=(HB, HB, VM, VM, HB, HB, VM),
        scratch_shapes=[
            pltpu.VMEM((4, d, hidden), BF),
            pltpu.VMEM((4, hidden, d), BF),
            pltpu.VMEM((4, own, hidden), F32),
            pltpu.VMEM((4, own, hidden), BF),
            pltpu.VMEM((4, own, hidden), BF),
            pltpu.VMEM((3, own, d), BF),
            pltpu.VMEM((own, d), F32),
            pltpu.VMEM((own, d), BF),
            pltpu.SemaphoreType.DMA((16,)),
            pltpu.SemaphoreType.DMA((13,)),
        ],
        compiler_params=params(60),
        cost_estimate=cost(21),
        name="dense_mlp",
    )(rows, keep, near, far, cot, gains, *pieces)


FIRST = 8


def far_grads_kernel(
    act_ref, pre_ref, near_ref, own_ref, act2_ref, pre2_ref, near2_ref, rows2_ref,
    cross_ref, hop_ref, first_ref,
):
    i = pl.program_id(0)
    d = own_ref.shape[2]
    part = first_ref.shape[0]

    @pl.when(i == 0)
    def _():
        up = dot_tn(own_ref[0], pre_ref[0]) + dot_tn(rows2_ref[0], pre2_ref[0])
        cross_ref[:d] = up.astype(BF)

    @pl.when(i == 1)
    def _():
        rows, rows2 = own_ref[0], rows2_ref[0]
        down = (dot_tn(rows, act_ref[0]) + dot_tn(rows2, act2_ref[0])).astype(BF)
        cross_ref[d:] = down[:part]
        hop_ref[0] = down[part:]
        near = (dot_tn(rows, near_ref[0]) + dot_tn(rows2, near2_ref[0])).astype(BF)
        first_ref[...] = near[:part]
        hop_ref[1] = near[part:]


def near_grads_kernel(pre_ref, own_ref, pre2_ref, rows2_ref, first_ref, crossed_ref, out_ref):
    d = own_ref.shape[2]
    up = dot_tn(own_ref[0], pre_ref[0]) + dot_tn(rows2_ref[0], pre2_ref[0])
    out_ref[:d] = (up + crossed_ref[:d].astype(F32)).astype(BF)
    out_ref[d:] = (first_ref[...].astype(F32) + crossed_ref[d:].astype(F32)).astype(BF)


def far_grads(keep, send, other):
    _, own, d = keep.shape
    part = d // FIRST
    at = lambda n: pl.BlockSpec((1, own, d), lambda i: (n, 0, 0))
    pair = pl.BlockSpec((1, own, d), lambda i: (4 + i, 0, 0))
    return pl.pallas_call(
        far_grads_kernel,
        out_shape=(
            shape((d + part, d), BF), shape((2, d - part, d), BF), shape((part, d), BF)
        ),
        grid=(2,),
        in_specs=[at(1), at(3), at(0), pair, at(1), at(3), at(0), pair],
        out_specs=(
            pl.BlockSpec((d + part, d), lambda i: (0, 0)),
            pl.BlockSpec((2, d - part, d), lambda i: (0, 0, 0)),
            pl.BlockSpec((part, d), lambda i: (0, 0)),
        ),
        compiler_params=params(56, grid=1),
        cost_estimate=cost(5),
        name="far_grads",
    )(keep, keep, keep, send, other, other, other, other)


def near_grads(keep, send, other, first, crossed):
    _, own, d = keep.shape
    at = lambda n: pl.BlockSpec((1, own, d), lambda i: (n, 0, 0))
    full = lambda a: pl.BlockSpec(a.shape, lambda i: (0, 0))
    return pl.pallas_call(
        near_grads_kernel,
        out_shape=shape(crossed.shape, BF),
        grid=(1,),
        in_specs=[at(2), at(4), at(2), at(4), full(first), full(crossed)],
        out_specs=full(crossed),
        compiler_params=params(56, grid=1),
        cost_estimate=cost(5),
        name="near_grads",
    )(keep, send, other, other, first, crossed)


def attention_back_kernel(
    heads, width, block, info, g0, g1, g2, g3, q_ref, k_ref, v_ref, mixed_n, mixed_f, lse_n, lse_f,
    mix_ref, qkv_ref, sel_ref, d_qkv_ref, keep_ref, send_ref, mid_ref,
    qs, ds, dq_acc, dk_acc, dv_acc,
):
    tensor, low = info[0], info[2]
    own = g0.shape[0]
    cols = heads * width
    total = k_ref.shape[0]
    lane = lanes(own, PAD)
    zero = jnp.zeros((own, PAD), BF)
    grads = (g0[...], g1[0], g2[...], g3[...])
    for r, grad in enumerate(grads):
        at = pl.multiple_of(jnp.bitwise_xor(tensor, r) * own, own)
        span = pl.ds(at, own)
        d_mixed = dot_nt(grad, mix_ref[...]).astype(BF)
        inner = d_mixed.astype(F32) * (mixed_n if r < 2 else mixed_f)[r % 2].astype(F32)
        q = q_ref[span, :]
        lse = (lse_n if r < 2 else lse_f)[r % 2]
        for h in range(heads):
            here = (lane >= h * width) & (lane < (h + 1) * width)
            delta = -jnp.sum(jnp.where(here, inner, 0.0), axis=-1, keepdims=True)
            row_lse = -jnp.sum(jnp.where(lanes(own, 128) == h, lse, 0.0), axis=-1, keepdims=True)
            left = jnp.where(here | (lane == cols + 3), q, zero)
            right = jnp.where(here, d_mixed, zero)
            for p, (a, b) in enumerate(zip(three_pieces(row_lse), three_pieces(delta))):
                left = jnp.where(lane == cols + p, a, left)
                right = jnp.where(lane == cols + p, b, right)
            qs[h, span, :] = left
            ds[h, span, :] = right
    dq_acc[...] = jnp.zeros_like(dq_acc)
    lane_k = lanes(block, PAD)
    allowed = subs(block, block) <= lanes(block, block)
    for j in range(total // block):
        first = j * block
        k, v = k_ref[first : first + block, :], v_ref[first : first + block, :]
        dk = jnp.zeros((block, PAD), F32)
        dv = jnp.zeros((block, PAD), F32)
        stacked, keys = [], []
        for h in range(heads):
            qh, dh = qs[h, first:, :], ds[h, first:, :]
            scores = dot_nt(k, qh)
            d_probs = dot_nt(v, dh)
            head = jnp.where(allowed, scores[:, :block], NEGATIVE)
            probs = jnp.exp(head)
            if first + block < total:
                probs = jnp.concatenate([probs, jnp.exp(scores[:, block:])], 1)
            d_scores = (probs * d_probs).astype(BF)
            dv = dv + dot(probs.astype(BF), dh)
            dk = dk + dot(d_scores, qh)
            stacked.append(d_scores)
            keys.append(
                jnp.where((lane_k >= h * width) & (lane_k < (h + 1) * width), k, jnp.zeros_like(k))
            )
        dq_acc[first:, :] += dot_tn(jnp.concatenate(stacked, 0), jnp.concatenate(keys, 0))
        dk_acc[...] = dk
        dv_acc[...] = dv
        d_qkv_ref[1, first : first + block, :] = dk_acc[:, :cols].astype(BF)
        d_qkv_ref[2, first : first + block, :] = dv_acc[:, :cols].astype(BF)
    d_qkv_ref[0] = (dq_acc[:, :cols] * width ** (-0.5)).astype(BF)
    pick = sel_ref.shape[1]
    sel = jnp.where(info[1] == 0, sel_ref[0:1, :], sel_ref[1:2, :])
    table = (sel == subs(total, pick)).astype(F32).astype(BF)
    part = jnp.zeros((pick, qkv_ref.shape[2]), F32)
    for i in range(3):
        part = part + dot(dot_tn(table, d_qkv_ref[i]).astype(BF), qkv_ref[i][:cols, :])
    half = pick // 2
    keep_ref[...] = jnp.where(low == 0, part[:half], part[half:]).astype(BF)
    send_ref[...] = jnp.where(low == 0, part[half:], part[:half]).astype(BF)
    mine = jnp.where(low == 0, sel[:, :half], sel[:, half:])
    mid = jnp.zeros((half, qkv_ref.shape[2]), F32)
    for r, grad in enumerate(grads):
        table = (mine == subs(own, half) + jnp.bitwise_xor(tensor, r) * own).astype(F32).astype(BF)
        mid = mid + dot_tn(table, grad)
    mid_ref[...] = mid.astype(BF)


def attention_back(
    info, grads, q, k, v, mixed, lse, mix_w, qkv_w, selected, heads, width, block=256
):
    keep, other, far, far_other = grads
    own, d = keep.shape
    total = k.shape[0] * k.shape[1]
    flat = lambda a: a.reshape(total, PAD)
    half = shape((selected.shape[1] // 2, d), BF)
    at = lambda n: pl.BlockSpec((1, own, d), lambda i: (n, 0, 0))
    full = lambda a: pl.BlockSpec(a.shape, lambda i: (0,) * a.ndim)
    rest = (flat(q), flat(k), flat(v), *mixed, *lse, mix_w, qkv_w, selected)
    return pl.pallas_call(
        functools.partial(attention_back_kernel, heads, width, block),
        out_shape=(shape((3, total, heads * width), BF), half, half, half),
        grid=(1,),
        in_specs=[SM, full(keep), at(6), full(far), full(far_other)] + [full(a) for a in rest],
        out_specs=(
            pl.BlockSpec((3, total, heads * width), lambda i: (0, 0, 0)),
        ) + (pl.BlockSpec(half.shape, lambda i: (0, 0)),) * 3,
        scratch_shapes=[
            pltpu.VMEM((heads, total, PAD), BF),
            pltpu.VMEM((heads, total, PAD), BF),
            pltpu.VMEM((total, PAD), F32),
            pltpu.VMEM((block, PAD), F32),
            pltpu.VMEM((block, PAD), F32),
        ],
        compiler_params=params(60, grid=1),
        cost_estimate=cost(35),
        name="attention_back",
    )(info, keep, other, far, far_other, *rest)


def spread_back_kernel(cols, info, d_ref, qkv_ref, send_ref, keep_ref):
    i = pl.program_id(0)
    total = dot(d_ref[0, 0], qkv_ref[0][:cols, :])
    for n in (1, 2):
        total = total + dot(d_ref[n, 0], qkv_ref[n][:cols, :])
    total = total.astype(BF)

    @pl.when(i < 2)
    def _():
        send_ref[0] = total

    @pl.when(i >= 2)
    def _():
        keep_ref[0] = total


def spread_back(info, d_qkv, qkv_w, count):
    _, total, cols = d_qkv.shape
    own = total // count
    d = qkv_w.shape[2]
    pos = lambda i: jnp.where(i < 2, 3 - 2 * i, 6 - 2 * i)
    out = shape((2, own, d), BF)
    return pl.pallas_call(
        functools.partial(spread_back_kernel, cols),
        out_shape=(out, out),
        grid_spec=pltpu.PrefetchScalarGridSpec(
            num_scalar_prefetch=1,
            grid=(count,),
            in_specs=[
                pl.BlockSpec(
                    (3, 1, own, cols), lambda i, info: (0, jnp.bitwise_xor(pos(i), info[0]), 0, 0)
                ),
                pl.BlockSpec(qkv_w.shape, lambda i, info: (0, 0, 0)),
            ],
            out_specs=(
                pl.BlockSpec((1, own, d), lambda i, info: (1 - jnp.minimum(i, 1), 0, 0)),
                pl.BlockSpec((1, own, d), lambda i, info: (1 - jnp.maximum(i - 2, 0), 0, 0)),
            ),
        ),
        compiler_params=params(grid=1),
        cost_estimate=cost(5),
        name="spread_back",
    )(info, d_qkv.reshape(3, count, own, cols), qkv_w)


def attn_grads_kernel(
    cols, info, d_ref, normed_ref, g0, g1, g2, g3, mixed_n, mixed_f, pack_ref, acc,
):
    i = pl.program_id(0)

    @pl.when(i == 0)
    def _():
        acc[...] = jnp.zeros_like(acc)

    for n in range(3):
        acc[n * cols : (n + 1) * cols, :] += dot_tn(d_ref[n, 0], normed_ref[0])
    for r, grad in enumerate((g0, g1, g2, g3)):
        @pl.when(i == r)
        def _():
            mixed = (mixed_n if r < 2 else mixed_f)[r % 2]
            rows = grad[0] if r == 1 else grad[...]
            acc[3 * cols :, :] += dot_tn(mixed[:, :cols], rows)

    @pl.when(i == 3)
    def _():
        pack_ref[...] = jnp.transpose(acc[...]).astype(BF)


def attn_grads(info, d_qkv, normed, grads, mixed):
    _, total, cols = d_qkv.shape
    count, own, d = normed.shape
    full = lambda dims: pl.BlockSpec(dims, lambda i, info: (0,) * len(dims))
    return pl.pallas_call(
        functools.partial(attn_grads_kernel, cols),
        out_shape=shape((d, 4 * cols), BF),
        grid_spec=pltpu.PrefetchScalarGridSpec(
            num_scalar_prefetch=1,
            grid=(count,),
            in_specs=[
                pl.BlockSpec(
                    (3, 1, own, cols), lambda i, info: (0, jnp.bitwise_xor(i, info[0]), 0, 0)
                ),
                pl.BlockSpec((1, own, d), lambda i, info: (jnp.bitwise_xor(i, info[0]), 0, 0)),
            ]
            + [
                full((own, d)), pl.BlockSpec((1, own, d), lambda i, info: (6, 0, 0)),
                full((own, d)), full((own, d)),
            ]
            + [full(mixed[0].shape)] * 2,
            out_specs=full((d, 4 * cols)),
            scratch_shapes=[pltpu.VMEM((4 * cols, d), F32)],
        ),
        compiler_params=params(grid=1),
        cost_estimate=cost(8),
        name="attn_grads",
    )(info, d_qkv.reshape(3, count, own, cols), normed, *grads, *mixed)


def routed_mlp_grads_kernel(
    info, normed_ref, pre_ref, act_ref, grad_ref, part_ref, far_ref, last_ref, last_far, last_cross,
    pack_ref,
):
    hidden = pre_ref.shape[1]

    @pl.when(info[1] == 0)
    def _():
        pack_ref[:, :hidden] = dot_tn(normed_ref[...], pre_ref[...]).astype(BF)
        pack_ref[:, hidden:] = dot_tn(grad_ref[...], act_ref[...]).astype(BF)

    @pl.when(info[1] != 0)
    def _():
        d = normed_ref.shape[1]
        total = (part_ref[...].astype(F32) + far_ref[...].astype(F32)).astype(BF)
        part = part_ref.shape[0] - d
        pack_ref[:, :hidden] = total[:d]
        pack_ref[:part, hidden:] = total[d:]
        total = last_ref[1].astype(F32) + last_far[1].astype(F32) + last_cross[...].astype(F32)
        pack_ref[part:, hidden:] = total.astype(BF)


def routed_mlp_grads(info, normed, pre, act, grad, *dense):
    return pl.pallas_call(
        routed_mlp_grads_kernel,
        out_shape=shape((normed.shape[1], 2 * pre.shape[1]), BF),
        in_specs=[SM] + [VM] * 9,
        out_specs=VM,
        compiler_params=params(),
        cost_estimate=cost(5),
        name="routed_mlp_grads",
    )(info, normed, pre, act, grad, *dense)


def routed_attn_grads_kernel(
    info, normed_ref, d_ref, low_ref, mixed_ref, part_ref, hop_ref, vec_ref, pack_ref
):
    cols = mixed_ref.shape[1]
    wide = 4 * cols
    vecs = jnp.concatenate(
        [vec_ref[...], jnp.zeros((128 - vec_ref.shape[0], vec_ref.shape[1]), F32)], 0
    )
    pack_ref[:, wide:] = jnp.transpose(vecs).astype(BF)

    @pl.when(info[1] == 0)
    def _():
        rows = [dot_tn(d_ref[n], normed_ref[...]) for n in range(3)]
        rows.append(dot_tn(mixed_ref[...], low_ref[...]))
        pack_ref[:, :wide] = jnp.transpose(jnp.concatenate(rows, 0)).astype(BF)

    @pl.when(info[1] != 0)
    def _():
        pack_ref[:, :wide] = (part_ref[...].astype(F32) + hop_ref[...].astype(F32)).astype(BF)


def routed_attn_grads(info, normed, d_qkv, d_low, mixed, part, far, vecs):
    return pl.pallas_call(
        routed_attn_grads_kernel,
        out_shape=shape((normed.shape[1], 4 * mixed.shape[1] + 128), BF),
        in_specs=[SM] + [VM] * 7,
        out_specs=VM,
        compiler_params=params(),
        cost_estimate=cost(3),
        name="routed_attn_grads",
    )(info, normed, d_qkv, d_low, mixed, part, far, vecs)


def rows_back_kernel(keep_ref, near_ref, far_ref, rows_ref, d_mid_ref, gains_ref, d_rows_ref, vec_ref):
    d_normed = keep_ref[0].astype(F32) + near_ref[0].astype(F32) + far_ref[...].astype(F32)
    unit, scale = unit_rows(rows_ref[...].astype(F32))
    vec_ref[...] = jnp.sum(d_normed * unit, axis=0, keepdims=True)
    d_rows = d_mid_ref[...] + norm_back(unit, scale, gains_ref[0:1, :], d_normed)
    d_rows_ref[...] = d_rows.astype(BF)


def rows_back(keep, near, far, rows, d_mid, gains):
    own, d = rows.shape
    return pl.pallas_call(
        rows_back_kernel,
        out_shape=(shape((own, d), BF), shape((1, d), F32)),
        in_specs=[VM] * 6,
        out_specs=(VM, VM),
        compiler_params=params(),
        cost_estimate=cost(4),
        name="rows_back",
    )(keep, near, far, rows, d_mid, gains)


def sel_back_kernel(near_ref, far_ref, picked_ref, upd_ref, mid_ref, gains_ref, out_ref):
    d_normed = near_ref[...].astype(F32) + far_ref[...].astype(F32)
    rows = (picked_ref[...].astype(F32) + upd_ref[...].astype(F32)).astype(BF).astype(F32)
    unit, scale = unit_rows(rows)
    d_rows = mid_ref[...].astype(F32) + norm_back(unit, scale, gains_ref[0:1, :], d_normed)
    out_ref[...] = d_rows.astype(BF)


def sel_back(near, far, picked, upd, mid, gains):
    return pl.pallas_call(
        sel_back_kernel,
        out_shape=shape(near.shape, BF),
        in_specs=[VM] * 6,
        out_specs=VM,
        compiler_params=params(),
        cost_estimate=cost(2.3),
        name="sel_back",
    )(near, far, picked, upd, mid, gains)


def add(a, b):
    return (a.astype(F32) + b.astype(F32)).astype(BF)


def core_sum(keep, send):
    return add(keep, swap(send, "tensor", 1))


def whole_sum(keep, send):
    near = core_sum(keep, send)
    return add(near, swap(near, "tensor", 2))


def scatter_groups(pack):
    count, me = lax.axis_size("dp"), lax.axis_index("dp")
    if count != 4:
        return lax.psum_scatter(pack, "dp", scatter_dimension=0, tiled=True)
    for bit in (1, 2):
        rows = pack.shape[0] // 2
        side = (me // bit) % 2
        if bit == 1:
            quarters = pack.reshape(2, 2, rows // 2, pack.shape[1])
            take = lambda at: lax.dynamic_index_in_dim(quarters, at, 1, keepdims=False)
            keep, send = take(side), take(1 - side)
        else:
            keep = lax.dynamic_index_in_dim(pack, side, 0, keepdims=False)
            send = lax.dynamic_index_in_dim(pack, 1 - side, 0, keepdims=False)
        pack = add(keep, swap(send, "dp", bit))
    return pack


def body(
    tokens, qkv_weight, out_weight, up_weight, down_weight, vectors, lengths, selected, cotangent
):
    section = lax.axis_index("section")
    tensor = lax.axis_index("tensor")
    group = lax.axis_size("dp")
    heads = HEADS // lax.axis_size("tensor")
    low = tensor & 1
    is_dense = section == 1
    gains = vectors[0]
    qkv_w = jnp.swapaxes(qkv_weight[0], 1, 2)
    mix_w, up_w, down_w = out_weight[0], up_weight[0], down_weight[0]
    cols = qkv_w.shape[1]
    width = cols // heads
    d = mix_w.shape[1]

    barrier = lax.optimization_barrier
    core = lambda block: swap(block, "tensor", 1)
    cross = lambda block: swap(block, "tensor", 2)

    halves = up_w.shape[0] // 2
    parity = lax.axis_index("dp") & 1
    take = lambda w, at: lax.dynamic_slice_in_dim(w, at * halves, halves, 0)
    mine = (take(up_w, parity), take(down_w, parity))
    up_far = hop(mine[0], 1, 0)
    down_far = hop(after(mine[1], up_far), 1, 0)

    near = core_sum(*pick_rows(tokens, selected))
    far = cross(near)
    info = jnp.stack([tensor, section, low, lengths[section]]).astype(jnp.int32)
    my_tokens = lax.dynamic_index_in_dim(tokens, section, 0, keepdims=False)
    part = my_tokens.shape[0] // 2
    tok_a, tok_b = my_tokens[:part], my_tokens[part:]
    far, my_tokens, info, tok_a, tok_b = barrier((far, my_tokens, info, tok_a, tok_b))
    tok2a = cross(after(tok_a, far))
    packed = pack_weights(gains, qkv_w, mix_w)
    picked_half = add(near, far)
    picked_other = core(picked_half)

    picked, normed, q, k, v, mixed, keep, send = routed_attn(
        info, picked_half, picked_other, gains, qkv_w, mix_w, heads
    )
    send, tok2a, up_far = barrier((send, tok2a, up_far))
    near = core_sum(keep, send)
    far = cross(near)
    far, packed, down_far = barrier((far, packed, down_far))
    attn_half = add(near, far)
    tok2b = cross(after(tok_b, far))
    tok1 = core(my_tokens)
    attn_other = core(attn_half)
    packed_far = hop(after(packed, down_far), 1, 0)
    attn, normed2, act, slope, keep, send = routed_mlp(
        info, picked, attn_half, attn_other, gains, up_w, down_w
    )
    piece0a = jnp.stack(
        [jnp.where(is_dense, own, far) for own, far in zip(mine, (up_far, down_far))]
    )
    send, tok2b = barrier((send, tok2b))
    near = core_sum(keep, send)
    far = cross(near)
    far, piece0a = barrier((far, piece0a))
    both_half, update_half = make_update(picked_half, attn_half, near, far, gains)
    piece2a = cross(after(piece0a, far))
    piece1a = core(piece0a)
    tok3a, tok3b = core(tok2a), core(tok2b)
    arrived = hop(update_half[1], 0, 1)
    my_update = jnp.where(is_dense, arrived, update_half[0])
    my_update, piece1a, packed_far = barrier((my_update, piece1a, packed_far))
    d_gains, d_qkv_w, d_mix_w = prepare(info, gains, qkv_w, mix_w, packed_far)
    my_update_other = core(my_update)
    my_update_other, d_gains = barrier((my_update_other, d_gains))
    toks = (my_tokens, tok1, tok2a, tok2b, tok3a, tok3b)

    piece0b = swap(piece0a, "dp", 1)
    piece2a, piece0b = barrier((after(piece2a, my_update_other), piece0b))
    piece2b = swap(piece2a, "dp", 1)

    rows, d_normed_rows, dq_in, dk_in, dv_in = project(
        info, toks, my_update, my_update_other, selected, d_gains, d_qkv_w, heads, width,
        lax.axis_size("tensor"),
    )
    send, keep, mixed_f, lse_f = attention(info, dq_in, dk_in, dv_in, d_mix_w, heads, width, 2)
    send, piece2b = barrier((send, piece2b))
    near = core_sum(keep, send)
    far = cross(near)
    send, keep, mixed_n, lse_n = attention(info, dq_in, dk_in, dv_in, d_mix_w, heads, width, 0)
    piece3a = core(after(piece2a, send))
    piece3b = core(after(piece2b, send))
    piece1b = core(after(piece0b, send))
    send, far = barrier((send, far))
    near = core(send)
    my_cot = lax.dynamic_slice_in_dim(cotangent, section, 1, 0)
    result, result_low, d_mid, d_mid_low, mlp_keep, mlp_send, m_vec = mlp_pass(
        rows, keep, near, far, my_cot, d_gains,
        (piece0a, piece0b, piece1a, piece1b, piece2a, piece2b, piece3a, piece3b),
    )
    grad_f = cross(d_mid_low)
    mlp_other = core(mlp_send)
    mlp_f, last, first = far_grads(mlp_keep, mlp_send, mlp_other)
    grad_f, mlp_f, last = barrier((grad_f, mlp_f, last))
    grads = (d_mid_low, mlp_other, grad_f, core(grad_f))
    mlp_f2 = cross(mlp_f)
    last_h = hop(last, 0, 1)

    d_qkv, keep, send, mid_sel = attention_back(
        info, grads, dq_in, dk_in, dv_in, (mixed_n, mixed_f), (lse_n, lse_f),
        d_mix_w, d_qkv_w, selected, heads, width,
    )
    near = core_sum(keep, send)
    far = cross(near)
    mlp_part = near_grads(mlp_keep, mlp_send, after(mlp_other, near), first, mlp_f2)
    last_f = add(last[0], after(last_h[0], mlp_part))
    far, mlp_part, last_f = barrier((far, mlp_part, last_f))
    last_f2 = cross(last_f)
    mlp_hop = hop(mlp_part, 0, 1)
    my_picked = lax.dynamic_index_in_dim(picked_half, section, 0, keepdims=False)
    my_d_sel = sel_back(near, far, my_picked, my_update, mid_sel, d_gains)
    back = hop(my_d_sel, 1, 0)
    attn_part = attn_grads(
        info, after(d_qkv, my_d_sel), d_normed_rows, grads, (mixed_n, mixed_f)
    )
    back, attn_part, last_f2 = barrier((back, attn_part, last_f2))
    sel_other = core(jnp.concatenate([my_d_sel[None], back[None], both_half], 0))

    d_sel, r_d_mlp, r_d_pre, gain_two, keep2, send2 = routed_back_mlp(
        info, my_d_sel, back, sel_other, picked, attn, gains, slope, up_w, down_w
    )
    send2, mlp_hop = barrier((send2, mlp_hop))
    near = core_sum(keep2, send2)
    far = cross(near)
    r_mlp = routed_mlp_grads(
        info, normed2, r_d_pre, act, r_d_mlp, mlp_part, mlp_hop, last, last_h, last_f2
    )
    row_send, row_keep = spread_back(info, after(d_qkv, r_mlp), d_qkv_w, 4)
    far, row_send = barrier((far, row_send))
    row_core = core(row_send)
    half = add(near, far)
    other = core(half)
    row_far = cross(add(row_keep[1], row_core[1]))
    attn_hop = hop(attn_part, 0, 1)
    hidden = up_w.shape[1]
    r_d_mid, r_d_low, r_d_qkv, r_vec, keep2, send2 = routed_back_attn(
        info, half, other, d_sel, picked, attn, both_half, sel_other, gains, q, k, v,
        qkv_w, mix_w, heads,
    )
    near = core_sum(keep2, send2)
    mlp_sum = lax.psum_scatter(r_mlp, "dp", scatter_dimension=0, tiled=True)
    near, row_far, attn_hop = barrier((near, row_far, attn_hop))
    far = cross(near)
    d_rows, row_vec = rows_back(row_keep, row_core, row_far, rows, d_mid, d_gains)
    d_rows_far = hop(d_rows, 1, 0)
    far, d_rows = barrier((far, d_rows))
    sent_result = hop(after(result_low, attn_hop), 0, 1)
    half = add(near, far)
    other = core(half)
    vecs = jnp.concatenate([r_vec[0:1], gain_two, r_vec[1:2], row_vec, m_vec], 0)
    vecs = vecs + swap(vecs, "tensor", 1)
    vecs = vecs + swap(vecs, "tensor", 2)
    r_attn = routed_attn_grads(
        info, normed, r_d_qkv, r_d_low, mixed, after(attn_part, half), attn_hop, vecs
    )
    attn_sum = scatter_groups(r_attn)

    combined = finish(
        info, half, other, r_d_mid, picked, gains, selected, d_rows, d_rows_far, sent_result, result
    )
    share = d // group
    up_grad = mlp_sum[:, :hidden].astype(F32)
    down_grad = jnp.swapaxes(mlp_sum[:, hidden:], 0, 1).astype(F32)
    qkv_grad = jnp.swapaxes(attn_sum[:, : 3 * cols].reshape(share, 3, cols), 0, 1).astype(F32)
    mix_grad = jnp.swapaxes(attn_sum[:, 3 * cols : 4 * cols], 0, 1).astype(F32)

    vecs = jnp.transpose(attn_sum[:, 4 * cols : 4 * cols + 8].astype(F32))
    dense_vec = vecs[3:6] + hop(vecs[3:6], 0, 1)
    vecs = jnp.where(is_dense, dense_vec, vecs[:3])
    return (
        combined[None],
        qkv_grad[None],
        mix_grad[None],
        up_grad[None],
        down_grad[None],
        vecs[None],
    )


def solution(mesh):
    placed = (
        P("dp", "tensor", None),
        P("section", None, None, "tensor"),
        P("section", "tensor", None),
        P("section", None, "tensor"),
        P("section", "tensor", None),
        P("section", None, None),
        P("dp"),
        P("dp", None),
        P("dp", "tensor", None),
    )
    return jax.shard_map(
        body,
        mesh=mesh,
        in_specs=placed,
        out_specs=(
            P("section", "dp", "tensor", None),
            P("section", None, "dp", "tensor"),
            P("section", "tensor", "dp"),
            P("section", "dp", "tensor"),
            P("section", "tensor", "dp"),
            P("section", None, "dp"),
        ),
        check_vma=False,
    )
```

profile of v0, /device:TPU:0, one launch (start us, length us, event | category | flops | bytes accessed | tf_op | source)
XLA Modules:
  0.0 428.7 jit_solution(1934442359536640042)
XLA Ops:
  7.2 3.1 pick.1
  13.4 3.0 collective-permute-start.1
  29.1 5.1 %routed_attn.1 = (bf16[512,768]{1,0:T(8,128)(2,1)}, bf16[512,768]{1,0:T(8,128)(2,1)}, bf16[512,192]{1,0:T(8,128)(2,1)}, bf16[512,192]{1,0:T(8,128)(2,1)}, bf16[5...) custom-call(s32[4]{0:T(128)} %pad_add_fusion.info, ...), custom_call_target="tpu_custom_call" | custom-call | flops 500000000 | bytes 16500000 | tf_op jit(solution)/shard_map/routed_attn/pallas_call | solution.py:195
  34.4 3.1 collective-permute-done.4.tok2a
  42.3 2.4 pack.1
  44.7 10.5 %collective-permute-done.8 = bf16[384,768]{1,0:T(8,128)(2,1)S(1)} collective-permute-done((bf16[384,768]{1,0:T(8,128)(2,1)S(1)}, bf16[384,768]{1,0:T(8,128)(2,1)S(1)}, u32[]{:S(2)}, u32[]{:S(2)}) %collective-permute-start.8) | collective-permute-done | bytes 589856 | tf_op jit(solution)/shard_map/ppermute | solution.py:25
  57.9 5.8 %routed_mlp.1 = (bf16[512,768]{1,0:T(8,128)(2,1)}, bf16[512,768]{1,0:T(8,128)(2,1)}, bf16[512,768]{1,0:T(8,128)(2,1)}, f32[512,768]{1,0:T(8,128)}, bf16[2,128,76...) custom-call(s32[4]{0:T(128)} %pad_add_fusion.info, bf16[512,768]{1,0:T(8,128)(2,1)} %get-tuple-element.138.picked_ref, ...), custom_call_target="tpu_custom_call" | custom-call | flops 600000000 | bytes 19800000 | tf_op jit(solution)/shard_map/routed_mlp/pallas_call | solution.py:227
  63.7 3.2 collective-permute-done.10.tok2b
  73.1 9.1 %collective-permute-done.14.mlp2_ref = bf16[2,128,768]{2,1,0:T(8,128)(2,1)S(1)} collective-permute-done((bf16[2,128,768]{2,1,0:T(8,128)(2,1)S(1)}, bf16[2,128,768]{2,1,0:T(8,128)(2,1)S(1)}, u32[]{:S(2)}, u32[]{:S(2)}) %collective-permute-start.14) | collective-permute-done | bytes 393248 | tf_op jit(solution)/shard_map/ppermute | solution.py:21
  85.5 2.5 update.1
  89.0 4.4 %collective-permute-start.15 = (bf16[128,768]{1,0:T(8,128)(2,1)S(1)}, bf16[128,768]{1,0:T(8,128)(2,1)S(1)}, u32[]{:S(2)}, u32[]{:S(2)}) collective-permute-start(bf16[128,768]{1,0:T(8,128)(2,1)S(1)} %slice_bitcast_fusion.2), channel_id=1, source_target_pairs={{0,16},{1,17},{2,18},{3,19},{4,20},{5,21},{6,22},{7,23},{8,24},{9,... | collective-permute-start | bytes 589832 | tf_op jit(solution)/shard_map/ppermute | solution.py:25
  93.4 4.2 collective-permute-done.15
  100.0 3.0 prepare.1
  103.0 7.6 %collective-permute-done.19.p2a = bf16[2,384,768]{2,1,0:T(8,128)(2,1)} collective-permute-done((bf16[2,384,768]{2,1,0:T(8,128)(2,1)S(1)}, bf16[2,384,768]{2,1,0:T(8,128)(2,1)}, u32[]{:S(2)}, u32[]{:S(2)}) %collective-permute-start.19) | collective-permute-done | bytes 1179680 | tf_op jit(solution)/shard_map/ppermute | solution.py:21
  117.8 10.3 %project.1 = (bf16[512,768]{1,0:T(8,128)(2,1)}, bf16[4,512,768]{2,1,0:T(8,128)(2,1)}, bf16[4,512,256]{2,1,0:T(8,128)(2,1)}, bf16[4,512,256]{2,1,0:T(8,128)(2,1)}, bf16[4,512,256]{2,1,0:T(8,128)(2,1)}) custom-call(s32[4]{0:T(128)} %pad_add_fusion.info, bf16[512,768]{1,0:T(8,128)(2,1)} %dynamic-slice_bitcast_fusion.tok0, bf16[512,768]{1,0:T(8,128)(2,1)} %copy-done.37, ...), custom_call_target="tpu_custom_call" | custom-call | flops 900000000 | bytes 29700000 | tf_op jit(solution)/shard_map/project/pallas_call | solution.py:526
  128.2 23.7 %attention.3 = (bf16[512,768]{1,0:T(8,128)(2,1)}, bf16[512,768]{1,0:T(8,128)(2,1)}, bf16[2,512,256]{2,1,0:T(8,128)(2,1)}, f32[2,512,128]{2,1,0:T(8,128)}) custom-call(s32[4]{0:T(128)} %pad_add_fusion.info, bf16[4,512,256]{2,1,0:T(8,128)(2,1)} %get-tuple-element.163.q_ref, bf16[2048,256]{1,0:T(8,128)(2,1)} %bitcast.96, bf16[2048,256]{1,0:T(8,128)(2,1)} %bitcast.99, ...), custom_call_target="tpu_custom_call" | custom-call | flops 30000000 | bytes 990000 | tf_op jit(solution)/shard_map/attention/pallas_call | solution.py:607
  152.1 2.4 collective-permute-done.22
  155.9 9.8 %attention.2 = (bf16[512,768]{1,0:T(8,128)(2,1)}, bf16[512,768]{1,0:T(8,128)(2,1)}, bf16[2,512,256]{2,1,0:T(8,128)(2,1)}, f32[2,512,128]{2,1,0:T(8,128)}) custom-call(s32[4]{0:T(128)} %pad_add_fusion.info, bf16[4,512,256]{2,1,0:T(8,128)(2,1)} %get-tuple-element.163.q_ref, bf16[2048,256]{1,0:T(8,128)(2,1)} %bitcast.97, bf16[2048,256]{1,0:T(8,128)(2,1)} %bitcast.100, ...), custom_call_target="tpu_custom_call" | custom-call | flops 30000000 | bytes 990000 | tf_op jit(solution)/shard_map/attention/pallas_call | solution.py:607
  166.3 9.1 %collective-permute-done.23.far_ref = bf16[512,768]{1,0:T(8,128)(2,1)S(1)} collective-permute-done((bf16[512,768]{1,0:T(8,128)(2,1)S(1)}, bf16[512,768]{1,0:T(8,128)(2,1)S(1)}, u32[]{:S(2)}, u32[]{:S(2)}) %collective-permute-start.23) | collective-permute-done | bytes 786464 | tf_op jit(solution)/shard_map/ppermute | solution.py:21
  178.8 22.4 %dense_mlp.1 = (f32[512,768]{1,0:T(8,128)}, bf16[512,768]{1,0:T(8,128)(2,1)}, f32[512,768]{1,0:T(8,128)}, bf16[512,768]{1,0:T(8,128)(2,1)}, bf16[4,512,768]{2,1,...) custom-call(bf16[512,768]{1,0:T(8,128)(2,1)} %get-tuple-element.162.rows_ref, ...), custom_call_target="tpu_custom_call" | custom-call | flops 2100000000 | bytes 69300000 | tf_op jit(solution)/shard_map/dense_mlp/pallas_call | solution.py:716
  202.8 7.7 %collective-permute-done.28.act2_ref.pre2_ref.near2_ref.rows2_ref.g1 = bf16[7,512,768]{2,1,0:T(8,128)(2,1)S(1)} collective-permute-done((bf16[7,512,768]{2,1,0:T(8,128)(2,1)}, bf16[7,512,768]{2,1,0:T(8,128)(2,1)S(1)}, u32[]{:S(2)}, u32[]{:S(2)}) %collective-permute-start.28) | collective-permute-done | bytes 5505056 | tf_op jit(solution)/shard_map/ppermute | solution.py:21
  210.5 2.4 copy-done.2
  212.9 8.7 %far_grads.1 = (bf16[864,768]{1,0:T(8,128)(2,1)}, bf16[2,672,768]{2,1,0:T(8,128)(2,1)}, bf16[96,768]{1,0:T(8,128)(2,1)}) custom-call(bf16[4,512,768]{2,1,0:T(8,128)(2,1)} %get-tuple-element.185.act_ref.pre_ref.near_ref, bf16[4,512,768]{2,1,0:T(8,128)(2,1)} %get-tuple-element.185.act_ref.pre_ref.near_ref, ...), custom_call_target="tpu_custom_call" | custom-call | flops 500000000 | bytes 16500000 | tf_op jit(solution)/shard_map/far_grads/pallas_call | solution.py:780
  221.6 4.4 %collective-permute-start.34 = (bf16[2,672,768]{2,1,0:T(8,128)(2,1)}, bf16[2,672,768]{2,1,0:T(8,128)(2,1)S(1)}, u32[]{:S(2)}, u32[]{:S(2)}) collective-permute-start(bf16[2,672,768]{2,1,0:T(8,128)(2,1)} %get-tuple-element.198.last_ref), channel_id=1, source_target_pairs={{0,16},{1,17},{2,18},{3,19},{4,20},{5,21},{6,22},{7,23},{8,24},{9,... | collective-permute-start | bytes 6193160 | tf_op jit(solution)/shard_map/ppermute | solution.py:25
  229.3 29.5 %attention_back.1 = (bf16[3,2048,192]{2,1,0:T(8,128)(2,1)}, bf16[128,768]{1,0:T(8,128)(2,1)}, bf16[128,768]{1,0:T(8,128)(2,1)}, bf16[128,768]{1,0:T(8,128)(2,1)}) custom-call(s32[4]{0:T(128)} %pad_add_fusion.info, bf16[512,768]{1,0:T(8,128)(2,1)} %get-tuple-element.183.g0, bf16[7,512,768]{2,1,0:T(8,128)(2,1)} %copy-done.2, bf16[512,768]{1,0:T(8,128)(2,1)} %copy-done.16, ...), custom_call_target="tpu_custom_call" | custom-call | flops 3500000000 | bytes 115500000 | tf_op jit(solution)/shard_map/attention_back/pallas_call | solution.py:902
  262.8 5.0 %near_grads.1.part_ref = bf16[864,768]{1,0:T(8,128)(2,1)} custom-call(bf16[4,512,768]{2,1,0:T(8,128)(2,1)} %get-tuple-element.185.act_ref.pre_ref.near_ref, bf16[7,512,768]{2,1,0:T(8,128)(2,1)} %get-tuple-element.184.own_ref, bf16[7,512,768]{2,1,0:T(8,128)(2,1)} %copy-done.2, bf16[7,512,768]{2,1,0:T(8,128)(2,1)} %copy-done.2, ...), custom_call_target="tpu_custom_call" | custom-call | flops 500000000 | bytes 16500000 | tf_op jit(solution)/shard_map/near_grads/pallas_call | solution.py:802
  267.9 2.8 collective-permute-done.34.last_far
  273.4 4.4 %collective-permute-start.38 = (bf16[864,768]{1,0:T(8,128)(2,1)S(1)}, bf16[864,768]{1,0:T(8,128)(2,1)S(1)}, u32[]{:S(2)}, u32[]{:S(2)}) collective-permute-start(bf16[864,768]{1,0:T(8,128)(2,1)S(1)} %copy-done.7), channel_id=1, source_target_pairs={{0,16},{1,17},{2,18},{3,19},{4,20},{5,21},{6,22},{7,23},{8,24},{9,... | collective-permute-start | bytes 3981320 | tf_op jit(solution)/shard_map/ppermute | solution.py:25
  278.5 2.2 sel_back.1.sel_own
  282.0 9.4 %attn_grads.1.part_ref = bf16[768,768]{1,0:T(8,128)(2,1)} custom-call(s32[4]{0:T(128)} %pad_add_fusion.info, bf16[3,4,512,192]{3,2,1,0:T(8,128)(2,1)} %bitcast.89, bf16[4,512,768]{2,1,0:T(8,128)(2,1)} %get-tuple-element.204.normed_ref, bf16[512,768]{1,0:T(8,128)(2,1)} %get-tuple-element.183.g0, bf16[7,512,768]{2,1,0:T(8,128)(2,1)} %copy-done.2, ...), custom_call_target="tpu_custom_call" | custom-call | flops 800000000 | bytes 26400000 | tf_op jit(solution)/shard_map/attn_grads/pallas_call | solution.py:995
  291.5 4.6 %collective-permute-done.36.last_cross = bf16[672,768]{1,0:T(8,128)(2,1)S(1)} collective-permute-done((bf16[672,768]{1,0:T(8,128)(2,1)S(1)}, bf16[672,768]{1,0:T(8,128)(2,1)S(1)}, u32[]{:S(2)}, u32[]{:S(2)}) %collective-permute-start.36) | collective-permute-done | bytes 1032224 | tf_op jit(solution)/shard_map/ppermute | solution.py:21
  296.2 2.3 collective-permute-done.37.sel_other.both_other
  299.4 5.6 %routed_back_mlp.1 = (f32[512,768]{1,0:T(8,128)}, bf16[512,768]{1,0:T(8,128)(2,1)}, bf16[512,768]{1,0:T(8,128)(2,1)}, f32[1,768]{1,0:T(1,128)}, bf16[2,128,768]{...) custom-call(s32[4]{0:T(128)} %pad_add_fusion.info, bf16[128,768]{1,0:T(8,128)(2,1)} %sel_back.1.sel_own, ...), custom_call_target="tpu_custom_call" | custom-call | flops 600000000 | bytes 19800000 | tf_op jit(solution)/shard_map/routed_back_mlp/pallas_call | solution.py:292
  309.6 7.0 %routed_mlp_grads.1 = bf16[768,1536]{1,0:T(8,128)(2,1)} custom-call(s32[4]{0:T(128)} %pad_add_fusion.info, bf16[512,768]{1,0:T(8,128)(2,1)} %get-tuple-element.214.normed_ref, bf16[512,768]{1,0:T(8,128)(2,1)} %get-tuple-element.215.pre_ref, bf16[512,768]{1,0:T(8,128)(2,1)} %get-tuple-element.216.act_ref, bf16[512,768]{1,0:T(8,128)(2,1)} %get-tuple-element.217.grad_ref, ...), custom_call_target="tpu_custom_call" | custom-call | flops 500000000 | bytes 16500000 | tf_op jit(solution)/shard_map/routed_mlp_grads/pallas_call | solution.py:1044
  316.5 7.5 %spread_back.1 = (bf16[2,512,768]{2,1,0:T(8,128)(2,1)}, bf16[2,512,768]{2,1,0:T(8,128)(2,1)}) custom-call(s32[4]{0:T(128)} %pad_add_fusion.info, bf16[3,4,512,192]{3,2,1,0:T(8,128)(2,1)} %bitcast.90, bf16[3,256,768]{2,1,0:T(8,128)(2,1)} %get-tuple-element.161.qkv_ref), custom_call_target="tpu_custom_call" | custom-call | flops 500000000 | bytes 16500000 | tf_op jit(solution)/shard_map/spread_back/pallas_call | solution.py:945
  324.1 4.9 %collective-permute-start.45 = (bf16[768,768]{1,0:T(8,128)(2,1)S(1)}, bf16[768,768]{1,0:T(8,128)(2,1)}, u32[]{:S(2)}, u32[]{:S(2)}) collective-permute-start(bf16[768,768]{1,0:T(8,128)(2,1)S(1)} %copy-done.10), channel_id=1, source_target_pairs={{0,16},{1,17},{2,18},{3,19},{4,20},{5,21},{6,22},{7,23},{8,24},{9,... | collective-permute-start | bytes 3538952 | tf_op jit(solution)/shard_map/ppermute | solution.py:25
  332.4 8.6 %routed_back_attn.1 = (f32[512,768]{1,0:T(8,128)}, bf16[512,768]{1,0:T(8,128)(2,1)}, bf16[3,512,192]{2,1,0:T(8,128)(2,1)}, f32[2,768]{1,0:T(2,128)}, bf16[2,128,...) custom-call(s32[4]{0:T(128)} %pad_add_fusion.info, bf16[2,128,768]{2,1,0:T(8,128)(2,1)} %copy-done.25, ...), custom_call_target="tpu_custom_call" | custom-call | flops 800000000 | bytes 26400000 | tf_op jit(solution)/shard_map/routed_back_attn/pallas_call | solution.py:368
  344.0 9.6 %collective-permute-done.45.hop_ref = bf16[768,768]{1,0:T(8,128)(2,1)} collective-permute-done((bf16[768,768]{1,0:T(8,128)(2,1)S(1)}, bf16[768,768]{1,0:T(8,128)(2,1)}, u32[]{:S(2)}, u32[]{:S(2)}) %collective-permute-start.45) | collective-permute-done | bytes 1179680 | tf_op jit(solution)/shard_map/ppermute | solution.py:25
  355.3 4.8 %rows_back.1 = (bf16[512,768]{1,0:T(8,128)(2,1)}, f32[1,768]{1,0:T(1,128)}) custom-call(bf16[2,512,768]{2,1,0:T(8,128)(2,1)} %get-tuple-element.229.keep_ref, bf16[2,512,768]{2,1,0:T(8,128)(2,1)} %collective-permute-done.43.near_ref, bf16[512,768]{1,0:T(8,128)(2,1)} %copy-done.36, bf16[512,768]{1,0:T(8,128)(2,1)} %get-tuple-element.162.rows_ref, ...), custom_call_target="tpu_custom_call" | custom-call | flops 400000000 | bytes 13200000 | tf_op jit(solution)/shard_map/rows_back/pallas_call | solution.py:1098
  363.1 2.8 collective-permute-done.51
  366.6 4.7 %routed_attn_grads.1 = bf16[768,896]{1,0:T(8,128)(2,1)} custom-call(s32[4]{0:T(128)} %pad_add_fusion.info, bf16[512,768]{1,0:T(8,128)(2,1)} %get-tuple-element.243.normed_ref, bf16[3,512,192]{2,1,0:T(8,128)(2,1)} %get-tuple-element.244.d_ref, bf16[512,768]{1,0:T(8,128)(2,1)} %get-tuple-element.245.low_ref, bf16[512,192]{1,0:T(8,128)(2,1)} %get-tuple-element.246.mixed_ref, ...), custom_call_target="tpu_custom_call" | custom-call | flops 300000000 | bytes 9900000 | tf_op jit(solution)/shard_map/routed_attn_grads/pallas_call | solution.py:1077
  373.2 4.8 %collective-permute-start.49 = (bf16[512,768]{1,0:T(8,128)(2,1)}, bf16[512,768]{1,0:T(8,128)(2,1)}, u32[]{:S(2)}, u32[]{:S(2)}) collective-permute-start(bf16[512,768]{1,0:T(8,128)(2,1)} %get-tuple-element.241), channel_id=1, source_target_pairs={{0,16},{1,17},{2,18},{3,19},{4,20},{5,21},{6,22},{7,23},{8,24},{9,... | collective-permute-start | bytes 2359304 | tf_op jit(solution)/shard_map/ppermute | solution.py:25
  379.9 9.7 %collective-permute-done.52 = bf16[2,192,896]{2,1,0:T(8,128)(2,1)} collective-permute-done((bf16[2,192,896]{2,1,0:T(8,128)(2,1)S(1)}, bf16[2,192,896]{2,1,0:T(8,128)(2,1)}, u32[]{:S(2)}, u32[]{:S(2)}) %collective-permute-start.52) | collective-permute-done | bytes 688160 | tf_op jit(solution)/shard_map/ppermute | solution.py:21
  391.4 2.6 collective-permute-start.53
  394.0 4.5 %collective-permute-done.48.far_ref = bf16[512,768]{1,0:T(8,128)(2,1)} collective-permute-done((bf16[512,768]{1,0:T(8,128)(2,1)}, bf16[512,768]{1,0:T(8,128)(2,1)}, u32[]{:S(2)}, u32[]{:S(2)}) %collective-permute-start.48) | collective-permute-done | bytes 786464 | tf_op jit(solution)/shard_map/ppermute | solution.py:25
  398.5 6.1 %finish.1 = f32[2,512,768]{2,1,0:T(8,128)} custom-call(s32[4]{0:T(128)} %pad_add_fusion.info, bf16[2,128,768]{2,1,0:T(8,128)(2,1)} %copy-done.22, bf16[2,128,768]{2,1,0:T(8,128)(2,1)} %collective-permute-done.47.other_ref, f32[512,768]{1,0:T(8,128)} %get-tuple-element.237.d_mid_ref, bf16[512,768]{1,0:T(8,128)(2,1)} %get-tuple-element.138.picked_ref, ...), custom_call_target="tpu_custom_call" | custom-call | flops 600000000 | bytes 19800000 | tf_op jit(solution)/shard_map/finish/pallas_call | solution.py:409
  404.7 8.4 %collective-permute-done.53 = bf16[192,896]{0,1:T(8,128)(2,1)S(1)} collective-permute-done((bf16[192,896]{0,1:T(8,128)(2,1)S(1)}, bf16[192,896]{0,1:T(8,128)(2,1)S(1)}, u32[]{:S(2)}, u32[]{:S(2)}) %collective-permute-start.53) | collective-permute-done | bytes 344096 | tf_op jit(solution)/shard_map/ppermute | solution.py:21
  413.2 3.8 collective-permute-start.54
  (255 shorter events, 90.5 us)
Async XLA Ops:
  7.2 412.3 %reduce-scatter.2.cloned.1.call-start = ((), (), s32[]{:S(2)}) async-start(), calls=%async_computation.1 | async-start | bytes 2949120 | tf_op jit(solution)/shard_map/reduce_scatter | solution.py:1306
  13.4 12.4 %collective-permute-start.1 = (bf16[2,128,768]{2,1,0:T(8,128)(2,1)S(1)}, bf16[2,128,768]{2,1,0:T(8,128)(2,1)S(1)}, u32[]{:S(2)}, u32[]{:S(2)}) collective-permute-start(bf16[2,128,768]{2,1,0:T(8,128)(2,1)S(1)} %add_convert_fusion.10), channel_id=1, source_target_pairs={{0,2},{1,3},{2,0},{3,1},{4,6},{5,7},{6,4},{7,5},{8,10},{9,11},{10,... | collective-permute-start | bytes 1179656 | tf_op jit(solution)/shard_map/ppermute | solution.py:21
  17.2 17.2 %collective-permute-start.5 = (bf16[384,768]{1,0:T(8,128)(2,1)}, bf16[384,768]{1,0:T(8,128)(2,1)S(1)}, u32[]{:S(2)}, u32[]{:S(2)}) collective-permute-start(bf16[384,768]{1,0:T(8,128)(2,1)} %dynamic-slice_bitcast_fusion.3), channel_id=1, source_target_pairs={{16,0},{17,1},{18,2},{19,3},{20,4},{21,5},{22,6},{23,7},{24,8},{25... | collective-permute-start | bytes 1769480 | tf_op jit(solution)/shard_map/ppermute | solution.py:25
  25.9 2.5 collective-permute-start.3
  26.0 11.5 %collective-permute-start.4 = (bf16[256,768]{1,0:T(8,128)(2,1)S(1)}, bf16[256,768]{1,0:T(8,128)(2,1)S(1)}, u32[]{:S(2)}, u32[]{:S(2)}) collective-permute-start(bf16[256,768]{1,0:T(8,128)(2,1)S(1)} %get-tuple-element.136), channel_id=1, source_target_pairs={{0,2},{1,3},{2,0},{3,1},{4,6},{5,7},{6,4},{7,5},{8,10},{9,11},{10,... | collective-permute-start | bytes 1179656 | tf_op jit(solution)/shard_map/ppermute | solution.py:21
  37.6 17.6 %collective-permute-start.8 = (bf16[384,768]{1,0:T(8,128)(2,1)S(1)}, bf16[384,768]{1,0:T(8,128)(2,1)S(1)}, u32[]{:S(2)}, u32[]{:S(2)}) collective-permute-start(bf16[384,768]{1,0:T(8,128)(2,1)S(1)} %dynamic-slice_bitcast_fusion.2), channel_id=1, source_target_pairs={{16,0},{17,1},{18,2},{19,3},{20,4},{21,5},{22,6},{23,7},{24,8},{25... | collective-permute-start | bytes 1769480 | tf_op jit(solution)/shard_map/ppermute | solution.py:25
  40.5 14.7 %collective-permute-start.7 = (bf16[2,128,768]{2,1,0:T(8,128)(2,1)S(1)}, bf16[2,128,768]{2,1,0:T(8,128)(2,1)S(1)}, u32[]{:S(2)}, u32[]{:S(2)}) collective-permute-start(bf16[2,128,768]{2,1,0:T(8,128)(2,1)S(1)} %add_convert_fusion.8), channel_id=1, source_target_pairs={{0,2},{1,3},{2,0},{3,1},{4,6},{5,7},{6,4},{7,5},{8,10},{9,11},{10,... | collective-permute-start | bytes 1179656 | tf_op jit(solution)/shard_map/ppermute | solution.py:21
  55.4 11.5 %collective-permute-start.10 = (bf16[256,768]{1,0:T(8,128)(2,1)S(1)}, bf16[256,768]{1,0:T(8,128)(2,1)S(1)}, u32[]{:S(2)}, u32[]{:S(2)}) collective-permute-start(bf16[256,768]{1,0:T(8,128)(2,1)S(1)} %get-tuple-element.145), channel_id=1, source_target_pairs={{0,2},{1,3},{2,0},{3,1},{4,6},{5,7},{6,4},{7,5},{8,10},{9,11},{10,... | collective-permute-start | bytes 1179656 | tf_op jit(solution)/shard_map/ppermute | solution.py:21
  67.8 31.1 %collective-permute-start.17 = (bf16[784,768]{1,0:T(8,128)(2,1)}, bf16[784,768]{1,0:T(8,128)(2,1)S(1)}, u32[]{:S(2)}, u32[]{:S(2)}) collective-permute-start(bf16[784,768]{1,0:T(8,128)(2,1)} %pack.1), channel_id=1, source_target_pairs={{16,0},{17,1},{18,2},{19,3},{20,4},{21,5},{22,6},{23,7},{24,8},{25... | collective-permute-start | bytes 3612680 | tf_op jit(solution)/shard_map/ppermute | solution.py:25
  70.9 11.2 %collective-permute-start.14 = (bf16[2,128,768]{2,1,0:T(8,128)(2,1)S(1)}, bf16[2,128,768]{2,1,0:T(8,128)(2,1)S(1)}, u32[]{:S(2)}, u32[]{:S(2)}) collective-permute-start(bf16[2,128,768]{2,1,0:T(8,128)(2,1)S(1)} %add_convert_fusion.6.mlp_ref), channel_id=1, source_target_pairs={{0,2},{1,3},{2,0},{3,1},{4,6},{5,7},{6,4},{7,5},{8,10},{9,11},{10,... | collective-permute-start | bytes 1179656 | tf_op jit(solution)/shard_map/ppermute | solution.py:21
  82.2 16.8 %collective-permute-start.16 = (bf16[2,384,768]{2,1,0:T(8,128)(2,1)S(1)}, bf16[2,384,768]{2,1,0:T(8,128)(2,1)S(1)}, u32[]{:S(2)}, u32[]{:S(2)}) collective-permute-start(bf16[2,384,768]{2,1,0:T(8,128)(2,1)S(1)} %pad_maximum_fusion.p0a), channel_id=1, source_target_pairs={{0,1},{1,0},{2,3},{3,2},{4,5},{5,4},{6,7},{7,6},{8,9},{9,8},{10,11... | collective-permute-start | bytes 3538952 | tf_op jit(solution)/shard_map/ppermute | solution.py:21
  82.2 28.5 %collective-permute-start.19 = (bf16[2,384,768]{2,1,0:T(8,128)(2,1)S(1)}, bf16[2,384,768]{2,1,0:T(8,128)(2,1)}, u32[]{:S(2)}, u32[]{:S(2)}) collective-permute-start(bf16[2,384,768]{2,1,0:T(8,128)(2,1)S(1)} %pad_maximum_fusion.p0a), channel_id=1, source_target_pairs={{0,2},{1,3},{2,0},{3,1},{4,6},{5,7},{6,4},{7,5},{8,10},{9,11},{10,... | collective-permute-start | bytes 3538952 | tf_op jit(solution)/shard_map/ppermute | solution.py:21
  83.9 28.2 %collective-permute-start.20 = (bf16[2,384,768]{2,1,0:T(8,128)(2,1)S(1)}, bf16[2,384,768]{2,1,0:T(8,128)(2,1)}, u32[]{:S(2)}, u32[]{:S(2)}) collective-permute-start(bf16[2,384,768]{2,1,0:T(8,128)(2,1)S(1)} %pad_maximum_fusion.p0a), channel_id=1, source_target_pairs={{0,4},{4,0},{8,12},{12,8},{1,5},{5,1},{9,13},{13,9},{2,6},{6,2},{1... | collective-permute-start | bytes 3538952 | tf_op jit(solution)/shard_map/ppermute | solution.py:21
  89.0 8.7 %collective-permute-start.15 = (bf16[128,768]{1,0:T(8,128)(2,1)S(1)}, bf16[128,768]{1,0:T(8,128)(2,1)S(1)}, u32[]{:S(2)}, u32[]{:S(2)}) collective-permute-start(bf16[128,768]{1,0:T(8,128)(2,1)S(1)} %slice_bitcast_fusion.2), channel_id=1, source_target_pairs={{0,16},{1,17},{2,18},{3,19},{4,20},{5,21},{6,22},{7,23},{8,24},{9,... | collective-permute-start | bytes 589832 | tf_op jit(solution)/shard_map/ppermute | solution.py:25
  99.0 4.0 collective-permute-start.18
  112.1 39.8 %collective-permute-start.21 = (bf16[2,384,768]{2,1,0:T(8,128)(2,1)}, bf16[2,384,768]{2,1,0:T(8,128)(2,1)S(1)}, u32[]{:S(2)}, u32[]{:S(2)}) collective-permute-start(bf16[2,384,768]{2,1,0:T(8,128)(2,1)} %collective-permute-done.19.p2a), channel_id=1, source_target_pairs={{0,4},{4,0},{8,12},{12,8},{1,5},{5,1},{9,13},{13,9},{2,6},{6,2},{1... | collective-permute-start | bytes 3538952 | tf_op jit(solution)/shard_map/ppermute | solution.py:21
  113.7 2.3 collective-permute-start.2
  113.7 2.8 collective-permute-start.11
  114.2 2.9 collective-permute-start.12
  151.9 2.6 collective-permute-start.22
  155.8 19.7 %collective-permute-start.23 = (bf16[512,768]{1,0:T(8,128)(2,1)S(1)}, bf16[512,768]{1,0:T(8,128)(2,1)S(1)}, u32[]{:S(2)}, u32[]{:S(2)}) collective-permute-start(bf16[512,768]{1,0:T(8,128)(2,1)S(1)} %add_convert_fusion.1), channel_id=1, source_target_pairs={{0,2},{1,3},{2,0},{3,1},{4,6},{5,7},{6,4},{7,5},{8,10},{9,11},{10,... | collective-permute-start | bytes 2359304 | tf_op jit(solution)/shard_map/ppermute | solution.py:21
  165.6 10.9 %collective-permute-start.25 = (bf16[2,384,768]{2,1,0:T(8,128)(2,1)}, bf16[2,384,768]{2,1,0:T(8,128)(2,1)S(1)}, u32[]{:S(2)}, u32[]{:S(2)}) collective-permute-start(bf16[2,384,768]{2,1,0:T(8,128)(2,1)} %collective-permute-done.20.p0b), channel_id=1, source_target_pairs={{0,1},{1,0},{2,3},{3,2},{4,5},{5,4},{6,7},{7,6},{8,9},{9,8},{10,11... | collective-permute-start | bytes 3538952 | tf_op jit(solution)/shard_map/ppermute | solution.py:21
  165.8 10.6 %collective-permute-start.26 = (bf16[2,384,768]{2,1,0:T(8,128)(2,1)}, bf16[2,384,768]{2,1,0:T(8,128)(2,1)S(1)}, u32[]{:S(2)}, u32[]{:S(2)}) collective-permute-start(bf16[2,384,768]{2,1,0:T(8,128)(2,1)} %collective-permute-done.19.p2a), channel_id=1, source_target_pairs={{0,1},{1,0},{2,3},{3,2},{4,5},{5,4},{6,7},{7,6},{8,9},{9,8},{10,11... | collective-permute-start | bytes 3538952 | tf_op jit(solution)/shard_map/ppermute | solution.py:21
  166.2 10.3 %collective-permute-start.27 = (bf16[2,384,768]{2,1,0:T(8,128)(2,1)S(1)}, bf16[2,384,768]{2,1,0:T(8,128)(2,1)S(1)}, u32[]{:S(2)}, u32[]{:S(2)}) collective-permute-start(bf16[2,384,768]{2,1,0:T(8,128)(2,1)S(1)} %collective-permute-done.21.p2b), channel_id=1, source_target_pairs={{0,1},{1,0},{2,3},{3,2},{4,5},{5,4},{6,7},{7,6},{8,9},{9,8},{10,11... | collective-permute-start | bytes 3538952 | tf_op jit(solution)/shard_map/ppermute | solution.py:21
  175.4 2.5 collective-permute-start.24
  201.2 9.3 %collective-permute-start.28 = (bf16[7,512,768]{2,1,0:T(8,128)(2,1)}, bf16[7,512,768]{2,1,0:T(8,128)(2,1)S(1)}, u32[]{:S(2)}, u32[]{:S(2)}) collective-permute-start(bf16[7,512,768]{2,1,0:T(8,128)(2,1)} %get-tuple-element.184.own_ref), channel_id=1, source_target_pairs={{0,1},{1,0},{2,3},{3,2},{4,5},{5,4},{6,7},{7,6},{8,9},{9,8},{10,11... | collective-permute-start | bytes 16515080 | tf_op jit(solution)/shard_map/ppermute | solution.py:21
  201.4 20.2 %collective-permute-start.29 = (bf16[512,768]{1,0:T(8,128)(2,1)}, bf16[512,768]{1,0:T(8,128)(2,1)S(1)}, u32[]{:S(2)}, u32[]{:S(2)}) collective-permute-start(bf16[512,768]{1,0:T(8,128)(2,1)} %get-tuple-element.183.g0), channel_id=1, source_target_pairs={{0,2},{1,3},{2,0},{3,1},{4,6},{5,7},{6,4},{7,5},{8,10},{9,11},{10,... | collective-permute-start | bytes 2359304 | tf_op jit(solution)/shard_map/ppermute | solution.py:21
  221.6 49.1 %collective-permute-start.34 = (bf16[2,672,768]{2,1,0:T(8,128)(2,1)}, bf16[2,672,768]{2,1,0:T(8,128)(2,1)S(1)}, u32[]{:S(2)}, u32[]{:S(2)}) collective-permute-start(bf16[2,672,768]{2,1,0:T(8,128)(2,1)} %get-tuple-element.198.last_ref), channel_id=1, source_target_pairs={{0,16},{1,17},{2,18},{3,19},{4,20},{5,21},{6,22},{7,23},{8,24},{9,... | collective-permute-start | bytes 6193160 | tf_op jit(solution)/shard_map/ppermute | solution.py:25
  226.0 2.4 collective-permute-start.30
  226.1 36.7 %collective-permute-start.33 = (bf16[864,768]{1,0:T(8,128)(2,1)}, bf16[864,768]{1,0:T(8,128)(2,1)}, u32[]{:S(2)}, u32[]{:S(2)}) collective-permute-start(bf16[864,768]{1,0:T(8,128)(2,1)} %get-tuple-element.197), channel_id=1, source_target_pairs={{0,2},{1,3},{2,0},{3,1},{4,6},{5,7},{6,4},{7,5},{8,10},{9,11},{10,... | collective-permute-start | bytes 3981320 | tf_op jit(solution)/shard_map/ppermute | solution.py:21
  261.4 10.7 %collective-permute-start.32 = (bf16[128,768]{1,0:T(8,128)(2,1)S(1)}, bf16[128,768]{1,0:T(8,128)(2,1)S(1)}, u32[]{:S(2)}, u32[]{:S(2)}) collective-permute-start(bf16[128,768]{1,0:T(8,128)(2,1)S(1)} %add_convert_fusion.11.near_ref), channel_id=1, source_target_pairs={{0,2},{1,3},{2,0},{3,1},{4,6},{5,7},{6,4},{7,5},{8,10},{9,11},{10,... | collective-permute-start | bytes 589832 | tf_op jit(solution)/shard_map/ppermute | solution.py:21
  272.0 24.0 %collective-permute-start.36 = (bf16[672,768]{1,0:T(8,128)(2,1)S(1)}, bf16[672,768]{1,0:T(8,128)(2,1)S(1)}, u32[]{:S(2)}, u32[]{:S(2)}) collective-permute-start(bf16[672,768]{1,0:T(8,128)(2,1)S(1)} %fusion), channel_id=1, source_target_pairs={{0,2},{1,3},{2,0},{3,1},{4,6},{5,7},{6,4},{7,5},{8,10},{9,11},{10,... | collective-permute-start | bytes 3096584 | tf_op jit(solution)/shard_map/ppermute | solution.py:21
  273.4 31.8 %collective-permute-start.38 = (bf16[864,768]{1,0:T(8,128)(2,1)S(1)}, bf16[864,768]{1,0:T(8,128)(2,1)S(1)}, u32[]{:S(2)}, u32[]{:S(2)}) collective-permute-start(bf16[864,768]{1,0:T(8,128)(2,1)S(1)} %copy-done.7), channel_id=1, source_target_pairs={{0,16},{1,17},{2,18},{3,19},{4,20},{5,21},{6,22},{7,23},{8,24},{9,... | collective-permute-start | bytes 3981320 | tf_op jit(solution)/shard_map/ppermute | solution.py:25
  280.7 10.7 %collective-permute-start.35 = (bf16[128,768]{1,0:T(8,128)(2,1)}, bf16[128,768]{1,0:T(8,128)(2,1)S(1)}, u32[]{:S(2)}, u32[]{:S(2)}) collective-permute-start(bf16[128,768]{1,0:T(8,128)(2,1)} %sel_back.1.sel_own), channel_id=1, source_target_pairs={{16,0},{17,1},{18,2},{19,3},{20,4},{21,5},{22,6},{23,7},{24,8},{25... | collective-permute-start | bytes 589832 | tf_op jit(solution)/shard_map/ppermute | solution.py:25
  296.1 2.4 collective-permute-start.37
  308.3 15.8 %collective-permute-start.40 = (bf16[2,128,768]{2,1,0:T(8,128)(2,1)S(1)}, bf16[2,128,768]{2,1,0:T(8,128)(2,1)S(1)}, u32[]{:S(2)}, u32[]{:S(2)}) collective-permute-start(bf16[2,128,768]{2,1,0:T(8,128)(2,1)S(1)} %add_convert_fusion.5), channel_id=1, source_target_pairs={{0,2},{1,3},{2,0},{3,1},{4,6},{5,7},{6,4},{7,5},{8,10},{9,11},{10,... | collective-permute-start | bytes 1179656 | tf_op jit(solution)/shard_map/ppermute | solution.py:21
  324.0 5.3 %collective-permute-start.43 = (bf16[2,512,768]{2,1,0:T(8,128)(2,1)}, bf16[2,512,768]{2,1,0:T(8,128)(2,1)}, u32[]{:S(2)}, u32[]{:S(2)}) collective-permute-start(bf16[2,512,768]{2,1,0:T(8,128)(2,1)} %get-tuple-element.230), channel_id=1, source_target_pairs={{0,1},{1,0},{2,3},{3,2},{4,5},{5,4},{6,7},{7,6},{8,9},{9,8},{10,11... | collective-permute-start | bytes 4718600 | tf_op jit(solution)/shard_map/ppermute | solution.py:21
  324.1 29.4 %collective-permute-start.45 = (bf16[768,768]{1,0:T(8,128)(2,1)S(1)}, bf16[768,768]{1,0:T(8,128)(2,1)}, u32[]{:S(2)}, u32[]{:S(2)}) collective-permute-start(bf16[768,768]{1,0:T(8,128)(2,1)S(1)} %copy-done.10), channel_id=1, source_target_pairs={{0,16},{1,17},{2,18},{3,19},{4,20},{5,21},{6,22},{7,23},{8,24},{9,... | collective-permute-start | bytes 3538952 | tf_op jit(solution)/shard_map/ppermute | solution.py:25
  329.2 2.5 collective-permute-start.41
  330.6 22.9 %collective-permute-start.44 = (bf16[512,768]{1,0:T(8,128)(2,1)S(1)}, bf16[512,768]{1,0:T(8,128)(2,1)S(1)}, u32[]{:S(2)}, u32[]{:S(2)}) collective-permute-start(bf16[512,768]{1,0:T(8,128)(2,1)S(1)} %fusion.3), channel_id=1, source_target_pairs={{0,2},{1,3},{2,0},{3,1},{4,6},{5,7},{6,4},{7,5},{8,10},{9,11},{10,... | collective-permute-start | bytes 2359304 | tf_op jit(solution)/shard_map/ppermute | solution.py:21
  353.5 13.0 %collective-permute-start.46 = (bf16[2,128,768]{2,1,0:T(8,128)(2,1)S(1)}, bf16[2,128,768]{2,1,0:T(8,128)(2,1)S(1)}, u32[]{:S(2)}, u32[]{:S(2)}) collective-permute-start(bf16[2,128,768]{2,1,0:T(8,128)(2,1)S(1)} %add_convert_fusion.3), channel_id=1, source_target_pairs={{0,2},{1,3},{2,0},{3,1},{4,6},{5,7},{6,4},{7,5},{8,10},{9,11},{10,... | collective-permute-start | bytes 1179656 | tf_op jit(solution)/shard_map/ppermute | solution.py:21
  362.1 3.8 collective-permute-start.51
  372.7 16.9 %collective-permute-start.52 = (bf16[2,192,896]{2,1,0:T(8,128)(2,1)S(1)}, bf16[2,192,896]{2,1,0:T(8,128)(2,1)}, u32[]{:S(2)}, u32[]{:S(2)}) collective-permute-start(bf16[2,192,896]{2,1,0:T(8,128)(2,1)S(1)} %get-tuple-element.267), channel_id=1, source_target_pairs={{0,4},{4,0},{8,12},{12,8},{1,5},{5,1},{9,13},{13,9},{2,6},{6,2},{1... | collective-permute-start | bytes 2064392 | tf_op jit(solution)/shard_map/ppermute | solution.py:21
  373.2 20.8 %collective-permute-start.49 = (bf16[512,768]{1,0:T(8,128)(2,1)}, bf16[512,768]{1,0:T(8,128)(2,1)}, u32[]{:S(2)}, u32[]{:S(2)}) collective-permute-start(bf16[512,768]{1,0:T(8,128)(2,1)} %get-tuple-element.241), channel_id=1, source_target_pairs={{0,16},{1,17},{2,18},{3,19},{4,20},{5,21},{6,22},{7,23},{8,24},{9,... | collective-permute-start | bytes 2359304 | tf_op jit(solution)/shard_map/ppermute | solution.py:25
  378.0 20.5 %collective-permute-start.48 = (bf16[512,768]{1,0:T(8,128)(2,1)}, bf16[512,768]{1,0:T(8,128)(2,1)}, u32[]{:S(2)}, u32[]{:S(2)}) collective-permute-start(bf16[512,768]{1,0:T(8,128)(2,1)} %get-tuple-element.238.d_rows_ref), channel_id=1, source_target_pairs={{16,0},{17,1},{18,2},{19,3},{20,4},{21,5},{22,6},{23,7},{24,8},{25... | collective-permute-start | bytes 2359304 | tf_op jit(solution)/shard_map/ppermute | solution.py:25
  379.3 14.7 %collective-permute-start.47 = (bf16[2,128,768]{2,1,0:T(8,128)(2,1)S(1)}, bf16[2,128,768]{2,1,0:T(8,128)(2,1)}, u32[]{:S(2)}, u32[]{:S(2)}) collective-permute-start(bf16[2,128,768]{2,1,0:T(8,128)(2,1)S(1)} %add_convert_fusion.2.own_ref), channel_id=1, source_target_pairs={{0,1},{1,0},{2,3},{3,2},{4,5},{5,4},{6,7},{7,6},{8,9},{9,8},{10,11... | collective-permute-start | bytes 1179656 | tf_op jit(solution)/shard_map/ppermute | solution.py:21
  391.4 21.7 %collective-permute-start.53 = (bf16[192,896]{0,1:T(8,128)(2,1)S(1)}, bf16[192,896]{0,1:T(8,128)(2,1)S(1)}, u32[]{:S(2)}, u32[]{:S(2)}) collective-permute-start(bf16[192,896]{0,1:T(8,128)(2,1)S(1)} %dynamic-slice_bitcast_fusion.4), channel_id=1, source_target_pairs={{0,8},{4,12},{8,0},{12,4},{1,9},{5,13},{9,1},{13,5},{2,10},{6,14},... | collective-permute-start | bytes 1032200 | tf_op jit(solution)/shard_map/ppermute | solution.py:21
  413.2 5.7 %collective-permute-start.54 = (f32[3,192]{1,0:T(4,128)S(1)}, f32[3,192]{1,0:T(4,128)S(1)}, u32[]{:S(2)}, u32[]{:S(2)}) collective-permute-start(f32[3,192]{1,0:T(4,128)S(1)} %slice.84), channel_id=1, source_target_pairs={{0,16},{1,17},{2,18},{3,19},{4,20},{5,21},{6,22},{7,23},{8,24},{9,... | collective-permute-start | bytes 6920 | tf_op jit(solution)/shard_map/ppermute | solution.py:25
  (68 other events, 609.9 us)
Sparse Core Ops, SparseCore 0:
  329.2 46.7 reduce-scatter.1
where the time goes:
time: 433 us; the launch traced here: 429 us
  Pallas kernels  187 us (43%)
  waiting for transfers between devices  119 us (27%)
  starting transfers between devices  64.7 us (15%)
  local copies, waits for them, and re-layouts  26.7 us (6%)
  other arithmetic  16.3 us (4%)
  between operations  15 us (3%)
    ppermute x44, waiting for transfers between devices, swap(): return lax.ppermute(block, axis, [(i, i ^ bit) for i in range(count)])  86.4 us
    pallas_call x2, Pallas kernels, attention(): pl.pallas_call(functools.partial(attention_kernel, heads, width, base, pe...  33.5 us
    ppermute x11, starting transfers between devices, hop(): return lax.ppermute(block, 'section', [(source, target)])  33.2 us
    ppermute x11, waiting for transfers between devices, hop(): return lax.ppermute(block, 'section', [(source, target)])  32.4 us
    ppermute x44, starting transfers between devices, swap(): return lax.ppermute(block, axis, [(i, i ^ bit) for i in range(count)])  31.5 us
    pallas_call x1, Pallas kernels, attention_back(): pl.pallas_call(functools.partial(attention_back_kernel, heads, width, blo...  29.5 us
    pallas_call x1, Pallas kernels, mlp_pass(): pl.pallas_call(functools.partial(mlp_kernel, half), out_shape=(wide, low,...  22.4 us
    unnamed x124, local copies, waits for them, and re-layouts  14.8 us
  transfers between devices with their start and end apart: 56, of which 34 were waited for; matrix products, arithmetic and copies ran while one was open for 6% of the time, Pallas kernels for 38%

commit v1 on v0

--- a/solution.py
+++ b/solution.py
@@ -1053,36 +1053,31 @@
 
 
 def routed_attn_grads_kernel(
-    info, normed_ref, d_ref, low_ref, mixed_ref, part_ref, hop_ref, vec_ref, pack_ref
+    info, normed_ref, d_ref, low_ref, mixed_ref, part_ref, hop_ref, pack_ref
 ):
     cols = mixed_ref.shape[1]
-    wide = 4 * cols
-    vecs = jnp.concatenate(
-        [vec_ref[...], jnp.zeros((128 - vec_ref.shape[0], vec_ref.shape[1]), F32)], 0
-    )
-    pack_ref[:, wide:] = jnp.transpose(vecs).astype(BF)
 
     @pl.when(info[1] == 0)
     def _():
         rows = [dot_tn(d_ref[n], normed_ref[...]) for n in range(3)]
         rows.append(dot_tn(mixed_ref[...], low_ref[...]))
-        pack_ref[:, :wide] = jnp.transpose(jnp.concatenate(rows, 0)).astype(BF)
+        pack_ref[...] = jnp.transpose(jnp.concatenate(rows, 0)).astype(BF)
 
     @pl.when(info[1] != 0)
     def _():
-        pack_ref[:, :wide] = (part_ref[...].astype(F32) + hop_ref[...].astype(F32)).astype(BF)
-
-
-def routed_attn_grads(info, normed, d_qkv, d_low, mixed, part, far, vecs):
+        pack_ref[...] = (part_ref[...].astype(F32) + hop_ref[...].astype(F32)).astype(BF)
+
+
+def routed_attn_grads(info, normed, d_qkv, d_low, mixed, part, far):
     return pl.pallas_call(
         routed_attn_grads_kernel,
-        out_shape=shape((normed.shape[1], 4 * mixed.shape[1] + 128), BF),
-        in_specs=[SM] + [VM] * 7,
+        out_shape=shape((normed.shape[1], 4 * mixed.shape[1]), BF),
+        in_specs=[SM] + [VM] * 6,
         out_specs=VM,
         compiler_params=params(),
         cost_estimate=cost(3),
         name="routed_attn_grads",
-    )(info, normed, d_qkv, d_low, mixed, part, far, vecs)
+    )(info, normed, d_qkv, d_low, mixed, part, far)
 
 
 def rows_back_kernel(keep_ref, near_ref, far_ref, rows_ref, d_mid_ref, gains_ref, d_rows_ref, vec_ref):
@@ -1303,21 +1298,19 @@
         qkv_w, mix_w, heads,
     )
     near = core_sum(keep2, send2)
-    mlp_sum = lax.psum_scatter(r_mlp, "dp", scatter_dimension=0, tiled=True)
     near, row_far, attn_hop = barrier((near, row_far, attn_hop))
     far = cross(near)
+    r_attn = routed_attn_grads(
+        info, normed, r_d_qkv, r_d_low, mixed, after(attn_part, near), attn_hop
+    )
+    mlp_sum = lax.psum_scatter(r_mlp, "dp", scatter_dimension=0, tiled=True)
+    d_mid = after(d_mid, r_attn)
     d_rows, row_vec = rows_back(row_keep, row_core, row_far, rows, d_mid, d_gains)
     d_rows_far = hop(d_rows, 1, 0)
     far, d_rows = barrier((far, d_rows))
     sent_result = hop(after(result_low, attn_hop), 0, 1)
     half = add(near, far)
     other = core(half)
-    vecs = jnp.concatenate([r_vec[0:1], gain_two, r_vec[1:2], row_vec, m_vec], 0)
-    vecs = vecs + swap(vecs, "tensor", 1)
-    vecs = vecs + swap(vecs, "tensor", 2)
-    r_attn = routed_attn_grads(
-        info, normed, r_d_qkv, r_d_low, mixed, after(attn_part, half), attn_hop, vecs
-    )
     attn_sum = scatter_groups(r_attn)
 
     combined = finish(
@@ -1329,7 +1322,13 @@
     qkv_grad = jnp.swapaxes(attn_sum[:, : 3 * cols].reshape(share, 3, cols), 0, 1).astype(F32)
     mix_grad = jnp.swapaxes(attn_sum[:, 3 * cols : 4 * cols], 0, 1).astype(F32)
 
-    vecs = jnp.transpose(attn_sum[:, 4 * cols : 4 * cols + 8].astype(F32))
+    vecs = jnp.concatenate([r_vec[0:1], gain_two, r_vec[1:2], row_vec, m_vec], 0)
+    for axis in ("tensor", "dp"):
+        bit = 1
+        while bit < lax.axis_size(axis):
+            vecs = vecs + swap(vecs, axis, bit)
+            bit *= 2
+    vecs = lax.dynamic_slice_in_dim(vecs, lax.axis_index("dp") * share, share, 1)
     dense_vec = vecs[3:6] + hop(vecs[3:6], 0, 1)
     vecs = jnp.where(is_dense, dense_vec, vecs[:3])
     return (

time: 433 us -> 426 us (0.984)
  waiting for transfers between devices: 119 us -> 106 us
    ppermute x44 -> x46, waiting for transfers between devices: 86.4 us -> 76.4 us  [swap(): return lax.ppermute(block, axis, [(i, i ^ bit) for i in range(count)])]
    ppermute x44 -> x46, starting transfers between devices: 31.5 us -> 33.4 us  [swap(): return lax.ppermute(block, axis, [(i, i ^ bit) for i in range(count)])]
    unnamed x124 -> x128, local copies, waits for them, and re-layouts: 14.8 us -> 16.7 us
  transfers between devices with their start and end apart: 56 -> 58, of which waited for: 34 -> 34; matrix products, arithmetic and copies ran while one was open for 6% -> 7% of each run, Pallas kernels for 38% -> 38%
where the time goes in v1:
time: 426 us; the launch traced here: 421 us
  Pallas kernels  186 us (44%)
  waiting for transfers between devices  106 us (25%)
  starting transfers between devices  66.7 us (16%)
  local copies, waits for them, and re-layouts  28.4 us (7%)
  other arithmetic  19.1 us (4%)
  between operations  15 us (4%)
    ppermute x46, waiting for transfers between devices, swap(): return lax.ppermute(block, axis, [(i, i ^ bit) for i in range(count)])  76.4 us
    pallas_call x2, Pallas kernels, attention(): pl.pallas_call(functools.partial(attention_kernel, heads, width, base, pe...  33.4 us
    ppermute x46, starting transfers between devices, swap(): return lax.ppermute(block, axis, [(i, i ^ bit) for i in range(count)])  33.4 us
    ppermute x11, starting transfers between devices, hop(): return lax.ppermute(block, 'section', [(source, target)])  33.3 us
    pallas_call x1, Pallas kernels, attention_back(): pl.pallas_call(functools.partial(attention_back_kernel, heads, width, blo...  29.4 us
    ppermute x11, waiting for transfers between devices, hop(): return lax.ppermute(block, 'section', [(source, target)])  29.1 us
    pallas_call x1, Pallas kernels, mlp_pass(): pl.pallas_call(functools.partial(mlp_kernel, half), out_shape=(wide, low,...  22.4 us
    unnamed x128, local copies, waits for them, and re-layouts  16.7 us
  transfers between devices with their start and end apart: 58, of which 34 were waited for; matrix products, arithmetic and copies ran while one was open for 7% of the time, Pallas kernels for 38%

profile of v1, /device:TPU:0, one launch (start us, length us, event | category | flops | bytes accessed | tf_op | source)
XLA Modules:
  0.0 421.1 jit_solution(6585133131164951933)
XLA Ops:
  7.2 3.1 pick.1
  13.4 3.0 collective-permute-start.1
  29.1 5.1 %routed_attn.1 = (bf16[512,768]{1,0:T(8,128)(2,1)}, bf16[512,768]{1,0:T(8,128)(2,1)}, bf16[512,192]{1,0:T(8,128)(2,1)}, bf16[512,192]{1,0:T(8,128)(2,1)}, bf16[5...) custom-call(s32[4]{0:T(128)} %pad_add_fusion.info, ...), custom_call_target="tpu_custom_call" | custom-call | flops 500000000 | bytes 16500000 | tf_op jit(solution)/shard_map/routed_attn/pallas_call | solution.py:195
  34.4 3.1 collective-permute-done.4.tok2a
  42.3 2.4 pack.1
  44.7 10.5 %collective-permute-done.8 = bf16[384,768]{1,0:T(8,128)(2,1)S(1)} collective-permute-done((bf16[384,768]{1,0:T(8,128)(2,1)S(1)}, bf16[384,768]{1,0:T(8,128)(2,1)S(1)}, u32[]{:S(2)}, u32[]{:S(2)}) %collective-permute-start.8) | collective-permute-done | bytes 589856 | tf_op jit(solution)/shard_map/ppermute | solution.py:25
  58.0 5.8 %routed_mlp.1 = (bf16[512,768]{1,0:T(8,128)(2,1)}, bf16[512,768]{1,0:T(8,128)(2,1)}, bf16[512,768]{1,0:T(8,128)(2,1)}, f32[512,768]{1,0:T(8,128)}, bf16[2,128,76...) custom-call(s32[4]{0:T(128)} %pad_add_fusion.info, bf16[512,768]{1,0:T(8,128)(2,1)} %get-tuple-element.139.picked_ref, ...), custom_call_target="tpu_custom_call" | custom-call | flops 600000000 | bytes 19800000 | tf_op jit(solution)/shard_map/routed_mlp/pallas_call | solution.py:227
  63.8 3.1 collective-permute-done.10.tok2b
  73.1 9.1 %collective-permute-done.14.mlp2_ref = bf16[2,128,768]{2,1,0:T(8,128)(2,1)S(1)} collective-permute-done((bf16[2,128,768]{2,1,0:T(8,128)(2,1)S(1)}, bf16[2,128,768]{2,1,0:T(8,128)(2,1)S(1)}, u32[]{:S(2)}, u32[]{:S(2)}) %collective-permute-start.14) | collective-permute-done | bytes 393248 | tf_op jit(solution)/shard_map/ppermute | solution.py:21
  85.5 2.5 update.1
  89.0 4.4 %collective-permute-start.15 = (bf16[128,768]{1,0:T(8,128)(2,1)S(1)}, bf16[128,768]{1,0:T(8,128)(2,1)S(1)}, u32[]{:S(2)}, u32[]{:S(2)}) collective-permute-start(bf16[128,768]{1,0:T(8,128)(2,1)S(1)} %slice_bitcast_fusion.2), channel_id=1, source_target_pairs={{0,16},{1,17},{2,18},{3,19},{4,20},{5,21},{6,22},{7,23},{8,24},{9,... | collective-permute-start | bytes 589832 | tf_op jit(solution)/shard_map/ppermute | solution.py:25
  93.4 4.2 %collective-permute-done.15 = bf16[128,768]{1,0:T(8,128)(2,1)S(1)} collective-permute-done((bf16[128,768]{1,0:T(8,128)(2,1)S(1)}, bf16[128,768]{1,0:T(8,128)(2,1)S(1)}, u32[]{:S(2)}, u32[]{:S(2)}) %collective-permute-start.15) | collective-permute-done | bytes 196640 | tf_op jit(solution)/shard_map/ppermute | solution.py:25
  100.0 3.0 prepare.1
  103.0 7.7 %collective-permute-done.19.p2a = bf16[2,384,768]{2,1,0:T(8,128)(2,1)} collective-permute-done((bf16[2,384,768]{2,1,0:T(8,128)(2,1)S(1)}, bf16[2,384,768]{2,1,0:T(8,128)(2,1)}, u32[]{:S(2)}, u32[]{:S(2)}) %collective-permute-start.19) | collective-permute-done | bytes 1179680 | tf_op jit(solution)/shard_map/ppermute | solution.py:21
  117.9 10.3 %project.1 = (bf16[512,768]{1,0:T(8,128)(2,1)}, bf16[4,512,768]{2,1,0:T(8,128)(2,1)}, bf16[4,512,256]{2,1,0:T(8,128)(2,1)}, bf16[4,512,256]{2,1,0:T(8,128)(2,1)}, bf16[4,512,256]{2,1,0:T(8,128)(2,1)}) custom-call(s32[4]{0:T(128)} %pad_add_fusion.info, bf16[512,768]{1,0:T(8,128)(2,1)} %dynamic-slice_bitcast_fusion.tok0, bf16[512,768]{1,0:T(8,128)(2,1)} %copy-done.38, ...), custom_call_target="tpu_custom_call" | custom-call | flops 900000000 | bytes 29700000 | tf_op jit(solution)/shard_map/project/pallas_call | solution.py:526
  128.2 23.7 %attention.3 = (bf16[512,768]{1,0:T(8,128)(2,1)}, bf16[512,768]{1,0:T(8,128)(2,1)}, bf16[2,512,256]{2,1,0:T(8,128)(2,1)}, f32[2,512,128]{2,1,0:T(8,128)}) custom-call(s32[4]{0:T(128)} %pad_add_fusion.info, bf16[4,512,256]{2,1,0:T(8,128)(2,1)} %get-tuple-element.164.q_ref, bf16[2048,256]{1,0:T(8,128)(2,1)} %bitcast.94, bf16[2048,256]{1,0:T(8,128)(2,1)} %bitcast.97, ...), custom_call_target="tpu_custom_call" | custom-call | flops 30000000 | bytes 990000 | tf_op jit(solution)/shard_map/attention/pallas_call | solution.py:607
  152.1 2.3 collective-permute-done.22
  155.9 9.7 %attention.2 = (bf16[512,768]{1,0:T(8,128)(2,1)}, bf16[512,768]{1,0:T(8,128)(2,1)}, bf16[2,512,256]{2,1,0:T(8,128)(2,1)}, f32[2,512,128]{2,1,0:T(8,128)}) custom-call(s32[4]{0:T(128)} %pad_add_fusion.info, bf16[4,512,256]{2,1,0:T(8,128)(2,1)} %get-tuple-element.164.q_ref, bf16[2048,256]{1,0:T(8,128)(2,1)} %bitcast.95, bf16[2048,256]{1,0:T(8,128)(2,1)} %bitcast.98, ...), custom_call_target="tpu_custom_call" | custom-call | flops 30000000 | bytes 990000 | tf_op jit(solution)/shard_map/attention/pallas_call | solution.py:607
  166.4 9.1 %collective-permute-done.23.far_ref = bf16[512,768]{1,0:T(8,128)(2,1)S(1)} collective-permute-done((bf16[512,768]{1,0:T(8,128)(2,1)S(1)}, bf16[512,768]{1,0:T(8,128)(2,1)S(1)}, u32[]{:S(2)}, u32[]{:S(2)}) %collective-permute-start.23) | collective-permute-done | bytes 786464 | tf_op jit(solution)/shard_map/ppermute | solution.py:21
  178.9 22.4 %dense_mlp.1 = (f32[512,768]{1,0:T(8,128)}, bf16[512,768]{1,0:T(8,128)(2,1)}, f32[512,768]{1,0:T(8,128)}, bf16[512,768]{1,0:T(8,128)(2,1)}, bf16[4,512,768]{2,1,...) custom-call(bf16[512,768]{1,0:T(8,128)(2,1)} %get-tuple-element.163.rows_ref, ...), custom_call_target="tpu_custom_call" | custom-call | flops 2100000000 | bytes 69300000 | tf_op jit(solution)/shard_map/dense_mlp/pallas_call | solution.py:716
  202.8 7.7 %collective-permute-done.28.act2_ref.pre2_ref.near2_ref.rows2_ref.g1 = bf16[7,512,768]{2,1,0:T(8,128)(2,1)S(1)} collective-permute-done((bf16[7,512,768]{2,1,0:T(8,128)(2,1)}, bf16[7,512,768]{2,1,0:T(8,128)(2,1)S(1)}, u32[]{:S(2)}, u32[]{:S(2)}) %collective-permute-start.28) | collective-permute-done | bytes 5505056 | tf_op jit(solution)/shard_map/ppermute | solution.py:21
  210.6 2.4 copy-done.2
  213.0 8.7 %far_grads.1 = (bf16[864,768]{1,0:T(8,128)(2,1)}, bf16[2,672,768]{2,1,0:T(8,128)(2,1)}, bf16[96,768]{1,0:T(8,128)(2,1)}) custom-call(bf16[4,512,768]{2,1,0:T(8,128)(2,1)} %get-tuple-element.186.act_ref.pre_ref.near_ref, bf16[4,512,768]{2,1,0:T(8,128)(2,1)} %get-tuple-element.186.act_ref.pre_ref.near_ref, ...), custom_call_target="tpu_custom_call" | custom-call | flops 500000000 | bytes 16500000 | tf_op jit(solution)/shard_map/far_grads/pallas_call | solution.py:780
  221.7 4.4 %collective-permute-start.34 = (bf16[2,672,768]{2,1,0:T(8,128)(2,1)}, bf16[2,672,768]{2,1,0:T(8,128)(2,1)S(1)}, u32[]{:S(2)}, u32[]{:S(2)}) collective-permute-start(bf16[2,672,768]{2,1,0:T(8,128)(2,1)} %get-tuple-element.199.last_ref), channel_id=1, source_target_pairs={{0,16},{1,17},{2,18},{3,19},{4,20},{5,21},{6,22},{7,23},{8,24},{9,... | collective-permute-start | bytes 6193160 | tf_op jit(solution)/shard_map/ppermute | solution.py:25
  229.3 29.4 %attention_back.1 = (bf16[3,2048,192]{2,1,0:T(8,128)(2,1)}, bf16[128,768]{1,0:T(8,128)(2,1)}, bf16[128,768]{1,0:T(8,128)(2,1)}, bf16[128,768]{1,0:T(8,128)(2,1)}) custom-call(s32[4]{0:T(128)} %pad_add_fusion.info, bf16[512,768]{1,0:T(8,128)(2,1)} %get-tuple-element.184.g0, bf16[7,512,768]{2,1,0:T(8,128)(2,1)} %copy-done.2, bf16[512,768]{1,0:T(8,128)(2,1)} %copy-done.16, ...), custom_call_target="tpu_custom_call" | custom-call | flops 3500000000 | bytes 115500000 | tf_op jit(solution)/shard_map/attention_back/pallas_call | solution.py:902
  262.9 5.0 %near_grads.1.part_ref = bf16[864,768]{1,0:T(8,128)(2,1)} custom-call(bf16[4,512,768]{2,1,0:T(8,128)(2,1)} %get-tuple-element.186.act_ref.pre_ref.near_ref, bf16[7,512,768]{2,1,0:T(8,128)(2,1)} %get-tuple-element.185.own_ref, bf16[7,512,768]{2,1,0:T(8,128)(2,1)} %copy-done.2, bf16[7,512,768]{2,1,0:T(8,128)(2,1)} %copy-done.2, ...), custom_call_target="tpu_custom_call" | custom-call | flops 500000000 | bytes 16500000 | tf_op jit(solution)/shard_map/near_grads/pallas_call | solution.py:802
  267.9 2.8 collective-permute-done.34.last_far
  273.5 4.4 %collective-permute-start.38 = (bf16[864,768]{1,0:T(8,128)(2,1)S(1)}, bf16[864,768]{1,0:T(8,128)(2,1)S(1)}, u32[]{:S(2)}, u32[]{:S(2)}) collective-permute-start(bf16[864,768]{1,0:T(8,128)(2,1)S(1)} %copy-done.7), channel_id=1, source_target_pairs={{0,16},{1,17},{2,18},{3,19},{4,20},{5,21},{6,22},{7,23},{8,24},{9,... | collective-permute-start | bytes 3981320 | tf_op jit(solution)/shard_map/ppermute | solution.py:25
  278.6 2.2 sel_back.1.sel_own
  282.1 9.4 %attn_grads.1.part_ref = bf16[768,768]{1,0:T(8,128)(2,1)} custom-call(s32[4]{0:T(128)} %pad_add_fusion.info, bf16[3,4,512,192]{3,2,1,0:T(8,128)(2,1)} %bitcast.87, bf16[4,512,768]{2,1,0:T(8,128)(2,1)} %get-tuple-element.205.normed_ref, bf16[512,768]{1,0:T(8,128)(2,1)} %get-tuple-element.184.g0, bf16[7,512,768]{2,1,0:T(8,128)(2,1)} %copy-done.2, ...), custom_call_target="tpu_custom_call" | custom-call | flops 800000000 | bytes 26400000 | tf_op jit(solution)/shard_map/attn_grads/pallas_call | solution.py:995
  291.5 4.6 %collective-permute-done.36.last_cross = bf16[672,768]{1,0:T(8,128)(2,1)S(1)} collective-permute-done((bf16[672,768]{1,0:T(8,128)(2,1)S(1)}, bf16[672,768]{1,0:T(8,128)(2,1)S(1)}, u32[]{:S(2)}, u32[]{:S(2)}) %collective-permute-start.36) | collective-permute-done | bytes 1032224 | tf_op jit(solution)/shard_map/ppermute | solution.py:21
  296.3 2.3 collective-permute-done.37.sel_other.both_other
  299.5 5.6 %routed_back_mlp.1 = (f32[512,768]{1,0:T(8,128)}, bf16[512,768]{1,0:T(8,128)(2,1)}, bf16[512,768]{1,0:T(8,128)(2,1)}, f32[1,768]{1,0:T(1,128)}, bf16[2,128,768]{...) custom-call(s32[4]{0:T(128)} %pad_add_fusion.info, bf16[128,768]{1,0:T(8,128)(2,1)} %sel_back.1.sel_own, ...), custom_call_target="tpu_custom_call" | custom-call | flops 600000000 | bytes 19800000 | tf_op jit(solution)/shard_map/routed_back_mlp/pallas_call | solution.py:292
  309.6 7.0 %routed_mlp_grads.1 = bf16[768,1536]{1,0:T(8,128)(2,1)} custom-call(s32[4]{0:T(128)} %pad_add_fusion.info, bf16[512,768]{1,0:T(8,128)(2,1)} %get-tuple-element.215.normed_ref, bf16[512,768]{1,0:T(8,128)(2,1)} %get-tuple-element.216.pre_ref, bf16[512,768]{1,0:T(8,128)(2,1)} %get-tuple-element.217.act_ref, bf16[512,768]{1,0:T(8,128)(2,1)} %get-tuple-element.218.grad_ref, ...), custom_call_target="tpu_custom_call" | custom-call | flops 500000000 | bytes 16500000 | tf_op jit(solution)/shard_map/routed_mlp_grads/pallas_call | solution.py:1044
  316.6 7.4 %spread_back.1 = (bf16[2,512,768]{2,1,0:T(8,128)(2,1)}, bf16[2,512,768]{2,1,0:T(8,128)(2,1)}) custom-call(s32[4]{0:T(128)} %pad_add_fusion.info, bf16[3,4,512,192]{3,2,1,0:T(8,128)(2,1)} %bitcast.88, bf16[3,256,768]{2,1,0:T(8,128)(2,1)} %get-tuple-element.162.qkv_ref), custom_call_target="tpu_custom_call" | custom-call | flops 500000000 | bytes 16500000 | tf_op jit(solution)/shard_map/spread_back/pallas_call | solution.py:945
  325.3 4.7 %collective-permute-start.45 = (bf16[768,768]{1,0:T(8,128)(2,1)S(1)}, bf16[768,768]{1,0:T(8,128)(2,1)}, u32[]{:S(2)}, u32[]{:S(2)}) collective-permute-start(bf16[768,768]{1,0:T(8,128)(2,1)S(1)} %copy-done.10), channel_id=1, source_target_pairs={{0,16},{1,17},{2,18},{3,19},{4,20},{5,21},{6,22},{7,23},{8,24},{9,... | collective-permute-start | bytes 3538952 | tf_op jit(solution)/shard_map/ppermute | solution.py:25
  330.2 2.3 fusion.2
  334.4 8.1 %routed_back_attn.1 = (f32[512,768]{1,0:T(8,128)}, bf16[512,768]{1,0:T(8,128)(2,1)}, bf16[3,512,192]{2,1,0:T(8,128)(2,1)}, f32[2,768]{1,0:T(2,128)}, bf16[2,128,...) custom-call(s32[4]{0:T(128)} %pad_add_fusion.info, bf16[2,128,768]{2,1,0:T(8,128)(2,1)} %copy-done.25, ...), custom_call_target="tpu_custom_call" | custom-call | flops 800000000 | bytes 26400000 | tf_op jit(solution)/shard_map/routed_back_attn/pallas_call | solution.py:368
  345.5 8.5 %collective-permute-done.45.hop_ref = bf16[768,768]{1,0:T(8,128)(2,1)} collective-permute-done((bf16[768,768]{1,0:T(8,128)(2,1)S(1)}, bf16[768,768]{1,0:T(8,128)(2,1)}, u32[]{:S(2)}, u32[]{:S(2)}) %collective-permute-start.45) | collective-permute-done | bytes 1179680 | tf_op jit(solution)/shard_map/ppermute | solution.py:25
  355.0 4.4 %routed_attn_grads.1 = bf16[768,768]{1,0:T(8,128)(2,1)} custom-call(s32[4]{0:T(128)} %pad_add_fusion.info, bf16[512,768]{1,0:T(8,128)(2,1)} %get-tuple-element.236.normed_ref, bf16[3,512,192]{2,1,0:T(8,128)(2,1)} %get-tuple-element.237.d_ref, bf16[512,768]{1,0:T(8,128)(2,1)} %get-tuple-element.238.low_ref, bf16[512,192]{1,0:T(8,128)(2,1)} %get-tuple-element.239.mixed_ref, ...), custom_call_target="tpu_custom_call" | custom-call | flops 300000000 | bytes 9900000 | tf_op jit(solution)/shard_map/routed_attn_grads/pallas_call | solution.py:1072
  362.0 4.8 %rows_back.1 = (bf16[512,768]{1,0:T(8,128)(2,1)}, f32[1,768]{1,0:T(1,128)}) custom-call(bf16[2,512,768]{2,1,0:T(8,128)(2,1)} %get-tuple-element.230.keep_ref, bf16[2,512,768]{2,1,0:T(8,128)(2,1)} %collective-permute-done.43.near_ref, bf16[512,768]{1,0:T(8,128)(2,1)} %copy-done.37, bf16[512,768]{1,0:T(8,128)(2,1)} %get-tuple-element.163.rows_ref, ...), custom_call_target="tpu_custom_call" | custom-call | flops 400000000 | bytes 13200000 | tf_op jit(solution)/shard_map/rows_back/pallas_call | solution.py:1093
  369.9 2.7 collective-permute-done.53
  375.4 5.5 %collective-permute-start.49 = (bf16[512,768]{1,0:T(8,128)(2,1)}, bf16[512,768]{1,0:T(8,128)(2,1)}, u32[]{:S(2)}, u32[]{:S(2)}) collective-permute-start(bf16[512,768]{1,0:T(8,128)(2,1)} %get-tuple-element.248), channel_id=1, source_target_pairs={{0,16},{1,17},{2,18},{3,19},{4,20},{5,21},{6,22},{7,23},{8,24},{9,... | collective-permute-start | bytes 2359304 | tf_op jit(solution)/shard_map/ppermute | solution.py:25
  383.9 2.8 collective-permute-start.55
  390.5 3.4 collective-permute-start.56
  393.9 2.3 collective-permute-done.56
  397.7 6.1 %finish.1 = f32[2,512,768]{2,1,0:T(8,128)} custom-call(s32[4]{0:T(128)} %pad_add_fusion.info, bf16[2,128,768]{2,1,0:T(8,128)(2,1)} %copy-done.22, bf16[2,128,768]{2,1,0:T(8,128)(2,1)} %collective-permute-done.47.other_ref, f32[512,768]{1,0:T(8,128)} %get-tuple-element.245.d_mid_ref, bf16[512,768]{1,0:T(8,128)(2,1)} %get-tuple-element.139.picked_ref, ...), custom_call_target="tpu_custom_call" | custom-call | flops 600000000 | bytes 19800000 | tf_op jit(solution)/shard_map/finish/pallas_call | solution.py:409
  403.8 6.1 %collective-permute-done.51 = bf16[192,768]{0,1:T(8,128)(2,1)S(1)} collective-permute-done((bf16[192,768]{0,1:T(8,128)(2,1)S(1)}, bf16[192,768]{0,1:T(8,128)(2,1)S(1)}, u32[]{:S(2)}, u32[]{:S(2)}) %collective-permute-start.51) | collective-permute-done | bytes 294944 | tf_op jit(solution)/shard_map/ppermute | solution.py:21
  (264 shorter events, 96.4 us)
Async XLA Ops:
  7.2 404.7 %reduce-scatter.2.cloned.1.call-start = ((), (), s32[]{:S(2)}) async-start(), calls=%async_computation.1 | async-start | bytes 2949120 | tf_op jit(solution)/shard_map/reduce_scatter | solution.py:1306
  13.4 12.4 %collective-permute-start.1 = (bf16[2,128,768]{2,1,0:T(8,128)(2,1)S(1)}, bf16[2,128,768]{2,1,0:T(8,128)(2,1)S(1)}, u32[]{:S(2)}, u32[]{:S(2)}) collective-permute-start(bf16[2,128,768]{2,1,0:T(8,128)(2,1)S(1)} %add_convert_fusion.10), channel_id=1, source_target_pairs={{0,2},{1,3},{2,0},{3,1},{4,6},{5,7},{6,4},{7,5},{8,10},{9,11},{10,... | collective-permute-start | bytes 1179656 | tf_op jit(solution)/shard_map/ppermute | solution.py:21
  17.2 17.2 %collective-permute-start.5 = (bf16[384,768]{1,0:T(8,128)(2,1)}, bf16[384,768]{1,0:T(8,128)(2,1)S(1)}, u32[]{:S(2)}, u32[]{:S(2)}) collective-permute-start(bf16[384,768]{1,0:T(8,128)(2,1)} %dynamic-slice_bitcast_fusion.3), channel_id=1, source_target_pairs={{16,0},{17,1},{18,2},{19,3},{20,4},{21,5},{22,6},{23,7},{24,8},{25... | collective-permute-start | bytes 1769480 | tf_op jit(solution)/shard_map/ppermute | solution.py:25
  25.9 2.5 collective-permute-start.3
  26.0 11.5 %collective-permute-start.4 = (bf16[256,768]{1,0:T(8,128)(2,1)S(1)}, bf16[256,768]{1,0:T(8,128)(2,1)S(1)}, u32[]{:S(2)}, u32[]{:S(2)}) collective-permute-start(bf16[256,768]{1,0:T(8,128)(2,1)S(1)} %get-tuple-element.137), channel_id=1, source_target_pairs={{0,2},{1,3},{2,0},{3,1},{4,6},{5,7},{6,4},{7,5},{8,10},{9,11},{10,... | collective-permute-start | bytes 1179656 | tf_op jit(solution)/shard_map/ppermute | solution.py:21
  37.6 17.6 %collective-permute-start.8 = (bf16[384,768]{1,0:T(8,128)(2,1)S(1)}, bf16[384,768]{1,0:T(8,128)(2,1)S(1)}, u32[]{:S(2)}, u32[]{:S(2)}) collective-permute-start(bf16[384,768]{1,0:T(8,128)(2,1)S(1)} %dynamic-slice_bitcast_fusion.2), channel_id=1, source_target_pairs={{16,0},{17,1},{18,2},{19,3},{20,4},{21,5},{22,6},{23,7},{24,8},{25... | collective-permute-start | bytes 1769480 | tf_op jit(solution)/shard_map/ppermute | solution.py:25
  40.5 14.7 %collective-permute-start.7 = (bf16[2,128,768]{2,1,0:T(8,128)(2,1)S(1)}, bf16[2,128,768]{2,1,0:T(8,128)(2,1)S(1)}, u32[]{:S(2)}, u32[]{:S(2)}) collective-permute-start(bf16[2,128,768]{2,1,0:T(8,128)(2,1)S(1)} %add_convert_fusion.8), channel_id=1, source_target_pairs={{0,2},{1,3},{2,0},{3,1},{4,6},{5,7},{6,4},{7,5},{8,10},{9,11},{10,... | collective-permute-start | bytes 1179656 | tf_op jit(solution)/shard_map/ppermute | solution.py:21
  55.4 11.5 %collective-permute-start.10 = (bf16[256,768]{1,0:T(8,128)(2,1)S(1)}, bf16[256,768]{1,0:T(8,128)(2,1)S(1)}, u32[]{:S(2)}, u32[]{:S(2)}) collective-permute-start(bf16[256,768]{1,0:T(8,128)(2,1)S(1)} %get-tuple-element.146), channel_id=1, source_target_pairs={{0,2},{1,3},{2,0},{3,1},{4,6},{5,7},{6,4},{7,5},{8,10},{9,11},{10,... | collective-permute-start | bytes 1179656 | tf_op jit(solution)/shard_map/ppermute | solution.py:21
  67.9 31.1 %collective-permute-start.17 = (bf16[784,768]{1,0:T(8,128)(2,1)}, bf16[784,768]{1,0:T(8,128)(2,1)S(1)}, u32[]{:S(2)}, u32[]{:S(2)}) collective-permute-start(bf16[784,768]{1,0:T(8,128)(2,1)} %pack.1), channel_id=1, source_target_pairs={{16,0},{17,1},{18,2},{19,3},{20,4},{21,5},{22,6},{23,7},{24,8},{25... | collective-permute-start | bytes 3612680 | tf_op jit(solution)/shard_map/ppermute | solution.py:25
  71.0 11.2 %collective-permute-start.14 = (bf16[2,128,768]{2,1,0:T(8,128)(2,1)S(1)}, bf16[2,128,768]{2,1,0:T(8,128)(2,1)S(1)}, u32[]{:S(2)}, u32[]{:S(2)}) collective-permute-start(bf16[2,128,768]{2,1,0:T(8,128)(2,1)S(1)} %add_convert_fusion.6.mlp_ref), channel_id=1, source_target_pairs={{0,2},{1,3},{2,0},{3,1},{4,6},{5,7},{6,4},{7,5},{8,10},{9,11},{10,... | collective-permute-start | bytes 1179656 | tf_op jit(solution)/shard_map/ppermute | solution.py:21
  82.2 16.8 %collective-permute-start.16 = (bf16[2,384,768]{2,1,0:T(8,128)(2,1)S(1)}, bf16[2,384,768]{2,1,0:T(8,128)(2,1)S(1)}, u32[]{:S(2)}, u32[]{:S(2)}) collective-permute-start(bf16[2,384,768]{2,1,0:T(8,128)(2,1)S(1)} %pad_maximum_fusion.p0a), channel_id=1, source_target_pairs={{0,1},{1,0},{2,3},{3,2},{4,5},{5,4},{6,7},{7,6},{8,9},{9,8},{10,11... | collective-permute-start | bytes 3538952 | tf_op jit(solution)/shard_map/ppermute | solution.py:21
  82.2 28.5 %collective-permute-start.19 = (bf16[2,384,768]{2,1,0:T(8,128)(2,1)S(1)}, bf16[2,384,768]{2,1,0:T(8,128)(2,1)}, u32[]{:S(2)}, u32[]{:S(2)}) collective-permute-start(bf16[2,384,768]{2,1,0:T(8,128)(2,1)S(1)} %pad_maximum_fusion.p0a), channel_id=1, source_target_pairs={{0,2},{1,3},{2,0},{3,1},{4,6},{5,7},{6,4},{7,5},{8,10},{9,11},{10,... | collective-permute-start | bytes 3538952 | tf_op jit(solution)/shard_map/ppermute | solution.py:21
  83.9 28.2 %collective-permute-start.20 = (bf16[2,384,768]{2,1,0:T(8,128)(2,1)S(1)}, bf16[2,384,768]{2,1,0:T(8,128)(2,1)}, u32[]{:S(2)}, u32[]{:S(2)}) collective-permute-start(bf16[2,384,768]{2,1,0:T(8,128)(2,1)S(1)} %pad_maximum_fusion.p0a), channel_id=1, source_target_pairs={{0,4},{4,0},{8,12},{12,8},{1,5},{5,1},{9,13},{13,9},{2,6},{6,2},{1... | collective-permute-start | bytes 3538952 | tf_op jit(solution)/shard_map/ppermute | solution.py:21
  89.0 8.7 %collective-permute-start.15 = (bf16[128,768]{1,0:T(8,128)(2,1)S(1)}, bf16[128,768]{1,0:T(8,128)(2,1)S(1)}, u32[]{:S(2)}, u32[]{:S(2)}) collective-permute-start(bf16[128,768]{1,0:T(8,128)(2,1)S(1)} %slice_bitcast_fusion.2), channel_id=1, source_target_pairs={{0,16},{1,17},{2,18},{3,19},{4,20},{5,21},{6,22},{7,23},{8,24},{9,... | collective-permute-start | bytes 589832 | tf_op jit(solution)/shard_map/ppermute | solution.py:25
  99.0 4.0 collective-permute-start.18
  112.1 39.7 %collective-permute-start.21 = (bf16[2,384,768]{2,1,0:T(8,128)(2,1)}, bf16[2,384,768]{2,1,0:T(8,128)(2,1)S(1)}, u32[]{:S(2)}, u32[]{:S(2)}) collective-permute-start(bf16[2,384,768]{2,1,0:T(8,128)(2,1)} %collective-permute-done.19.p2a), channel_id=1, source_target_pairs={{0,4},{4,0},{8,12},{12,8},{1,5},{5,1},{9,13},{13,9},{2,6},{6,2},{1... | collective-permute-start | bytes 3538952 | tf_op jit(solution)/shard_map/ppermute | solution.py:21
  113.7 2.8 collective-permute-start.11
  114.2 2.9 collective-permute-start.12
  151.9 2.6 collective-permute-start.22
  155.8 19.7 %collective-permute-start.23 = (bf16[512,768]{1,0:T(8,128)(2,1)S(1)}, bf16[512,768]{1,0:T(8,128)(2,1)S(1)}, u32[]{:S(2)}, u32[]{:S(2)}) collective-permute-start(bf16[512,768]{1,0:T(8,128)(2,1)S(1)} %add_convert_fusion.1), channel_id=1, source_target_pairs={{0,2},{1,3},{2,0},{3,1},{4,6},{5,7},{6,4},{7,5},{8,10},{9,11},{10,... | collective-permute-start | bytes 2359304 | tf_op jit(solution)/shard_map/ppermute | solution.py:21
  165.6 10.9 %collective-permute-start.25 = (bf16[2,384,768]{2,1,0:T(8,128)(2,1)}, bf16[2,384,768]{2,1,0:T(8,128)(2,1)S(1)}, u32[]{:S(2)}, u32[]{:S(2)}) collective-permute-start(bf16[2,384,768]{2,1,0:T(8,128)(2,1)} %collective-permute-done.20.p0b), channel_id=1, source_target_pairs={{0,1},{1,0},{2,3},{3,2},{4,5},{5,4},{6,7},{7,6},{8,9},{9,8},{10,11... | collective-permute-start | bytes 3538952 | tf_op jit(solution)/shard_map/ppermute | solution.py:21
  165.9 10.6 %collective-permute-start.26 = (bf16[2,384,768]{2,1,0:T(8,128)(2,1)}, bf16[2,384,768]{2,1,0:T(8,128)(2,1)S(1)}, u32[]{:S(2)}, u32[]{:S(2)}) collective-permute-start(bf16[2,384,768]{2,1,0:T(8,128)(2,1)} %collective-permute-done.19.p2a), channel_id=1, source_target_pairs={{0,1},{1,0},{2,3},{3,2},{4,5},{5,4},{6,7},{7,6},{8,9},{9,8},{10,11... | collective-permute-start | bytes 3538952 | tf_op jit(solution)/shard_map/ppermute | solution.py:21
  166.2 10.3 %collective-permute-start.27 = (bf16[2,384,768]{2,1,0:T(8,128)(2,1)S(1)}, bf16[2,384,768]{2,1,0:T(8,128)(2,1)S(1)}, u32[]{:S(2)}, u32[]{:S(2)}) collective-permute-start(bf16[2,384,768]{2,1,0:T(8,128)(2,1)S(1)} %collective-permute-done.21.p2b), channel_id=1, source_target_pairs={{0,1},{1,0},{2,3},{3,2},{4,5},{5,4},{6,7},{7,6},{8,9},{9,8},{10,11... | collective-permute-start | bytes 3538952 | tf_op jit(solution)/shard_map/ppermute | solution.py:21
  175.5 2.5 collective-permute-start.24
  201.2 9.3 %collective-permute-start.28 = (bf16[7,512,768]{2,1,0:T(8,128)(2,1)}, bf16[7,512,768]{2,1,0:T(8,128)(2,1)S(1)}, u32[]{:S(2)}, u32[]{:S(2)}) collective-permute-start(bf16[7,512,768]{2,1,0:T(8,128)(2,1)} %get-tuple-element.185.own_ref), channel_id=1, source_target_pairs={{0,1},{1,0},{2,3},{3,2},{4,5},{5,4},{6,7},{7,6},{8,9},{9,8},{10,11... | collective-permute-start | bytes 16515080 | tf_op jit(solution)/shard_map/ppermute | solution.py:21
  201.5 20.3 %collective-permute-start.29 = (bf16[512,768]{1,0:T(8,128)(2,1)}, bf16[512,768]{1,0:T(8,128)(2,1)S(1)}, u32[]{:S(2)}, u32[]{:S(2)}) collective-permute-start(bf16[512,768]{1,0:T(8,128)(2,1)} %get-tuple-element.184.g0), channel_id=1, source_target_pairs={{0,2},{1,3},{2,0},{3,1},{4,6},{5,7},{6,4},{7,5},{8,10},{9,11},{10,... | collective-permute-start | bytes 2359304 | tf_op jit(solution)/shard_map/ppermute | solution.py:21
  221.7 49.1 %collective-permute-start.34 = (bf16[2,672,768]{2,1,0:T(8,128)(2,1)}, bf16[2,672,768]{2,1,0:T(8,128)(2,1)S(1)}, u32[]{:S(2)}, u32[]{:S(2)}) collective-permute-start(bf16[2,672,768]{2,1,0:T(8,128)(2,1)} %get-tuple-element.199.last_ref), channel_id=1, source_target_pairs={{0,16},{1,17},{2,18},{3,19},{4,20},{5,21},{6,22},{7,23},{8,24},{9,... | collective-permute-start | bytes 6193160 | tf_op jit(solution)/shard_map/ppermute | solution.py:25
  226.2 36.7 %collective-permute-start.33 = (bf16[864,768]{1,0:T(8,128)(2,1)}, bf16[864,768]{1,0:T(8,128)(2,1)}, u32[]{:S(2)}, u32[]{:S(2)}) collective-permute-start(bf16[864,768]{1,0:T(8,128)(2,1)} %get-tuple-element.198), channel_id=1, source_target_pairs={{0,2},{1,3},{2,0},{3,1},{4,6},{5,7},{6,4},{7,5},{8,10},{9,11},{10,... | collective-permute-start | bytes 3981320 | tf_op jit(solution)/shard_map/ppermute | solution.py:21
  261.4 10.7 %collective-permute-start.32 = (bf16[128,768]{1,0:T(8,128)(2,1)S(1)}, bf16[128,768]{1,0:T(8,128)(2,1)S(1)}, u32[]{:S(2)}, u32[]{:S(2)}) collective-permute-start(bf16[128,768]{1,0:T(8,128)(2,1)S(1)} %add_convert_fusion.11.near_ref), channel_id=1, source_target_pairs={{0,2},{1,3},{2,0},{3,1},{4,6},{5,7},{6,4},{7,5},{8,10},{9,11},{10,... | collective-permute-start | bytes 589832 | tf_op jit(solution)/shard_map/ppermute | solution.py:21
  272.1 24.0 %collective-permute-start.36 = (bf16[672,768]{1,0:T(8,128)(2,1)S(1)}, bf16[672,768]{1,0:T(8,128)(2,1)S(1)}, u32[]{:S(2)}, u32[]{:S(2)}) collective-permute-start(bf16[672,768]{1,0:T(8,128)(2,1)S(1)} %fusion), channel_id=1, source_target_pairs={{0,2},{1,3},{2,0},{3,1},{4,6},{5,7},{6,4},{7,5},{8,10},{9,11},{10,... | collective-permute-start | bytes 3096584 | tf_op jit(solution)/shard_map/ppermute | solution.py:21
  273.5 31.8 %collective-permute-start.38 = (bf16[864,768]{1,0:T(8,128)(2,1)S(1)}, bf16[864,768]{1,0:T(8,128)(2,1)S(1)}, u32[]{:S(2)}, u32[]{:S(2)}) collective-permute-start(bf16[864,768]{1,0:T(8,128)(2,1)S(1)} %copy-done.7), channel_id=1, source_target_pairs={{0,16},{1,17},{2,18},{3,19},{4,20},{5,21},{6,22},{7,23},{8,24},{9,... | collective-permute-start | bytes 3981320 | tf_op jit(solution)/shard_map/ppermute | solution.py:25
  280.8 10.7 %collective-permute-start.35 = (bf16[128,768]{1,0:T(8,128)(2,1)}, bf16[128,768]{1,0:T(8,128)(2,1)S(1)}, u32[]{:S(2)}, u32[]{:S(2)}) collective-permute-start(bf16[128,768]{1,0:T(8,128)(2,1)} %sel_back.1.sel_own), channel_id=1, source_target_pairs={{16,0},{17,1},{18,2},{19,3},{20,4},{21,5},{22,6},{23,7},{24,8},{25... | collective-permute-start | bytes 589832 | tf_op jit(solution)/shard_map/ppermute | solution.py:25
  296.2 2.4 collective-permute-start.37
  308.4 15.6 %collective-permute-start.40 = (bf16[2,128,768]{2,1,0:T(8,128)(2,1)S(1)}, bf16[2,128,768]{2,1,0:T(8,128)(2,1)S(1)}, u32[]{:S(2)}, u32[]{:S(2)}) collective-permute-start(bf16[2,128,768]{2,1,0:T(8,128)(2,1)S(1)} %add_convert_fusion.5), channel_id=1, source_target_pairs={{0,2},{1,3},{2,0},{3,1},{4,6},{5,7},{6,4},{7,5},{8,10},{9,11},{10,... | collective-permute-start | bytes 1179656 | tf_op jit(solution)/shard_map/ppermute | solution.py:21
  324.0 6.2 %collective-permute-start.43 = (bf16[2,512,768]{2,1,0:T(8,128)(2,1)}, bf16[2,512,768]{2,1,0:T(8,128)(2,1)}, u32[]{:S(2)}, u32[]{:S(2)}) collective-permute-start(bf16[2,512,768]{2,1,0:T(8,128)(2,1)} %get-tuple-element.231), channel_id=1, source_target_pairs={{0,1},{1,0},{2,3},{3,2},{4,5},{5,4},{6,7},{7,6},{8,9},{9,8},{10,11... | collective-permute-start | bytes 4718600 | tf_op jit(solution)/shard_map/ppermute | solution.py:21
  325.3 28.8 %collective-permute-start.45 = (bf16[768,768]{1,0:T(8,128)(2,1)S(1)}, bf16[768,768]{1,0:T(8,128)(2,1)}, u32[]{:S(2)}, u32[]{:S(2)}) collective-permute-start(bf16[768,768]{1,0:T(8,128)(2,1)S(1)} %copy-done.10), channel_id=1, source_target_pairs={{0,16},{1,17},{2,18},{3,19},{4,20},{5,21},{6,22},{7,23},{8,24},{9,... | collective-permute-start | bytes 3538952 | tf_op jit(solution)/shard_map/ppermute | solution.py:25
  330.1 3.5 collective-permute-start.41
  332.5 21.5 %collective-permute-start.44 = (bf16[512,768]{1,0:T(8,128)(2,1)}, bf16[512,768]{1,0:T(8,128)(2,1)S(1)}, u32[]{:S(2)}, u32[]{:S(2)}) collective-permute-start(bf16[512,768]{1,0:T(8,128)(2,1)} %fusion.2), channel_id=1, source_target_pairs={{0,2},{1,3},{2,0},{3,1},{4,6},{5,7},{6,4},{7,5},{8,10},{9,11},{10,... | collective-permute-start | bytes 2359304 | tf_op jit(solution)/shard_map/ppermute | solution.py:21
  354.0 32.7 %collective-permute-start.46 = (bf16[2,128,768]{2,1,0:T(8,128)(2,1)S(1)}, bf16[2,128,768]{2,1,0:T(8,128)(2,1)}, u32[]{:S(2)}, u32[]{:S(2)}) collective-permute-start(bf16[2,128,768]{2,1,0:T(8,128)(2,1)S(1)} %add_convert_fusion.3), channel_id=1, source_target_pairs={{0,2},{1,3},{2,0},{3,1},{4,6},{5,7},{6,4},{7,5},{8,10},{9,11},{10,... | collective-permute-start | bytes 1179656 | tf_op jit(solution)/shard_map/ppermute | solution.py:21
  361.5 26.4 %collective-permute-start.50 = (bf16[2,192,768]{2,1,0:T(8,128)(2,1)}, bf16[2,192,768]{2,1,0:T(8,128)(2,1)}, u32[]{:S(2)}, u32[]{:S(2)}) collective-permute-start(bf16[2,192,768]{2,1,0:T(8,128)(2,1)} %get-tuple-element.275), channel_id=1, source_target_pairs={{0,4},{4,0},{8,12},{12,8},{1,5},{5,1},{9,13},{13,9},{2,6},{6,2},{1... | collective-permute-start | bytes 1769480 | tf_op jit(solution)/shard_map/ppermute | solution.py:21
  368.8 3.8 collective-permute-start.53
  372.6 10.7 %collective-permute-start.54 = (f32[6,768]{1,0:T(8,128)S(1)}, f32[6,768]{1,0:T(8,128)S(1)}, u32[]{:S(2)}, u32[]{:S(2)}) collective-permute-start(f32[6,768]{1,0:T(8,128)S(1)} %add.127), channel_id=1, source_target_pairs={{0,4},{4,0},{8,12},{12,8},{1,5},{5,1},{9,13},{13,9},{2,6},{6,2},{1... | collective-permute-start | bytes 55304 | tf_op jit(solution)/shard_map/ppermute | solution.py:21
  374.2 22.6 %collective-permute-start.48 = (bf16[512,768]{1,0:T(8,128)(2,1)}, bf16[512,768]{1,0:T(8,128)(2,1)S(1)}, u32[]{:S(2)}, u32[]{:S(2)}) collective-permute-start(bf16[512,768]{1,0:T(8,128)(2,1)} %get-tuple-element.246.d_rows_ref), channel_id=1, source_target_pairs={{16,0},{17,1},{18,2},{19,3},{20,4},{21,5},{22,6},{23,7},{24,8},{25... | collective-permute-start | bytes 2359304 | tf_op jit(solution)/shard_map/ppermute | solution.py:25
  375.4 21.4 %collective-permute-start.49 = (bf16[512,768]{1,0:T(8,128)(2,1)}, bf16[512,768]{1,0:T(8,128)(2,1)}, u32[]{:S(2)}, u32[]{:S(2)}) collective-permute-start(bf16[512,768]{1,0:T(8,128)(2,1)} %get-tuple-element.248), channel_id=1, source_target_pairs={{0,16},{1,17},{2,18},{3,19},{4,20},{5,21},{6,22},{7,23},{8,24},{9,... | collective-permute-start | bytes 2359304 | tf_op jit(solution)/shard_map/ppermute | solution.py:25
  383.9 5.8 %collective-permute-start.55 = (f32[6,768]{1,0:T(8,128)}, f32[6,768]{1,0:T(8,128)}, u32[]{:S(2)}, u32[]{:S(2)}) collective-permute-start(f32[6,768]{1,0:T(8,128)} %add.128), channel_id=1, source_target_pairs={{0,8},{4,12},{8,0},{12,4},{1,9},{5,13},{9,1},{13,5},{2,10},{6,14},... | collective-permute-start | bytes 55304 | tf_op jit(solution)/shard_map/ppermute | solution.py:21
  387.8 9.0 %collective-permute-start.47 = (bf16[2,128,768]{2,1,0:T(8,128)(2,1)S(1)}, bf16[2,128,768]{2,1,0:T(8,128)(2,1)}, u32[]{:S(2)}, u32[]{:S(2)}) collective-permute-start(bf16[2,128,768]{2,1,0:T(8,128)(2,1)S(1)} %add_convert_fusion.2.own_ref), channel_id=1, source_target_pairs={{0,1},{1,0},{2,3},{3,2},{4,5},{5,4},{6,7},{7,6},{8,9},{9,8},{10,11... | collective-permute-start | bytes 1179656 | tf_op jit(solution)/shard_map/ppermute | solution.py:21
  389.6 20.4 %collective-permute-start.51 = (bf16[192,768]{0,1:T(8,128)(2,1)S(1)}, bf16[192,768]{0,1:T(8,128)(2,1)S(1)}, u32[]{:S(2)}, u32[]{:S(2)}) collective-permute-start(bf16[192,768]{0,1:T(8,128)(2,1)S(1)} %dynamic-slice_bitcast_fusion.6), channel_id=1, source_target_pairs={{0,8},{4,12},{8,0},{12,4},{1,9},{5,13},{9,1},{13,5},{2,10},{6,14},... | collective-permute-start | bytes 884744 | tf_op jit(solution)/shard_map/ppermute | solution.py:21
  390.5 5.7 %collective-permute-start.56 = (f32[3,192]{1,0:T(4,128)S(1)}, f32[3,192]{1,0:T(4,128)S(1)}, u32[]{:S(2)}, u32[]{:S(2)}) collective-permute-start(f32[3,192]{1,0:T(4,128)S(1)} %slice.79), channel_id=1, source_target_pairs={{0,16},{1,17},{2,18},{3,19},{4,20},{5,21},{6,22},{7,23},{8,24},{9,... | collective-permute-start | bytes 6920 | tf_op jit(solution)/shard_map/ppermute | solution.py:25
  (72 other events, 605.6 us)
Sparse Core Ops, SparseCore 0:
  324.2 52.9 reduce-scatter.1

commit v2 on v1

--- a/solution.py
+++ b/solution.py
@@ -1134,10 +1134,10 @@
     return add(near, swap(near, "tensor", 2))
 
 
-def scatter_groups(pack):
+def scatter_groups(pack, later):
     count, me = lax.axis_size("dp"), lax.axis_index("dp")
     if count != 4:
-        return lax.psum_scatter(pack, "dp", scatter_dimension=0, tiled=True)
+        return lax.psum_scatter(pack, "dp", scatter_dimension=0, tiled=True), later
     for bit in (1, 2):
         rows = pack.shape[0] // 2
         side = (me // bit) % 2
@@ -1149,7 +1149,9 @@
             keep = lax.dynamic_index_in_dim(pack, side, 0, keepdims=False)
             send = lax.dynamic_index_in_dim(pack, 1 - side, 0, keepdims=False)
         pack = add(keep, swap(send, "dp", bit))
-    return pack
+        if bit == 1:
+            later = after(later, pack)
+    return pack, later
 
 
 def body(
@@ -1311,7 +1313,10 @@
     sent_result = hop(after(result_low, attn_hop), 0, 1)
     half = add(near, far)
     other = core(half)
-    attn_sum = scatter_groups(r_attn)
+    vecs = jnp.concatenate([r_vec[0:1], gain_two, r_vec[1:2], row_vec, m_vec], 0)
+    vecs = vecs + core(vecs)
+    vecs = vecs + cross(vecs)
+    attn_sum, vecs = scatter_groups(r_attn, vecs)
 
     combined = finish(
         info, half, other, r_d_mid, picked, gains, selected, d_rows, d_rows_far, sent_result, result
@@ -1322,12 +1327,10 @@
     qkv_grad = jnp.swapaxes(attn_sum[:, : 3 * cols].reshape(share, 3, cols), 0, 1).astype(F32)
     mix_grad = jnp.swapaxes(attn_sum[:, 3 * cols : 4 * cols], 0, 1).astype(F32)
 
-    vecs = jnp.concatenate([r_vec[0:1], gain_two, r_vec[1:2], row_vec, m_vec], 0)
-    for axis in ("tensor", "dp"):
-        bit = 1
-        while bit < lax.axis_size(axis):
-            vecs = vecs + swap(vecs, axis, bit)
-            bit *= 2
+    bit = 1
+    while bit < lax.axis_size("dp"):
+        vecs = vecs + swap(vecs, "dp", bit)
+        bit *= 2
     vecs = lax.dynamic_slice_in_dim(vecs, lax.axis_index("dp") * share, share, 1)
     dense_vec = vecs[3:6] + hop(vecs[3:6], 0, 1)
     vecs = jnp.where(is_dense, dense_vec, vecs[:3])

time: 426 us -> 427 us (level)
    unnamed x128 -> x132, local copies, waits for them, and re-layouts: 16.7 us -> 17.3 us
  transfers between devices with their start and end apart: 58 -> 58, of which waited for: 34 -> 35; matrix products, arithmetic and copies ran while one was open for 7% -> 6% of each run, Pallas kernels for 38% -> 38%
where the time goes in v2:
time: 427 us; the launch traced here: 422 us
  Pallas kernels  186 us (44%)
  waiting for transfers between devices  108 us (25%)
  starting transfers between devices  65.6 us (15%)
  local copies, waits for them, and re-layouts  28.2 us (7%)
  other arithmetic  18.4 us (4%)
  between operations  15.1 us (4%)
    ppermute x46, waiting for transfers between devices, swap(): return lax.ppermute(block, axis, [(i, i ^ bit) for i in range(count)])  79.9 us
    pallas_call x2, Pallas kernels, attention(): pl.pallas_call(functools.partial(attention_kernel, heads, width, base, pe...  33.4 us
    ppermute x11, starting transfers between devices, hop(): return lax.ppermute(block, 'section', [(source, target)])  33 us
    ppermute x46, starting transfers between devices, swap(): return lax.ppermute(block, axis, [(i, i ^ bit) for i in range(count)])  32.6 us
    pallas_call x1, Pallas kernels, attention_back(): pl.pallas_call(functools.partial(attention_back_kernel, heads, width, blo...  29.5 us
    ppermute x11, waiting for transfers between devices, hop(): return lax.ppermute(block, 'section', [(source, target)])  28.2 us
    pallas_call x1, Pallas kernels, mlp_pass(): pl.pallas_call(functools.partial(mlp_kernel, half), out_shape=(wide, low,...  22.4 us
    unnamed x132, local copies, waits for them, and re-layouts  17.3 us
  transfers between devices with their start and end apart: 58, of which 35 were waited for; matrix products, arithmetic and copies ran while one was open for 6% of the time, Pallas kernels for 38%

profile of v2, /device:TPU:0, one launch (start us, length us, event | category | flops | bytes accessed | tf_op | source)
XLA Modules:
  0.0 421.8 jit_solution(14353376635322492021)
XLA Ops:
  7.2 3.1 pick.1
  13.4 3.0 collective-permute-start.1
  29.1 5.1 %routed_attn.1 = (bf16[512,768]{1,0:T(8,128)(2,1)}, bf16[512,768]{1,0:T(8,128)(2,1)}, bf16[512,192]{1,0:T(8,128)(2,1)}, bf16[512,192]{1,0:T(8,128)(2,1)}, bf16[5...) custom-call(s32[4]{0:T(128)} %pad_add_fusion.info, ...), custom_call_target="tpu_custom_call" | custom-call | flops 500000000 | bytes 16500000 | tf_op jit(solution)/shard_map/routed_attn/pallas_call | solution.py:195
  34.4 3.1 collective-permute-done.4.tok2a
  42.3 2.4 pack.1
  44.7 10.5 %collective-permute-done.8 = bf16[384,768]{1,0:T(8,128)(2,1)S(1)} collective-permute-done((bf16[384,768]{1,0:T(8,128)(2,1)S(1)}, bf16[384,768]{1,0:T(8,128)(2,1)S(1)}, u32[]{:S(2)}, u32[]{:S(2)}) %collective-permute-start.8) | collective-permute-done | bytes 589856 | tf_op jit(solution)/shard_map/ppermute | solution.py:25
  58.0 5.8 %routed_mlp.1 = (bf16[512,768]{1,0:T(8,128)(2,1)}, bf16[512,768]{1,0:T(8,128)(2,1)}, bf16[512,768]{1,0:T(8,128)(2,1)}, f32[512,768]{1,0:T(8,128)}, bf16[2,128,76...) custom-call(s32[4]{0:T(128)} %pad_add_fusion.info, bf16[512,768]{1,0:T(8,128)(2,1)} %get-tuple-element.140.picked_ref, ...), custom_call_target="tpu_custom_call" | custom-call | flops 600000000 | bytes 19800000 | tf_op jit(solution)/shard_map/routed_mlp/pallas_call | solution.py:227
  63.8 3.1 collective-permute-done.10.tok2b
  73.1 9.1 %collective-permute-done.14.mlp2_ref = bf16[2,128,768]{2,1,0:T(8,128)(2,1)S(1)} collective-permute-done((bf16[2,128,768]{2,1,0:T(8,128)(2,1)S(1)}, bf16[2,128,768]{2,1,0:T(8,128)(2,1)S(1)}, u32[]{:S(2)}, u32[]{:S(2)}) %collective-permute-start.14) | collective-permute-done | bytes 393248 | tf_op jit(solution)/shard_map/ppermute | solution.py:21
  85.5 2.5 update.1
  89.0 4.4 %collective-permute-start.15 = (bf16[128,768]{1,0:T(8,128)(2,1)S(1)}, bf16[128,768]{1,0:T(8,128)(2,1)S(1)}, u32[]{:S(2)}, u32[]{:S(2)}) collective-permute-start(bf16[128,768]{1,0:T(8,128)(2,1)S(1)} %slice_bitcast_fusion.2), channel_id=1, source_target_pairs={{0,16},{1,17},{2,18},{3,19},{4,20},{5,21},{6,22},{7,23},{8,24},{9,... | collective-permute-start | bytes 589832 | tf_op jit(solution)/shard_map/ppermute | solution.py:25
  93.4 4.2 %collective-permute-done.15 = bf16[128,768]{1,0:T(8,128)(2,1)S(1)} collective-permute-done((bf16[128,768]{1,0:T(8,128)(2,1)S(1)}, bf16[128,768]{1,0:T(8,128)(2,1)S(1)}, u32[]{:S(2)}, u32[]{:S(2)}) %collective-permute-start.15) | collective-permute-done | bytes 196640 | tf_op jit(solution)/shard_map/ppermute | solution.py:25
  100.0 3.0 prepare.1
  103.0 7.7 %collective-permute-done.19.p2a = bf16[2,384,768]{2,1,0:T(8,128)(2,1)} collective-permute-done((bf16[2,384,768]{2,1,0:T(8,128)(2,1)S(1)}, bf16[2,384,768]{2,1,0:T(8,128)(2,1)}, u32[]{:S(2)}, u32[]{:S(2)}) %collective-permute-start.19) | collective-permute-done | bytes 1179680 | tf_op jit(solution)/shard_map/ppermute | solution.py:21
  117.9 10.3 %project.1 = (bf16[512,768]{1,0:T(8,128)(2,1)}, bf16[4,512,768]{2,1,0:T(8,128)(2,1)}, bf16[4,512,256]{2,1,0:T(8,128)(2,1)}, bf16[4,512,256]{2,1,0:T(8,128)(2,1)}, bf16[4,512,256]{2,1,0:T(8,128)(2,1)}) custom-call(s32[4]{0:T(128)} %pad_add_fusion.info, bf16[512,768]{1,0:T(8,128)(2,1)} %dynamic-slice_bitcast_fusion.tok0, bf16[512,768]{1,0:T(8,128)(2,1)} %copy-done.38, ...), custom_call_target="tpu_custom_call" | custom-call | flops 900000000 | bytes 29700000 | tf_op jit(solution)/shard_map/project/pallas_call | solution.py:526
  128.2 23.7 %attention.3 = (bf16[512,768]{1,0:T(8,128)(2,1)}, bf16[512,768]{1,0:T(8,128)(2,1)}, bf16[2,512,256]{2,1,0:T(8,128)(2,1)}, f32[2,512,128]{2,1,0:T(8,128)}) custom-call(s32[4]{0:T(128)} %pad_add_fusion.info, bf16[4,512,256]{2,1,0:T(8,128)(2,1)} %get-tuple-element.165.q_ref, bf16[2048,256]{1,0:T(8,128)(2,1)} %bitcast.94, bf16[2048,256]{1,0:T(8,128)(2,1)} %bitcast.97, ...), custom_call_target="tpu_custom_call" | custom-call | flops 30000000 | bytes 990000 | tf_op jit(solution)/shard_map/attention/pallas_call | solution.py:607
  152.1 2.3 collective-permute-done.22
  155.9 9.8 %attention.2 = (bf16[512,768]{1,0:T(8,128)(2,1)}, bf16[512,768]{1,0:T(8,128)(2,1)}, bf16[2,512,256]{2,1,0:T(8,128)(2,1)}, f32[2,512,128]{2,1,0:T(8,128)}) custom-call(s32[4]{0:T(128)} %pad_add_fusion.info, bf16[4,512,256]{2,1,0:T(8,128)(2,1)} %get-tuple-element.165.q_ref, bf16[2048,256]{1,0:T(8,128)(2,1)} %bitcast.95, bf16[2048,256]{1,0:T(8,128)(2,1)} %bitcast.98, ...), custom_call_target="tpu_custom_call" | custom-call | flops 30000000 | bytes 990000 | tf_op jit(solution)/shard_map/attention/pallas_call | solution.py:607
  166.3 9.1 %collective-permute-done.23.far_ref = bf16[512,768]{1,0:T(8,128)(2,1)S(1)} collective-permute-done((bf16[512,768]{1,0:T(8,128)(2,1)S(1)}, bf16[512,768]{1,0:T(8,128)(2,1)S(1)}, u32[]{:S(2)}, u32[]{:S(2)}) %collective-permute-start.23) | collective-permute-done | bytes 786464 | tf_op jit(solution)/shard_map/ppermute | solution.py:21
  178.9 22.4 %dense_mlp.1 = (f32[512,768]{1,0:T(8,128)}, bf16[512,768]{1,0:T(8,128)(2,1)}, f32[512,768]{1,0:T(8,128)}, bf16[512,768]{1,0:T(8,128)(2,1)}, bf16[4,512,768]{2,1,...) custom-call(bf16[512,768]{1,0:T(8,128)(2,1)} %get-tuple-element.164.rows_ref, ...), custom_call_target="tpu_custom_call" | custom-call | flops 2100000000 | bytes 69300000 | tf_op jit(solution)/shard_map/dense_mlp/pallas_call | solution.py:716
  202.8 7.7 %collective-permute-done.28.act2_ref.pre2_ref.near2_ref.rows2_ref.g1 = bf16[7,512,768]{2,1,0:T(8,128)(2,1)S(1)} collective-permute-done((bf16[7,512,768]{2,1,0:T(8,128)(2,1)}, bf16[7,512,768]{2,1,0:T(8,128)(2,1)S(1)}, u32[]{:S(2)}, u32[]{:S(2)}) %collective-permute-start.28) | collective-permute-done | bytes 5505056 | tf_op jit(solution)/shard_map/ppermute | solution.py:21
  210.6 2.4 copy-done.2
  213.0 8.7 %far_grads.1 = (bf16[864,768]{1,0:T(8,128)(2,1)}, bf16[2,672,768]{2,1,0:T(8,128)(2,1)}, bf16[96,768]{1,0:T(8,128)(2,1)}) custom-call(bf16[4,512,768]{2,1,0:T(8,128)(2,1)} %get-tuple-element.187.act_ref.pre_ref.near_ref, bf16[4,512,768]{2,1,0:T(8,128)(2,1)} %get-tuple-element.187.act_ref.pre_ref.near_ref, ...), custom_call_target="tpu_custom_call" | custom-call | flops 500000000 | bytes 16500000 | tf_op jit(solution)/shard_map/far_grads/pallas_call | solution.py:780
  221.7 4.4 %collective-permute-start.34 = (bf16[2,672,768]{2,1,0:T(8,128)(2,1)}, bf16[2,672,768]{2,1,0:T(8,128)(2,1)S(1)}, u32[]{:S(2)}, u32[]{:S(2)}) collective-permute-start(bf16[2,672,768]{2,1,0:T(8,128)(2,1)} %get-tuple-element.200.last_ref), channel_id=1, source_target_pairs={{0,16},{1,17},{2,18},{3,19},{4,20},{5,21},{6,22},{7,23},{8,24},{9,... | collective-permute-start | bytes 6193160 | tf_op jit(solution)/shard_map/ppermute | solution.py:25
  229.3 29.5 %attention_back.1 = (bf16[3,2048,192]{2,1,0:T(8,128)(2,1)}, bf16[128,768]{1,0:T(8,128)(2,1)}, bf16[128,768]{1,0:T(8,128)(2,1)}, bf16[128,768]{1,0:T(8,128)(2,1)}) custom-call(s32[4]{0:T(128)} %pad_add_fusion.info, bf16[512,768]{1,0:T(8,128)(2,1)} %get-tuple-element.185.g0, bf16[7,512,768]{2,1,0:T(8,128)(2,1)} %copy-done.2, bf16[512,768]{1,0:T(8,128)(2,1)} %copy-done.16, ...), custom_call_target="tpu_custom_call" | custom-call | flops 3500000000 | bytes 115500000 | tf_op jit(solution)/shard_map/attention_back/pallas_call | solution.py:902
  262.9 5.0 %near_grads.1.part_ref = bf16[864,768]{1,0:T(8,128)(2,1)} custom-call(bf16[4,512,768]{2,1,0:T(8,128)(2,1)} %get-tuple-element.187.act_ref.pre_ref.near_ref, bf16[7,512,768]{2,1,0:T(8,128)(2,1)} %get-tuple-element.186.own_ref, bf16[7,512,768]{2,1,0:T(8,128)(2,1)} %copy-done.2, bf16[7,512,768]{2,1,0:T(8,128)(2,1)} %copy-done.2, ...), custom_call_target="tpu_custom_call" | custom-call | flops 500000000 | bytes 16500000 | tf_op jit(solution)/shard_map/near_grads/pallas_call | solution.py:802
  267.9 2.8 collective-permute-done.34.last_far
  273.5 4.4 %collective-permute-start.38 = (bf16[864,768]{1,0:T(8,128)(2,1)S(1)}, bf16[864,768]{1,0:T(8,128)(2,1)S(1)}, u32[]{:S(2)}, u32[]{:S(2)}) collective-permute-start(bf16[864,768]{1,0:T(8,128)(2,1)S(1)} %copy-done.7), channel_id=1, source_target_pairs={{0,16},{1,17},{2,18},{3,19},{4,20},{5,21},{6,22},{7,23},{8,24},{9,... | collective-permute-start | bytes 3981320 | tf_op jit(solution)/shard_map/ppermute | solution.py:25
  278.6 2.2 sel_back.1.sel_own
  282.1 9.4 %attn_grads.1.part_ref = bf16[768,768]{1,0:T(8,128)(2,1)} custom-call(s32[4]{0:T(128)} %pad_add_fusion.info, bf16[3,4,512,192]{3,2,1,0:T(8,128)(2,1)} %bitcast.87, bf16[4,512,768]{2,1,0:T(8,128)(2,1)} %get-tuple-element.206.normed_ref, bf16[512,768]{1,0:T(8,128)(2,1)} %get-tuple-element.185.g0, bf16[7,512,768]{2,1,0:T(8,128)(2,1)} %copy-done.2, ...), custom_call_target="tpu_custom_call" | custom-call | flops 800000000 | bytes 26400000 | tf_op jit(solution)/shard_map/attn_grads/pallas_call | solution.py:995
  291.5 4.6 %collective-permute-done.36.last_cross = bf16[672,768]{1,0:T(8,128)(2,1)S(1)} collective-permute-done((bf16[672,768]{1,0:T(8,128)(2,1)S(1)}, bf16[672,768]{1,0:T(8,128)(2,1)S(1)}, u32[]{:S(2)}, u32[]{:S(2)}) %collective-permute-start.36) | collective-permute-done | bytes 1032224 | tf_op jit(solution)/shard_map/ppermute | solution.py:21
  296.3 2.3 collective-permute-done.37.sel_other.both_other
  299.4 5.6 %routed_back_mlp.1 = (f32[512,768]{1,0:T(8,128)}, bf16[512,768]{1,0:T(8,128)(2,1)}, bf16[512,768]{1,0:T(8,128)(2,1)}, f32[1,768]{1,0:T(1,128)}, bf16[2,128,768]{...) custom-call(s32[4]{0:T(128)} %pad_add_fusion.info, bf16[128,768]{1,0:T(8,128)(2,1)} %sel_back.1.sel_own, ...), custom_call_target="tpu_custom_call" | custom-call | flops 600000000 | bytes 19800000 | tf_op jit(solution)/shard_map/routed_back_mlp/pallas_call | solution.py:292
  309.6 7.0 %routed_mlp_grads.1 = bf16[768,1536]{1,0:T(8,128)(2,1)} custom-call(s32[4]{0:T(128)} %pad_add_fusion.info, bf16[512,768]{1,0:T(8,128)(2,1)} %get-tuple-element.216.normed_ref, bf16[512,768]{1,0:T(8,128)(2,1)} %get-tuple-element.217.pre_ref, bf16[512,768]{1,0:T(8,128)(2,1)} %get-tuple-element.218.act_ref, bf16[512,768]{1,0:T(8,128)(2,1)} %get-tuple-element.219.grad_ref, ...), custom_call_target="tpu_custom_call" | custom-call | flops 500000000 | bytes 16500000 | tf_op jit(solution)/shard_map/routed_mlp_grads/pallas_call | solution.py:1044
  316.6 7.4 %spread_back.1 = (bf16[2,512,768]{2,1,0:T(8,128)(2,1)}, bf16[2,512,768]{2,1,0:T(8,128)(2,1)}) custom-call(s32[4]{0:T(128)} %pad_add_fusion.info, bf16[3,4,512,192]{3,2,1,0:T(8,128)(2,1)} %bitcast.88, bf16[3,256,768]{2,1,0:T(8,128)(2,1)} %get-tuple-element.163.qkv_ref), custom_call_target="tpu_custom_call" | custom-call | flops 500000000 | bytes 16500000 | tf_op jit(solution)/shard_map/spread_back/pallas_call | solution.py:945
  325.3 4.7 %collective-permute-start.45 = (bf16[768,768]{1,0:T(8,128)(2,1)S(1)}, bf16[768,768]{1,0:T(8,128)(2,1)}, u32[]{:S(2)}, u32[]{:S(2)}) collective-permute-start(bf16[768,768]{1,0:T(8,128)(2,1)S(1)} %copy-done.10), channel_id=1, source_target_pairs={{0,16},{1,17},{2,18},{3,19},{4,20},{5,21},{6,22},{7,23},{8,24},{9,... | collective-permute-start | bytes 3538952 | tf_op jit(solution)/shard_map/ppermute | solution.py:25
  330.2 2.3 fusion.2
  334.4 8.1 %routed_back_attn.1 = (f32[512,768]{1,0:T(8,128)}, bf16[512,768]{1,0:T(8,128)(2,1)}, bf16[3,512,192]{2,1,0:T(8,128)(2,1)}, f32[2,768]{1,0:T(2,128)}, bf16[2,128,...) custom-call(s32[4]{0:T(128)} %pad_add_fusion.info, bf16[2,128,768]{2,1,0:T(8,128)(2,1)} %copy-done.25, ...), custom_call_target="tpu_custom_call" | custom-call | flops 800000000 | bytes 26400000 | tf_op jit(solution)/shard_map/routed_back_attn/pallas_call | solution.py:368
  345.5 8.5 %collective-permute-done.45.hop_ref = bf16[768,768]{1,0:T(8,128)(2,1)} collective-permute-done((bf16[768,768]{1,0:T(8,128)(2,1)S(1)}, bf16[768,768]{1,0:T(8,128)(2,1)}, u32[]{:S(2)}, u32[]{:S(2)}) %collective-permute-start.45) | collective-permute-done | bytes 1179680 | tf_op jit(solution)/shard_map/ppermute | solution.py:25
  354.0 4.6 %routed_attn_grads.1 = bf16[768,768]{1,0:T(8,128)(2,1)} custom-call(s32[4]{0:T(128)} %pad_add_fusion.info, bf16[512,768]{1,0:T(8,128)(2,1)} %get-tuple-element.237.normed_ref, bf16[3,512,192]{2,1,0:T(8,128)(2,1)} %get-tuple-element.238.d_ref, bf16[512,768]{1,0:T(8,128)(2,1)} %get-tuple-element.239.low_ref, bf16[512,192]{1,0:T(8,128)(2,1)} %get-tuple-element.240.mixed_ref, ...), custom_call_target="tpu_custom_call" | custom-call | flops 300000000 | bytes 9900000 | tf_op jit(solution)/shard_map/routed_attn_grads/pallas_call | solution.py:1072
  361.5 4.8 %rows_back.1 = (bf16[512,768]{1,0:T(8,128)(2,1)}, f32[1,768]{1,0:T(1,128)}) custom-call(bf16[2,512,768]{2,1,0:T(8,128)(2,1)} %get-tuple-element.231.keep_ref, bf16[2,512,768]{2,1,0:T(8,128)(2,1)} %collective-permute-done.43.near_ref, bf16[512,768]{1,0:T(8,128)(2,1)} %copy-done.37, bf16[512,768]{1,0:T(8,128)(2,1)} %get-tuple-element.164.rows_ref, ...), custom_call_target="tpu_custom_call" | custom-call | flops 400000000 | bytes 13200000 | tf_op jit(solution)/shard_map/rows_back/pallas_call | solution.py:1093
  370.7 5.5 %collective-permute-start.49 = (bf16[512,768]{1,0:T(8,128)(2,1)}, bf16[512,768]{1,0:T(8,128)(2,1)}, u32[]{:S(2)}, u32[]{:S(2)}) collective-permute-start(bf16[512,768]{1,0:T(8,128)(2,1)} %get-tuple-element.249), channel_id=1, source_target_pairs={{0,16},{1,17},{2,18},{3,19},{4,20},{5,21},{6,22},{7,23},{8,24},{9,... | collective-permute-start | bytes 2359304 | tf_op jit(solution)/shard_map/ppermute | solution.py:25
  377.1 5.8 %collective-permute-done.50 = bf16[2,192,768]{2,1,0:T(8,128)(2,1)} collective-permute-done((bf16[2,192,768]{2,1,0:T(8,128)(2,1)S(1)}, bf16[2,192,768]{2,1,0:T(8,128)(2,1)}, u32[]{:S(2)}, u32[]{:S(2)}) %collective-permute-start.50) | collective-permute-done | bytes 589856 | tf_op jit(solution)/shard_map/ppermute | solution.py:21
  388.8 2.8 collective-permute-start.55
  393.9 3.1 collective-permute-start.56
  399.9 6.1 %finish.1 = f32[2,512,768]{2,1,0:T(8,128)} custom-call(s32[4]{0:T(128)} %pad_add_fusion.info, bf16[2,128,768]{2,1,0:T(8,128)(2,1)} %copy-done.22, bf16[2,128,768]{2,1,0:T(8,128)(2,1)} %copy-done.45, f32[512,768]{1,0:T(8,128)} %get-tuple-element.246.d_mid_ref, bf16[512,768]{1,0:T(8,128)(2,1)} %get-tuple-element.140.picked_ref, f32[3,768]{1,0:T(4,128)} %bitcast.115, ...), custom_call_target="tpu_custom_call" | custom-call | flops 600000000 | bytes 19800000 | tf_op jit(solution)/shard_map/finish/pallas_call | solution.py:409
  406.0 4.6 %collective-permute-done.51 = bf16[192,768]{0,1:T(8,128)(2,1)S(1)} collective-permute-done((bf16[192,768]{0,1:T(8,128)(2,1)S(1)}, bf16[192,768]{0,1:T(8,128)(2,1)S(1)}, u32[]{:S(2)}, u32[]{:S(2)}) %collective-permute-start.51) | collective-permute-done | bytes 294944 | tf_op jit(solution)/shard_map/ppermute | solution.py:21
  412.6 2.1 convert_bitcast_fusion.1
  (268 shorter events, 95.8 us)
Async XLA Ops:
  7.2 405.4 %reduce-scatter.2.cloned.1.call-start = ((), (), s32[]{:S(2)}) async-start(), calls=%async_computation.1 | async-start | bytes 2949120 | tf_op jit(solution)/shard_map/reduce_scatter | solution.py:1308
  13.4 12.4 %collective-permute-start.1 = (bf16[2,128,768]{2,1,0:T(8,128)(2,1)S(1)}, bf16[2,128,768]{2,1,0:T(8,128)(2,1)S(1)}, u32[]{:S(2)}, u32[]{:S(2)}) collective-permute-start(bf16[2,128,768]{2,1,0:T(8,128)(2,1)S(1)} %add_convert_fusion.10), channel_id=1, source_target_pairs={{0,2},{1,3},{2,0},{3,1},{4,6},{5,7},{6,4},{7,5},{8,10},{9,11},{10,... | collective-permute-start | bytes 1179656 | tf_op jit(solution)/shard_map/ppermute | solution.py:21
  17.2 17.2 %collective-permute-start.5 = (bf16[384,768]{1,0:T(8,128)(2,1)}, bf16[384,768]{1,0:T(8,128)(2,1)S(1)}, u32[]{:S(2)}, u32[]{:S(2)}) collective-permute-start(bf16[384,768]{1,0:T(8,128)(2,1)} %dynamic-slice_bitcast_fusion.3), channel_id=1, source_target_pairs={{16,0},{17,1},{18,2},{19,3},{20,4},{21,5},{22,6},{23,7},{24,8},{25... | collective-permute-start | bytes 1769480 | tf_op jit(solution)/shard_map/ppermute | solution.py:25
  25.9 2.5 collective-permute-start.3
  26.0 11.5 %collective-permute-start.4 = (bf16[256,768]{1,0:T(8,128)(2,1)S(1)}, bf16[256,768]{1,0:T(8,128)(2,1)S(1)}, u32[]{:S(2)}, u32[]{:S(2)}) collective-permute-start(bf16[256,768]{1,0:T(8,128)(2,1)S(1)} %get-tuple-element.138), channel_id=1, source_target_pairs={{0,2},{1,3},{2,0},{3,1},{4,6},{5,7},{6,4},{7,5},{8,10},{9,11},{10,... | collective-permute-start | bytes 1179656 | tf_op jit(solution)/shard_map/ppermute | solution.py:21
  37.6 17.6 %collective-permute-start.8 = (bf16[384,768]{1,0:T(8,128)(2,1)S(1)}, bf16[384,768]{1,0:T(8,128)(2,1)S(1)}, u32[]{:S(2)}, u32[]{:S(2)}) collective-permute-start(bf16[384,768]{1,0:T(8,128)(2,1)S(1)} %dynamic-slice_bitcast_fusion.2), channel_id=1, source_target_pairs={{16,0},{17,1},{18,2},{19,3},{20,4},{21,5},{22,6},{23,7},{24,8},{25... | collective-permute-start | bytes 1769480 | tf_op jit(solution)/shard_map/ppermute | solution.py:25
  40.5 14.7 %collective-permute-start.7 = (bf16[2,128,768]{2,1,0:T(8,128)(2,1)S(1)}, bf16[2,128,768]{2,1,0:T(8,128)(2,1)S(1)}, u32[]{:S(2)}, u32[]{:S(2)}) collective-permute-start(bf16[2,128,768]{2,1,0:T(8,128)(2,1)S(1)} %add_convert_fusion.8), channel_id=1, source_target_pairs={{0,2},{1,3},{2,0},{3,1},{4,6},{5,7},{6,4},{7,5},{8,10},{9,11},{10,... | collective-permute-start | bytes 1179656 | tf_op jit(solution)/shard_map/ppermute | solution.py:21
  55.4 11.5 %collective-permute-start.10 = (bf16[256,768]{1,0:T(8,128)(2,1)S(1)}, bf16[256,768]{1,0:T(8,128)(2,1)S(1)}, u32[]{:S(2)}, u32[]{:S(2)}) collective-permute-start(bf16[256,768]{1,0:T(8,128)(2,1)S(1)} %get-tuple-element.147), channel_id=1, source_target_pairs={{0,2},{1,3},{2,0},{3,1},{4,6},{5,7},{6,4},{7,5},{8,10},{9,11},{10,... | collective-permute-start | bytes 1179656 | tf_op jit(solution)/shard_map/ppermute | solution.py:21
  67.9 31.1 %collective-permute-start.17 = (bf16[784,768]{1,0:T(8,128)(2,1)}, bf16[784,768]{1,0:T(8,128)(2,1)S(1)}, u32[]{:S(2)}, u32[]{:S(2)}) collective-permute-start(bf16[784,768]{1,0:T(8,128)(2,1)} %pack.1), channel_id=1, source_target_pairs={{16,0},{17,1},{18,2},{19,3},{20,4},{21,5},{22,6},{23,7},{24,8},{25... | collective-permute-start | bytes 3612680 | tf_op jit(solution)/shard_map/ppermute | solution.py:25
  71.0 11.2 %collective-permute-start.14 = (bf16[2,128,768]{2,1,0:T(8,128)(2,1)S(1)}, bf16[2,128,768]{2,1,0:T(8,128)(2,1)S(1)}, u32[]{:S(2)}, u32[]{:S(2)}) collective-permute-start(bf16[2,128,768]{2,1,0:T(8,128)(2,1)S(1)} %add_convert_fusion.6.mlp_ref), channel_id=1, source_target_pairs={{0,2},{1,3},{2,0},{3,1},{4,6},{5,7},{6,4},{7,5},{8,10},{9,11},{10,... | collective-permute-start | bytes 1179656 | tf_op jit(solution)/shard_map/ppermute | solution.py:21
  82.2 16.8 %collective-permute-start.16 = (bf16[2,384,768]{2,1,0:T(8,128)(2,1)S(1)}, bf16[2,384,768]{2,1,0:T(8,128)(2,1)S(1)}, u32[]{:S(2)}, u32[]{:S(2)}) collective-permute-start(bf16[2,384,768]{2,1,0:T(8,128)(2,1)S(1)} %pad_maximum_fusion.p0a), channel_id=1, source_target_pairs={{0,1},{1,0},{2,3},{3,2},{4,5},{5,4},{6,7},{7,6},{8,9},{9,8},{10,11... | collective-permute-start | bytes 3538952 | tf_op jit(solution)/shard_map/ppermute | solution.py:21
  82.2 28.5 %collective-permute-start.19 = (bf16[2,384,768]{2,1,0:T(8,128)(2,1)S(1)}, bf16[2,384,768]{2,1,0:T(8,128)(2,1)}, u32[]{:S(2)}, u32[]{:S(2)}) collective-permute-start(bf16[2,384,768]{2,1,0:T(8,128)(2,1)S(1)} %pad_maximum_fusion.p0a), channel_id=1, source_target_pairs={{0,2},{1,3},{2,0},{3,1},{4,6},{5,7},{6,4},{7,5},{8,10},{9,11},{10,... | collective-permute-start | bytes 3538952 | tf_op jit(solution)/shard_map/ppermute | solution.py:21
  83.9 28.2 %collective-permute-start.20 = (bf16[2,384,768]{2,1,0:T(8,128)(2,1)S(1)}, bf16[2,384,768]{2,1,0:T(8,128)(2,1)}, u32[]{:S(2)}, u32[]{:S(2)}) collective-permute-start(bf16[2,384,768]{2,1,0:T(8,128)(2,1)S(1)} %pad_maximum_fusion.p0a), channel_id=1, source_target_pairs={{0,4},{4,0},{8,12},{12,8},{1,5},{5,1},{9,13},{13,9},{2,6},{6,2},{1... | collective-permute-start | bytes 3538952 | tf_op jit(solution)/shard_map/ppermute | solution.py:21
  89.0 8.7 %collective-permute-start.15 = (bf16[128,768]{1,0:T(8,128)(2,1)S(1)}, bf16[128,768]{1,0:T(8,128)(2,1)S(1)}, u32[]{:S(2)}, u32[]{:S(2)}) collective-permute-start(bf16[128,768]{1,0:T(8,128)(2,1)S(1)} %slice_bitcast_fusion.2), channel_id=1, source_target_pairs={{0,16},{1,17},{2,18},{3,19},{4,20},{5,21},{6,22},{7,23},{8,24},{9,... | collective-permute-start | bytes 589832 | tf_op jit(solution)/shard_map/ppermute | solution.py:25
  99.0 4.0 collective-permute-start.18
  112.1 39.7 %collective-permute-start.21 = (bf16[2,384,768]{2,1,0:T(8,128)(2,1)}, bf16[2,384,768]{2,1,0:T(8,128)(2,1)S(1)}, u32[]{:S(2)}, u32[]{:S(2)}) collective-permute-start(bf16[2,384,768]{2,1,0:T(8,128)(2,1)} %collective-permute-done.19.p2a), channel_id=1, source_target_pairs={{0,4},{4,0},{8,12},{12,8},{1,5},{5,1},{9,13},{13,9},{2,6},{6,2},{1... | collective-permute-start | bytes 3538952 | tf_op jit(solution)/shard_map/ppermute | solution.py:21
  113.7 2.8 collective-permute-start.11
  114.2 2.9 collective-permute-start.12
  151.9 2.6 collective-permute-start.22
  155.8 19.7 %collective-permute-start.23 = (bf16[512,768]{1,0:T(8,128)(2,1)S(1)}, bf16[512,768]{1,0:T(8,128)(2,1)S(1)}, u32[]{:S(2)}, u32[]{:S(2)}) collective-permute-start(bf16[512,768]{1,0:T(8,128)(2,1)S(1)} %add_convert_fusion.1), channel_id=1, source_target_pairs={{0,2},{1,3},{2,0},{3,1},{4,6},{5,7},{6,4},{7,5},{8,10},{9,11},{10,... | collective-permute-start | bytes 2359304 | tf_op jit(solution)/shard_map/ppermute | solution.py:21
  165.6 10.9 %collective-permute-start.25 = (bf16[2,384,768]{2,1,0:T(8,128)(2,1)}, bf16[2,384,768]{2,1,0:T(8,128)(2,1)S(1)}, u32[]{:S(2)}, u32[]{:S(2)}) collective-permute-start(bf16[2,384,768]{2,1,0:T(8,128)(2,1)} %collective-permute-done.20.p0b), channel_id=1, source_target_pairs={{0,1},{1,0},{2,3},{3,2},{4,5},{5,4},{6,7},{7,6},{8,9},{9,8},{10,11... | collective-permute-start | bytes 3538952 | tf_op jit(solution)/shard_map/ppermute | solution.py:21
  165.8 10.7 %collective-permute-start.26 = (bf16[2,384,768]{2,1,0:T(8,128)(2,1)}, bf16[2,384,768]{2,1,0:T(8,128)(2,1)S(1)}, u32[]{:S(2)}, u32[]{:S(2)}) collective-permute-start(bf16[2,384,768]{2,1,0:T(8,128)(2,1)} %collective-permute-done.19.p2a), channel_id=1, source_target_pairs={{0,1},{1,0},{2,3},{3,2},{4,5},{5,4},{6,7},{7,6},{8,9},{9,8},{10,11... | collective-permute-start | bytes 3538952 | tf_op jit(solution)/shard_map/ppermute | solution.py:21
  166.2 10.3 %collective-permute-start.27 = (bf16[2,384,768]{2,1,0:T(8,128)(2,1)S(1)}, bf16[2,384,768]{2,1,0:T(8,128)(2,1)S(1)}, u32[]{:S(2)}, u32[]{:S(2)}) collective-permute-start(bf16[2,384,768]{2,1,0:T(8,128)(2,1)S(1)} %collective-permute-done.21.p2b), channel_id=1, source_target_pairs={{0,1},{1,0},{2,3},{3,2},{4,5},{5,4},{6,7},{7,6},{8,9},{9,8},{10,11... | collective-permute-start | bytes 3538952 | tf_op jit(solution)/shard_map/ppermute | solution.py:21
  175.4 2.5 collective-permute-start.24
  201.2 9.3 %collective-permute-start.28 = (bf16[7,512,768]{2,1,0:T(8,128)(2,1)}, bf16[7,512,768]{2,1,0:T(8,128)(2,1)S(1)}, u32[]{:S(2)}, u32[]{:S(2)}) collective-permute-start(bf16[7,512,768]{2,1,0:T(8,128)(2,1)} %get-tuple-element.186.own_ref), channel_id=1, source_target_pairs={{0,1},{1,0},{2,3},{3,2},{4,5},{5,4},{6,7},{7,6},{8,9},{9,8},{10,11... | collective-permute-start | bytes 16515080 | tf_op jit(solution)/shard_map/ppermute | solution.py:21
  201.4 20.2 %collective-permute-start.29 = (bf16[512,768]{1,0:T(8,128)(2,1)}, bf16[512,768]{1,0:T(8,128)(2,1)S(1)}, u32[]{:S(2)}, u32[]{:S(2)}) collective-permute-start(bf16[512,768]{1,0:T(8,128)(2,1)} %get-tuple-element.185.g0), channel_id=1, source_target_pairs={{0,2},{1,3},{2,0},{3,1},{4,6},{5,7},{6,4},{7,5},{8,10},{9,11},{10,... | collective-permute-start | bytes 2359304 | tf_op jit(solution)/shard_map/ppermute | solution.py:21
  221.7 49.1 %collective-permute-start.34 = (bf16[2,672,768]{2,1,0:T(8,128)(2,1)}, bf16[2,672,768]{2,1,0:T(8,128)(2,1)S(1)}, u32[]{:S(2)}, u32[]{:S(2)}) collective-permute-start(bf16[2,672,768]{2,1,0:T(8,128)(2,1)} %get-tuple-element.200.last_ref), channel_id=1, source_target_pairs={{0,16},{1,17},{2,18},{3,19},{4,20},{5,21},{6,22},{7,23},{8,24},{9,... | collective-permute-start | bytes 6193160 | tf_op jit(solution)/shard_map/ppermute | solution.py:25
  226.1 2.4 collective-permute-start.30
  226.2 36.7 %collective-permute-start.33 = (bf16[864,768]{1,0:T(8,128)(2,1)}, bf16[864,768]{1,0:T(8,128)(2,1)}, u32[]{:S(2)}, u32[]{:S(2)}) collective-permute-start(bf16[864,768]{1,0:T(8,128)(2,1)} %get-tuple-element.199), channel_id=1, source_target_pairs={{0,2},{1,3},{2,0},{3,1},{4,6},{5,7},{6,4},{7,5},{8,10},{9,11},{10,... | collective-permute-start | bytes 3981320 | tf_op jit(solution)/shard_map/ppermute | solution.py:21
  261.4 10.7 %collective-permute-start.32 = (bf16[128,768]{1,0:T(8,128)(2,1)S(1)}, bf16[128,768]{1,0:T(8,128)(2,1)S(1)}, u32[]{:S(2)}, u32[]{:S(2)}) collective-permute-start(bf16[128,768]{1,0:T(8,128)(2,1)S(1)} %add_convert_fusion.11.near_ref), channel_id=1, source_target_pairs={{0,2},{1,3},{2,0},{3,1},{4,6},{5,7},{6,4},{7,5},{8,10},{9,11},{10,... | collective-permute-start | bytes 589832 | tf_op jit(solution)/shard_map/ppermute | solution.py:21
  272.1 24.0 %collective-permute-start.36 = (bf16[672,768]{1,0:T(8,128)(2,1)S(1)}, bf16[672,768]{1,0:T(8,128)(2,1)S(1)}, u32[]{:S(2)}, u32[]{:S(2)}) collective-permute-start(bf16[672,768]{1,0:T(8,128)(2,1)S(1)} %fusion), channel_id=1, source_target_pairs={{0,2},{1,3},{2,0},{3,1},{4,6},{5,7},{6,4},{7,5},{8,10},{9,11},{10,... | collective-permute-start | bytes 3096584 | tf_op jit(solution)/shard_map/ppermute | solution.py:21
  273.5 31.8 %collective-permute-start.38 = (bf16[864,768]{1,0:T(8,128)(2,1)S(1)}, bf16[864,768]{1,0:T(8,128)(2,1)S(1)}, u32[]{:S(2)}, u32[]{:S(2)}) collective-permute-start(bf16[864,768]{1,0:T(8,128)(2,1)S(1)} %copy-done.7), channel_id=1, source_target_pairs={{0,16},{1,17},{2,18},{3,19},{4,20},{5,21},{6,22},{7,23},{8,24},{9,... | collective-permute-start | bytes 3981320 | tf_op jit(solution)/shard_map/ppermute | solution.py:25
  280.8 10.7 %collective-permute-start.35 = (bf16[128,768]{1,0:T(8,128)(2,1)}, bf16[128,768]{1,0:T(8,128)(2,1)S(1)}, u32[]{:S(2)}, u32[]{:S(2)}) collective-permute-start(bf16[128,768]{1,0:T(8,128)(2,1)} %sel_back.1.sel_own), channel_id=1, source_target_pairs={{16,0},{17,1},{18,2},{19,3},{20,4},{21,5},{22,6},{23,7},{24,8},{25... | collective-permute-start | bytes 589832 | tf_op jit(solution)/shard_map/ppermute | solution.py:25
  308.3 15.6 %collective-permute-start.40 = (bf16[2,128,768]{2,1,0:T(8,128)(2,1)S(1)}, bf16[2,128,768]{2,1,0:T(8,128)(2,1)S(1)}, u32[]{:S(2)}, u32[]{:S(2)}) collective-permute-start(bf16[2,128,768]{2,1,0:T(8,128)(2,1)S(1)} %add_convert_fusion.5), channel_id=1, source_target_pairs={{0,2},{1,3},{2,0},{3,1},{4,6},{5,7},{6,4},{7,5},{8,10},{9,11},{10,... | collective-permute-start | bytes 1179656 | tf_op jit(solution)/shard_map/ppermute | solution.py:21
  324.0 6.2 %collective-permute-start.43 = (bf16[2,512,768]{2,1,0:T(8,128)(2,1)}, bf16[2,512,768]{2,1,0:T(8,128)(2,1)}, u32[]{:S(2)}, u32[]{:S(2)}) collective-permute-start(bf16[2,512,768]{2,1,0:T(8,128)(2,1)} %get-tuple-element.232), channel_id=1, source_target_pairs={{0,1},{1,0},{2,3},{3,2},{4,5},{5,4},{6,7},{7,6},{8,9},{9,8},{10,11... | collective-permute-start | bytes 4718600 | tf_op jit(solution)/shard_map/ppermute | solution.py:21
  325.3 28.8 %collective-permute-start.45 = (bf16[768,768]{1,0:T(8,128)(2,1)S(1)}, bf16[768,768]{1,0:T(8,128)(2,1)}, u32[]{:S(2)}, u32[]{:S(2)}) collective-permute-start(bf16[768,768]{1,0:T(8,128)(2,1)S(1)} %copy-done.10), channel_id=1, source_target_pairs={{0,16},{1,17},{2,18},{3,19},{4,20},{5,21},{6,22},{7,23},{8,24},{9,... | collective-permute-start | bytes 3538952 | tf_op jit(solution)/shard_map/ppermute | solution.py:25
  330.1 3.5 collective-permute-start.41
  332.5 21.5 %collective-permute-start.44 = (bf16[512,768]{1,0:T(8,128)(2,1)}, bf16[512,768]{1,0:T(8,128)(2,1)S(1)}, u32[]{:S(2)}, u32[]{:S(2)}) collective-permute-start(bf16[512,768]{1,0:T(8,128)(2,1)} %fusion.2), channel_id=1, source_target_pairs={{0,2},{1,3},{2,0},{3,1},{4,6},{5,7},{6,4},{7,5},{8,10},{9,11},{10,... | collective-permute-start | bytes 2359304 | tf_op jit(solution)/shard_map/ppermute | solution.py:21
  360.0 22.9 %collective-permute-start.50 = (bf16[2,192,768]{2,1,0:T(8,128)(2,1)S(1)}, bf16[2,192,768]{2,1,0:T(8,128)(2,1)}, u32[]{:S(2)}, u32[]{:S(2)}) collective-permute-start(bf16[2,192,768]{2,1,0:T(8,128)(2,1)S(1)} %get-tuple-element.277), channel_id=1, source_target_pairs={{0,4},{4,0},{8,12},{12,8},{1,5},{5,1},{9,13},{13,9},{2,6},{6,2},{1... | collective-permute-start | bytes 1769480 | tf_op jit(solution)/shard_map/ppermute | solution.py:21
  360.5 16.6 %collective-permute-start.46 = (bf16[2,128,768]{2,1,0:T(8,128)(2,1)S(1)}, bf16[2,128,768]{2,1,0:T(8,128)(2,1)}, u32[]{:S(2)}, u32[]{:S(2)}) collective-permute-start(bf16[2,128,768]{2,1,0:T(8,128)(2,1)S(1)} %add_convert_fusion.3), channel_id=1, source_target_pairs={{0,2},{1,3},{2,0},{3,1},{4,6},{5,7},{6,4},{7,5},{8,10},{9,11},{10,... | collective-permute-start | bytes 1179656 | tf_op jit(solution)/shard_map/ppermute | solution.py:21
  368.3 8.2 %collective-permute-start.53 = (f32[6,768]{1,0:T(8,128)S(1)}, f32[6,768]{1,0:T(8,128)S(1)}, u32[]{:S(2)}, u32[]{:S(2)}) collective-permute-start(f32[6,768]{1,0:T(8,128)S(1)} %add.126), channel_id=1, source_target_pairs={{0,2},{1,3},{2,0},{3,1},{4,6},{5,7},{6,4},{7,5},{8,10},{9,11},{10,... | collective-permute-start | bytes 55304 | tf_op jit(solution)/shard_map/ppermute | solution.py:21
  369.4 29.5 %collective-permute-start.48 = (bf16[512,768]{1,0:T(8,128)(2,1)}, bf16[512,768]{1,0:T(8,128)(2,1)S(1)}, u32[]{:S(2)}, u32[]{:S(2)}) collective-permute-start(bf16[512,768]{1,0:T(8,128)(2,1)} %get-tuple-element.247.d_rows_ref), channel_id=1, source_target_pairs={{16,0},{17,1},{18,2},{19,3},{20,4},{21,5},{22,6},{23,7},{24,8},{25... | collective-permute-start | bytes 2359304 | tf_op jit(solution)/shard_map/ppermute | solution.py:25
  370.7 28.2 %collective-permute-start.49 = (bf16[512,768]{1,0:T(8,128)(2,1)}, bf16[512,768]{1,0:T(8,128)(2,1)}, u32[]{:S(2)}, u32[]{:S(2)}) collective-permute-start(bf16[512,768]{1,0:T(8,128)(2,1)} %get-tuple-element.249), channel_id=1, source_target_pairs={{0,16},{1,17},{2,18},{3,19},{4,20},{5,21},{6,22},{7,23},{8,24},{9,... | collective-permute-start | bytes 2359304 | tf_op jit(solution)/shard_map/ppermute | solution.py:25
  384.9 3.8 collective-permute-start.54
  386.7 12.1 %collective-permute-start.47 = (bf16[2,128,768]{2,1,0:T(8,128)(2,1)S(1)}, bf16[2,128,768]{2,1,0:T(8,128)(2,1)S(1)}, u32[]{:S(2)}, u32[]{:S(2)}) collective-permute-start(bf16[2,128,768]{2,1,0:T(8,128)(2,1)S(1)} %add_convert_fusion.2.own_ref), channel_id=1, source_target_pairs={{0,1},{1,0},{2,3},{3,2},{4,5},{5,4},{6,7},{7,6},{8,9},{9,8},{10,11... | collective-permute-start | bytes 1179656 | tf_op jit(solution)/shard_map/ppermute | solution.py:21
  388.8 5.0 %collective-permute-start.55 = (f32[6,768]{1,0:T(8,128)S(1)}, f32[6,768]{1,0:T(8,128)S(1)}, u32[]{:S(2)}, u32[]{:S(2)}) collective-permute-start(f32[6,768]{1,0:T(8,128)S(1)} %add.128), channel_id=1, source_target_pairs={{0,8},{4,12},{8,0},{12,4},{1,9},{5,13},{9,1},{13,5},{2,10},{6,14},... | collective-permute-start | bytes 55304 | tf_op jit(solution)/shard_map/ppermute | solution.py:21
  391.6 19.0 %collective-permute-start.51 = (bf16[192,768]{0,1:T(8,128)(2,1)S(1)}, bf16[192,768]{0,1:T(8,128)(2,1)S(1)}, u32[]{:S(2)}, u32[]{:S(2)}) collective-permute-start(bf16[192,768]{0,1:T(8,128)(2,1)S(1)} %dynamic-slice_bitcast_fusion.6), channel_id=1, source_target_pairs={{0,8},{4,12},{8,0},{12,4},{1,9},{5,13},{9,1},{13,5},{2,10},{6,14},... | collective-permute-start | bytes 884744 | tf_op jit(solution)/shard_map/ppermute | solution.py:21
  393.9 4.4 %collective-permute-start.56 = (f32[3,192]{1,0:T(4,128)S(1)}, f32[3,192]{1,0:T(4,128)S(1)}, u32[]{:S(2)}, u32[]{:S(2)}) collective-permute-start(f32[3,192]{1,0:T(4,128)S(1)} %slice.79), channel_id=1, source_target_pairs={{0,16},{1,17},{2,18},{3,19},{4,20},{5,21},{6,22},{7,23},{8,24},{9,... | collective-permute-start | bytes 6920 | tf_op jit(solution)/shard_map/ppermute | solution.py:25
  (74 other events, 617.3 us)
Sparse Core Ops, SparseCore 0:
  324.2 54.2 reduce-scatter.1
